TPU v7x, 32 devices: a whole 2x2x4 slice. The times are simulated.
32 devices in a mesh: dp: 4 (over z), hist: 4 (over y, x), mp: 2 (over core).
Axes of the slice: x: 2, y: 2, z: 4, core: 2. Of those that a mesh axis runs over, the one named last changes fastest.
Arguments:
- history: bfloat16 [4, 8192, 2048], P('hist', 'dp'), may hold values from -6 to 6
- mixer_in: bfloat16 [2048, 100], replicated, may hold values from -0.125 to 0.125
- mixer_out: bfloat16 [100, 4, 4], replicated, may hold values from -0.625 to 0.625
- mixer_bias: float32 [4, 4], replicated, may hold values from -3 to 3
- norm_gain: bfloat16 [4, 2048], P(None, ('dp', 'hist')), may hold values from 0.5 to 1.5
- query_weight: bfloat16 [2048, 2048], P(('dp', 'hist'), 'mp'), may hold values from -0.125 to 0.125
- key_weight: bfloat16 [2048, 2048], P(('dp', 'hist'), 'mp'), may hold values from -0.125 to 0.125
- value_weight: bfloat16 [2048, 2048], P(('dp', 'hist'), 'mp'), may hold values from -0.125 to 0.125
- out_weight: bfloat16 [2048, 2048], P('mp', ('dp', 'hist')), may hold values from -0.75 to 0.75
- up_weight: bfloat16 [2048, 8192], P(('dp', 'hist'), 'mp'), may hold values from -0.125 to 0.125
- down_weight: bfloat16 [8192, 2048], P('mp', ('dp', 'hist')), may hold values from -0.0625 to 0.0625
- target: bfloat16 [8192, 2048], P(('dp', 'hist')), may hold values from -6 to 6
- loss_count: int32 [8192], P(('dp', 'hist')), may hold values from 1 to 4
- domain: int32 [4], P('dp'), may hold values from 0 to 21
- domain_scale: float32 [22], replicated, may hold values from 0.3 to 1.5
Outputs:
- output: bfloat16 [8192, 2048], P(('dp', 'hist'))
- mix_weights: float32 [8192, 4, 4], P(('dp', 'hist'))
- history_grad: bfloat16 [4, 8192, 2048], P('hist', 'dp')
- mixer_in_grad: float32 [2048, 100], replicated
- mixer_out_grad: float32 [100, 4, 4], replicated
- mixer_bias_grad: float32 [4, 4], replicated
- norm_gain_grad: float32 [4, 2048], P(None, ('dp', 'hist'))
- query_grad: float32 [2048, 2048], P(('dp', 'hist'), 'mp')
- key_grad: float32 [2048, 2048], P(('dp', 'hist'), 'mp')
- value_grad: float32 [2048, 2048], P(('dp', 'hist'), 'mp')
- out_grad: float32 [2048, 2048], P('mp', ('dp', 'hist'))
- up_grad: float32 [2048, 8192], P(('dp', 'hist'), 'mp')
- down_grad: float32 [8192, 2048], P('mp', ('dp', 'hist'))
All inputs are finite; a program needn't handle non-finite values.
Results may differ from a plain program's by a relative error of at most 0.015.
Values may be sent and summed in bfloat16 or wider, within the bound.
No kernel may reach another device: no remote copies, remote signals or barrier semaphores. Data moves between devices by JAX's collectives and lax.ppermute only.
A program may use at most 448 MiB of HBM per device.

v0:
```python
import jax
import jax.numpy as jnp
from jax import lax
from jax.sharding import PartitionSpec as P

HD = 128
ROT = 32
STREAMS = 4
SEQ = 2048


HIGHEST = lax.Precision.HIGHEST
EPS_NORM = 1e-05
EPS_RMS = 1e-06
ROPE_BASE = 10000.0


def from_root(block, axis, holder):
    block = jnp.where(lax.axis_index(axis) == holder, block, jnp.zeros_like(block))
    return lax.psum(block, axis)


def gelu_slope(value):
    return (
        0.5 * (1.0 + lax.erf(value * 0.7071067811865476))
        + value * jnp.exp(-0.5 * value * value) * 0.3989422804014327
    )


def rope_tables(positions):
    half = ROT // 2
    freq = ROPE_BASE ** (-2.0 * jnp.arange(half, dtype=jnp.float32) / ROT)
    angle = positions[:, None] * freq[None, :]
    return (jnp.cos(angle), jnp.sin(angle))


def rotate(values, cosine, sine, turn):
    half = ROT // 2
    cos_wide = cosine[:, None, :]
    sin_wide = sine[:, None, :] * turn
    first = values[..., :half]
    second = values[..., half:ROT]
    return jnp.concatenate(
        [
            first * cos_wide - second * sin_wide,
            second * cos_wide + first * sin_wide,
            values[..., ROT:],
        ],
        -1,
    )


def attention_probs(query, keys_all, allowed):
    scores = jnp.einsum(
        "qhd,khd->hqk", query, keys_all, preferred_element_type=jnp.float32
    ) * HD ** (-0.5)
    scores = jnp.where(allowed[None], scores, -1e30)
    shifted = jnp.exp(scores - jnp.max(scores, -1, keepdims=True))
    return shifted / jnp.sum(shifted, -1, keepdims=True)


def rms_unit(latest):
    inverse = lax.rsqrt(jnp.mean(latest * latest, -1, keepdims=True) + EPS_RMS)
    return (inverse, (latest * inverse).astype(jnp.bfloat16))


def rms_back(latest, inverse, unit_grad):
    return inverse * unit_grad - latest * inverse * inverse * inverse * jnp.mean(
        unit_grad * latest, -1, keepdims=True
    )


def shards(
    history,
    mixer_in,
    mixer_out,
    mixer_bias,
    norm_gain,
    query_weight,
    key_weight,
    value_weight,
    out_weight,
    up_weight,
    down_weight,
    target,
    loss_count,
    domain,
    domain_scale,
):
    hist_index = lax.axis_index("hist")
    hist_count = lax.axis_size("hist")
    local_layers, group_rows, width = history.shape
    rows = target.shape[0]
    local_heads = query_weight.shape[1] // HD
    gathered = (
        lax.all_gather(query_weight, ("dp", "hist"), axis=0, tiled=True),
        lax.all_gather(key_weight, ("dp", "hist"), axis=0, tiled=True),
        lax.all_gather(value_weight, ("dp", "hist"), axis=0, tiled=True),
        lax.all_gather(out_weight, ("dp", "hist"), axis=1, tiled=True),
        lax.all_gather(up_weight, ("dp", "hist"), axis=0, tiled=True),
        lax.all_gather(down_weight, ("dp", "hist"), axis=1, tiled=True),
        lax.all_gather(norm_gain, ("dp", "hist"), axis=1, tiled=True),
    )
    query_full, key_full, value_full, out_full, up_full, down_full, gain_full = gathered
    gain_single_precise = gain_full.astype(jnp.float32)
    mixer_in_float = mixer_in.astype(jnp.float32)
    row_global = hist_index * rows + jnp.arange(rows)
    first_layer = hist_index * local_layers
    latest = history[local_layers - 1].astype(jnp.float32)
    inverse, unit_low = rms_unit(latest)
    mixer_pre = jnp.dot(unit_low, mixer_in, preferred_element_type=jnp.float32)
    mixer_hidden = from_root(
        jax.nn.gelu(mixer_pre, approximate=False).astype(jnp.bfloat16), "hist", hist_count - 1
    )
    local_low = lax.dynamic_slice_in_dim(mixer_out, first_layer, local_layers, 2)
    local_cols = local_low.astype(jnp.float32)
    local_bias = lax.dynamic_slice_in_dim(mixer_bias, first_layer, local_layers, 1)
    mix_local = (
        jnp.einsum("tm,mcl->tcl", mixer_hidden, local_low, preferred_element_type=jnp.float32)
        + local_bias[None]
    )
    hidden_rows = lax.dynamic_slice_in_dim(mixer_hidden, hist_index * rows, rows, 0)
    mix_rows = (
        jnp.einsum("tm,mcl->tcl", hidden_rows, mixer_out, preferred_element_type=jnp.float32)
        + mixer_bias[None]
    )
    layer = 0
    total = mix_local[:, :, layer, None] * history[layer][:, None, :].astype(jnp.float32)
    streams = lax.psum_scatter(total, "hist", scatter_dimension=0, tiled=True)
    centered_input = streams - jnp.mean(streams, -1, keepdims=True)
    inverse_deviation = lax.rsqrt(
        jnp.mean(centered_input * centered_input, -1, keepdims=True) + EPS_NORM
    )
    standardized_input = centered_input * inverse_deviation
    normalized_reduced = (standardized_input * gain_single_precise[None]).astype(jnp.bfloat16)
    cosine, sine = rope_tables((row_global % SEQ).astype(jnp.float32))
    query_pre = jnp.dot(
        normalized_reduced[:, 0], query_full, preferred_element_type=jnp.float32
    ).reshape(rows, local_heads, HD)
    key_pre = jnp.dot(
        normalized_reduced[:, 1], key_full, preferred_element_type=jnp.float32
    ).reshape(rows, local_heads, HD)
    query = rotate(query_pre, cosine, sine, 1.0).astype(jnp.bfloat16)
    keys = rotate(key_pre, cosine, sine, 1.0).astype(jnp.bfloat16)
    values = (
        jnp.dot(normalized_reduced[:, 2], value_full, preferred_element_type=jnp.float32)
        .astype(jnp.bfloat16)
        .reshape(rows, local_heads, HD)
    )
    keys_all, values_all = (
        lax.all_gather(keys, "hist", axis=0, tiled=True),
        lax.all_gather(values, "hist", axis=0, tiled=True),
    )
    key_index = jnp.arange(group_rows)
    allowed = (key_index[None, :] <= row_global[:, None]) & (
        key_index[None, :] // SEQ == row_global[:, None] // SEQ
    )
    probs = attention_probs(query, keys_all, allowed)
    probs_low = probs.astype(jnp.bfloat16)
    attended = jnp.einsum("hqk,khd->qhd", probs_low, values_all, preferred_element_type=jnp.float32)
    attended_low = attended.reshape(rows, local_heads * HD).astype(jnp.bfloat16)
    hidden_pre = jnp.dot(normalized_reduced[:, 3], up_full, preferred_element_type=jnp.float32)
    hidden_act = jax.nn.gelu(hidden_pre, approximate=False).astype(jnp.bfloat16)
    branch = jnp.dot(attended_low, out_full, preferred_element_type=jnp.float32) + jnp.dot(
        hidden_act, down_full, preferred_element_type=jnp.float32
    )
    branch = lax.psum(branch.astype(jnp.bfloat16), "mp").astype(jnp.float32)
    output = (streams[:, 3] + branch).astype(jnp.bfloat16)
    seq_local = row_global // SEQ
    row_domain = jnp.sum(
        jnp.where(seq_local[:, None] == jnp.arange(domain.shape[0])[None, :], domain[None, :], 0), 1
    )
    row_scale = jnp.sum(
        jnp.where(
            row_domain[:, None] == jnp.arange(domain_scale.shape[0])[None, :],
            domain_scale[None, :],
            0.0,
        ),
        1,
    )
    cotangent = target.astype(jnp.float32) * (loss_count.astype(jnp.float32) * row_scale)[:, None]
    branch_grad = cotangent.astype(jnp.bfloat16)
    act_grad = jnp.dot(branch_grad, down_full.T, preferred_element_type=jnp.float32)
    pre_grad = (act_grad * gelu_slope(hidden_pre)).astype(jnp.bfloat16)
    down_part = jnp.dot(hidden_act.T, branch_grad, preferred_element_type=jnp.float32)
    up_part = jnp.dot(normalized_reduced[:, 3].T, pre_grad, preferred_element_type=jnp.float32)
    attended_grad = jnp.dot(branch_grad, out_full.T, preferred_element_type=jnp.float32).astype(
        jnp.bfloat16
    )
    out_part = jnp.dot(attended_low.T, branch_grad, preferred_element_type=jnp.float32)
    attended_grad = attended_grad.reshape(rows, local_heads, HD)
    prob_grad = jnp.einsum(
        "qhd,khd->hqk", attended_grad, values_all, preferred_element_type=jnp.float32
    )
    score_grad = (probs * (prob_grad - jnp.sum(probs * prob_grad, -1, keepdims=True))).astype(
        jnp.bfloat16
    )
    query_back = jnp.einsum(
        "hqk,khd->qhd", score_grad, keys_all, preferred_element_type=jnp.float32
    ) * HD ** (-0.5)
    key_terms = jnp.einsum(
        "hqk,qhd->khd", score_grad, query, preferred_element_type=jnp.float32
    ) * HD ** (-0.5)
    value_terms = jnp.einsum(
        "hqk,qhd->khd", probs_low, attended_grad, preferred_element_type=jnp.float32
    )
    key_back, value_back = (
        lax.psum_scatter(
            key_terms.astype(jnp.bfloat16), "hist", scatter_dimension=0, tiled=True
        ).astype(jnp.float32),
        lax.psum_scatter(
            value_terms.astype(jnp.bfloat16), "hist", scatter_dimension=0, tiled=True
        ).astype(jnp.float32),
    )
    query_back = (
        rotate(query_back, cosine, sine, -1.0).reshape(rows, local_heads * HD).astype(jnp.bfloat16)
    )
    key_back = (
        rotate(key_back, cosine, sine, -1.0).reshape(rows, local_heads * HD).astype(jnp.bfloat16)
    )
    value_back = value_back.reshape(rows, local_heads * HD).astype(jnp.bfloat16)
    query_part = jnp.dot(normalized_reduced[:, 0].T, query_back, preferred_element_type=jnp.float32)
    key_part = jnp.dot(normalized_reduced[:, 1].T, key_back, preferred_element_type=jnp.float32)
    value_part = jnp.dot(normalized_reduced[:, 2].T, value_back, preferred_element_type=jnp.float32)
    normalized_gradient = jnp.stack(
        [
            jnp.dot(query_back, query_full.T, preferred_element_type=jnp.float32),
            jnp.dot(key_back, key_full.T, preferred_element_type=jnp.float32),
            jnp.dot(value_back, value_full.T, preferred_element_type=jnp.float32),
            jnp.dot(pre_grad, up_full.T, preferred_element_type=jnp.float32),
        ],
        1,
    )
    normalized_gradient = lax.psum(normalized_gradient.astype(jnp.bfloat16), "mp").astype(
        jnp.float32
    )
    gradient_scaled = normalized_gradient * gain_single_precise[None]
    stream_grad = inverse_deviation * (
        gradient_scaled
        - jnp.mean(gradient_scaled, -1, keepdims=True)
        - standardized_input * jnp.mean(gradient_scaled * standardized_input, -1, keepdims=True)
    )
    gain_portion = jnp.sum(normalized_gradient * standardized_input, 0)
    stream_grad = jnp.concatenate(
        [stream_grad[:, :3], stream_grad[:, 3:] + cotangent[:, None, :]], 1
    )
    weight_parts = (
        lax.psum_scatter(query_part, ("dp", "hist"), scatter_dimension=0, tiled=True),
        lax.psum_scatter(key_part, ("dp", "hist"), scatter_dimension=0, tiled=True),
        lax.psum_scatter(value_part, ("dp", "hist"), scatter_dimension=0, tiled=True),
        lax.psum_scatter(out_part, ("dp", "hist"), scatter_dimension=1, tiled=True),
        lax.psum_scatter(up_part, ("dp", "hist"), scatter_dimension=0, tiled=True),
        lax.psum_scatter(down_part, ("dp", "hist"), scatter_dimension=1, tiled=True),
        lax.psum_scatter(gain_portion, ("dp", "hist"), scatter_dimension=1, tiled=True),
    )
    query_grad, key_grad, value_grad, out_grad, up_grad, down_grad, norm_gain_grad = weight_parts
    stream_low = stream_grad.astype(jnp.bfloat16)
    stream_all = lax.all_gather(stream_low, "hist", axis=0, tiled=True)
    layer = 0
    layer_total = jnp.zeros((group_rows, width), jnp.float32)
    for stream in range(STREAMS):
        layer_total = layer_total + mix_local[:, stream, layer, None] * stream_all[
            :, stream, :
        ].astype(jnp.float32)
    layer_grads = [layer_total]
    mix_cols = [
        jnp.einsum("tcd,td->tc", stream_all, history[layer], preferred_element_type=jnp.float32)
    ]
    mix_grad = jnp.stack(mix_cols, 2)
    hidden_grad = jnp.einsum("tcl,mcl->tm", mix_grad, local_cols, precision=HIGHEST)
    cols_local = jnp.einsum(
        "tm,tcl->mcl", mixer_hidden.astype(jnp.float32), mix_grad, precision=HIGHEST
    )
    cols_grad = lax.dynamic_update_slice_in_dim(
        jnp.zeros(mixer_out.shape, jnp.float32), cols_local, first_layer, 2
    )
    bias_grad = lax.dynamic_update_slice_in_dim(
        jnp.zeros(mixer_bias.shape, jnp.float32), jnp.sum(mix_grad, 0), first_layer, 1
    )
    hidden_grad = lax.psum(hidden_grad.astype(jnp.bfloat16), "hist").astype(jnp.float32)
    mixer_pre_grad = hidden_grad * gelu_slope(mixer_pre)
    is_last = (hist_index == hist_count - 1).astype(jnp.float32)
    in_grad = jnp.dot(unit_low.astype(jnp.float32).T, mixer_pre_grad, precision=HIGHEST) * is_last
    unit_grad = jnp.dot(mixer_pre_grad, mixer_in_float.T, precision=HIGHEST)
    layer_grads[local_layers - 1] = (
        layer_grads[local_layers - 1] + rms_back(latest, inverse, unit_grad) * is_last
    )
    history_grad = jnp.stack(layer_grads, 0).astype(jnp.bfloat16)
    mixer_in_grad, mixer_out_grad, mixer_bias_grad = lax.psum(
        (in_grad, cols_grad, bias_grad), ("dp", "hist")
    )
    return (
        output,
        mix_rows,
        history_grad,
        mixer_in_grad,
        mixer_out_grad,
        mixer_bias_grad,
        norm_gain_grad,
        query_grad,
        key_grad,
        value_grad,
        out_grad,
        up_grad,
        down_grad,
    )


def solution(mesh):
    in_specs = (
        P("hist", "dp", None),
        P(),
        P(),
        P(),
        P(None, ("dp", "hist")),
        P(("dp", "hist"), "mp"),
        P(("dp", "hist"), "mp"),
        P(("dp", "hist"), "mp"),
        P("mp", ("dp", "hist")),
        P(("dp", "hist"), "mp"),
        P("mp", ("dp", "hist")),
        P(("dp", "hist"), None),
        P(("dp", "hist")),
        P("dp"),
        P(),
    )
    out_specs = (
        P(("dp", "hist"), None),
        P(("dp", "hist"), None, None),
        P("hist", "dp", None),
        P(),
        P(),
        P(),
        P(None, ("dp", "hist")),
        P(("dp", "hist"), "mp"),
        P(("dp", "hist"), "mp"),
        P(("dp", "hist"), "mp"),
        P("mp", ("dp", "hist")),
        P(("dp", "hist"), "mp"),
        P("mp", ("dp", "hist")),
    )
    return jax.shard_map(shards, mesh=mesh, in_specs=in_specs, out_specs=out_specs, check_vma=False)
```

profile of v0, /device:TPU:0, one launch (start us, length us, event | category | flops | bytes accessed | tf_op | source)
XLA Modules:
  0.0 4153.5 jit_solution(12729534291563422707)
XLA Ops:
  35.0 34.5 all-reduce.7.cloned.1.call-done
  71.3 26.3 broadcast_multiply_fusion
  99.0 40.0 all_gather.30
  147.3 59.4 %all-gather.14.cloned.1.call-done = bf16[2048,1024]{1,0:T(8,128)(2,1)} async-done(((bf16[128,1024]{1,0:T(8,128)(2,1)}), bf16[2048,1024]{1,0:T(8,128)(2,1)}) %all-gather.14.cloned.1.call-update) | async-done | bytes 4194320 | tf_op jit(solution)/shard_map/all_gather | solution.py:96
  213.3 516.8 %reduce-scatter.13.cloned.1.call-done = f32[512,4,2048]{2,0,1:T(8,128)} async-done(((f32[2048,4,2048]{2,0,1:T(8,128)}), f32[512,4,2048]{2,0,1:T(8,128)}) %reduce-scatter.13.cloned.1.call-update) | async-done | bytes 16777232 | tf_op jit(solution)/shard_map/reduce_scatter | solution.py:129
  784.0 31.0 all-gather.18.cloned.1.call-done
  815.0 18.4 fusion.128
  833.5 36.5 all-gather.12.cloned.1.call-done
  870.0 23.1 multiply_reduce_fusion
  893.1 28.1 multiply_convert_fusion
  931.8 132.4 %all-gather.22.cloned.1.call-done = bf16[2048,4096]{1,0:T(8,128)(2,1)} async-done(((bf16[128,4096]{1,0:T(8,128)(2,1)}), bf16[2048,4096]{1,0:T(8,128)(2,1)}) %all-gather.22.cloned.1.call-update) | async-done | bytes 16777232 | tf_op jit(solution)/shard_map/all_gather | solution.py:100
  1064.2 30.7 fusion.22
  1094.9 219.7 %all-gather.24.cloned.1.call-done = bf16[4096,2048]{1,0:T(8,128)(2,1)} async-done(((bf16[4096,128]{1,0:T(8,128)(2,1)}), bf16[4096,2048]{1,0:T(8,128)(2,1)}) %all-gather.24.cloned.1.call-update) | async-done | bytes 16777232 | tf_op jit(solution)/shard_map/all_gather | solution.py:101
  1314.6 17.0 fusion.28
  1331.7 17.9 convert_bitcast_fusion
  1349.6 15.5 fusion.53
  1379.1 18.5 fusion.74
  1402.8 13.8 add_convert_fusion
  1436.6 40.5 all-reduce.13.cloned.1.call-done
  1521.1 296.3 %all-gather.26.cloned.1.call-done = bf16[2048,4,2048]{2,0,1:T(8,128)(2,1)} async-done(((bf16[512,4,2048]{2,0,1:T(8,128)(2,1)}), bf16[2048,4,2048]{2,0,1:T(8,128)(2,1)}) %all-gather.26.cloned.1.call-update) | async-done | bytes 33554448 | tf_op jit(solution)/shard_map/all_gather | solution.py:258
  1817.4 81.7 %fusion.129 = (f32[1,4]{1,0:T(1,128)S(1)}, f32[2048,1,4]{2,1,0:T(1,128)S(1)}) fusion(bf16[2048,2048,1]{1,0,2:T(8,128)(2,1)} %bitcast.173, bf16[2048,4,2048]{2,0,1:T(8,128)(2,1)} %all-gather.26.cloned.1.call-done), kind=kOutput, calls=%fused_computation.215 | convolution fusion | flops 33562620 | bytes 41975824 | tf_op jit(solution)/shard_map/tcd,td->tc/dot_general | solution.py:267
  1931.8 18.1 fusion.68
  1950.2 18.5 fusion.110
  1978.0 77.0 %all-reduce = (f32[100,4,4]{0,2,1:T(4,128)}, f32[4,4]{1,0:T(4,128)}) all-reduce(f32[100,4,4]{0,2,1:T(4,128)S(1)} %dynamic_update_slice.6, f32[4,4]{1,0:T(4,128)S(1)} %dynamic_update_slice.7), channel_id=1, replica_groups=mesh['dp'=4,'hist'=4,'mp'=2] {'dp','hist'}, use_global_device_ids=true, to_apply=%region_18.19 | all-reduce | flops 1616 | bytes 12928 | tf_op jit(solution)/shard_map/psum | solution.py:289
  2055.0 13.8 multiply_reduce_fusion.1
  2077.8 24.5 fusion.40
  2102.3 173.0 %reduce-scatter.21.cloned.1.call-done = f32[128,1024]{1,0:T(8,128)} async-done(((f32[2048,1024]{1,0:T(8,128)}), f32[128,1024]{1,0:T(8,128)}) %reduce-scatter.21.cloned.1.call-update) | async-done | bytes 524304 | tf_op jit(solution)/shard_map/reduce_scatter | solution.py:249
  2275.3 183.1 %reduce-scatter.19.cloned.1.call-done = f32[128,1024]{1,0:T(8,128)} async-done(((f32[2048,1024]{1,0:T(8,128)}), f32[128,1024]{1,0:T(8,128)}) %reduce-scatter.19.cloned.1.call-update) | async-done | bytes 524304 | tf_op jit(solution)/shard_map/reduce_scatter | solution.py:248
  2458.4 183.1 %reduce-scatter.23.cloned.1.call-done = f32[128,1024]{1,0:T(8,128)} async-done(((f32[2048,1024]{1,0:T(8,128)}), f32[128,1024]{1,0:T(8,128)}) %reduce-scatter.23.cloned.1.call-update) | async-done | bytes 524304 | tf_op jit(solution)/shard_map/reduce_scatter | solution.py:250
  2641.4 688.8 %reduce-scatter.27.cloned.1.call-done = f32[128,4096]{1,0:T(8,128)} async-done(((f32[2048,4096]{1,0:T(8,128)}), f32[128,4096]{1,0:T(8,128)}) %reduce-scatter.27.cloned.1.call-update) | async-done | bytes 2097168 | tf_op jit(solution)/shard_map/reduce_scatter | solution.py:252
  3330.2 691.8 %reduce-scatter.29.cloned.1.call-done = f32[4096,128]{1,0:T(8,128)} async-done(((f32[4096,2048]{1,0:T(8,128)}), f32[4096,128]{1,0:T(8,128)}) %reduce-scatter.29.cloned.1.call-update) | async-done | bytes 2097168 | tf_op jit(solution)/shard_map/reduce_scatter | solution.py:253
  4022.0 121.7 %all-reduce.11.cloned.1.call-done = f32[2048,100]{0,1:T(8,128)} async-done(((f32[2048,100]{0,1:T(8,128)}), f32[2048,100]{0,1:T(8,128)}) %all-reduce.11.cloned.1.call-update) | async-done | bytes 819216 | tf_op jit(solution)/shard_map/psum | solution.py:289
  (228 shorter events, 244.7 us)
Async XLA Ops:
  8.0 61.5 %all-reduce.7.cloned.1.call-start = ((), (), s32[]{:S(2)}) async-start(), calls=%async_computation.10 | async-start | bytes 851968 | tf_op jit(solution)/shard_map/psum | solution.py:20
  22.2 118.3 %all-gather.16.cloned.1.call-start = ((), (), s32[]{:S(2)}) async-start(), calls=%async_computation.15 | async-start | bytes 4456448 | tf_op jit(solution)/shard_map/all_gather | solution.py:97
  22.8 184.0 %all-gather.14.cloned.1.call-start = ((), (), s32[]{:S(2)}) async-start(), calls=%async_computation.14 | async-start | bytes 4456448 | tf_op jit(solution)/shard_map/all_gather | solution.py:96
  23.4 706.7 %reduce-scatter.13.cloned.1.call-start = ((), (), s32[]{:S(2)}) async-start(), calls=%async_computation.11 | async-start | bytes 83886080 | tf_op jit(solution)/shard_map/reduce_scatter | solution.py:129
  23.6 45.9 %copy-start.40 = (bf16[100,4,1]{0,2,1:T(2,128)(2,1)}, bf16[100,4,1]{0,2,1:T(2,128)(2,1)S(1)}, u32[]{:S(2)}) copy-start(bf16[100,4,1]{0,2,1:T(2,128)(2,1)S(1)} %constant_dynamic-slice_fusion) | copy-start | bytes 2404
  97.6 665.0 %all-gather.10.cloned.1.call-start = ((), (), s32[]{:S(2)}) async-start(), calls=%async_computation.12 | async-start | bytes 4456448 | tf_op jit(solution)/shard_map/all_gather | solution.py:98
  98.2 676.8 %all-gather.20.cloned.1.call-start = ((), (), s32[]{:S(2)}) async-start(), calls=%async_computation.17 | async-start | bytes 4456448 | tf_op jit(solution)/shard_map/all_gather | solution.py:99
  98.9 716.1 %all-gather.18.cloned.1.call-start = ((), (), s32[]{:S(2)}) async-start(), calls=%async_computation.16 | async-start | bytes 5242880 | tf_op jit(solution)/shard_map/all_gather | solution.py:151
  139.0 605.3 %copy-start.22 = (f32[4,2048]{1,0:T(4,128)}, f32[4,2048]{1,0:T(4,128)S(1)}, u32[]{:S(2)}) copy-start(f32[4,2048]{1,0:T(4,128)S(1)} %convert_element_type.173) | copy-start | bytes 98308
  140.5 618.8 %copy-start.27 = (f32[512,16]{0,1:T(8,128)}, f32[512,16]{0,1:T(8,128)S(1)}, u32[]{:S(2)}) copy-start(f32[512,16]{0,1:T(8,128)S(1)} %get-tuple-element.38) | copy-start | bytes 98308
  762.6 107.4 %all-gather.12.cloned.1.call-start = ((), (), s32[]{:S(2)}) async-start(), calls=%async_computation.13 | async-start | bytes 5242880 | tf_op jit(solution)/shard_map/all_gather | solution.py:152
  771.3 293.0 %all-gather.22.cloned.1.call-start = ((), (), s32[]{:S(2)}) async-start(), calls=%async_computation.18 | async-start | bytes 17825792 | tf_op jit(solution)/shard_map/all_gather | solution.py:100
  771.8 542.8 %all-gather.24.cloned.1.call-start = ((), (), s32[]{:S(2)}) async-start(), calls=%async_computation.19 | async-start | bytes 17825792 | tf_op jit(solution)/shard_map/all_gather | solution.py:101
  772.4 644.1 %reduce-scatter.15.cloned.1.call-start = ((), (), s32[]{:S(2)}) async-start(), calls=%async_computation.20 | async-start | bytes 5242880 | tf_op jit(solution)/shard_map/reduce_scatter | solution.py:208
  782.1 87.9 %copy-start.20 = (bf16[512,1024]{0,1:T(8,128)(2,1)}, bf16[512,1024]{0,1:T(8,128)(2,1)S(1)}, u32[]{:S(2)}) copy-start(bf16[512,1024]{0,1:T(8,128)(2,1)S(1)} %copy.87) | copy-start | bytes 3145732
  931.6 383.1 %copy-start.11 = (bf16[512,2048]{1,0:T(8,128)(2,1)S(1)}, bf16[512,2048]{1,0:T(8,128)(2,1)}, u32[]{:S(2)}) copy-start(bf16[512,2048]{1,0:T(8,128)(2,1)} %param.26) | copy-start | bytes 6291460
  931.6 383.1 %copy-start.38 = (f32[512]{0:T(512)S(1)}, f32[512]{0:T(512)}, u32[]{:S(2)}) copy-start(f32[512]{0:T(512)} %copy-done.37) | copy-start | bytes 6148
  931.6 495.9 %reduce-scatter.17.cloned.1.call-start = ((), (), s32[]{:S(2)}) async-start(), calls=%async_computation.21 | async-start | bytes 5242880 | tf_op jit(solution)/shard_map/reduce_scatter | solution.py:211
  1349.6 127.5 %all-reduce.13.cloned.1.call-start = ((), (), s32[]{:S(2)}) async-start(), calls=%async_computation.32 | async-start | bytes 20971520 | tf_op jit(solution)/shard_map/psum | solution.py:167
  1436.5 380.8 %all-gather.26.cloned.1.call-start = ((), (), s32[]{:S(2)}) async-start(), calls=%async_computation.22 | async-start | bytes 41943040 | tf_op jit(solution)/shard_map/all_gather | solution.py:258
  1519.0 456.4 %reduce-scatter.31.cloned.1.call-start = ((), (), s32[]{:S(2)}) async-start(), calls=%async_computation.31 | async-start | bytes 1114112
  1521.1 534.0 %all-reduce.9.cloned.1.call-start = ((), (), s32[]{:S(2)}) async-start(), calls=%async_computation.23 | async-start | bytes 851968 | tf_op jit(solution)/shard_map/psum | solution.py:280
  1817.4 81.7 %copy-start.41 = (bf16[100,4,1]{0,2,1:T(2,128)(2,1)S(1)}, bf16[100,4,1]{0,2,1:T(2,128)(2,1)}, u32[]{:S(2)}) copy-start(bf16[100,4,1]{0,2,1:T(2,128)(2,1)} %copy-done.40) | copy-start | bytes 2404
  1817.4 83.3 %copy-start.8 = (bf16[8,128,512]{2,1,0:T(8,128)(2,1)S(1)}, bf16[8,128,512]{2,1,0:T(8,128)(2,1)}, u32[]{:S(2)}) copy-start(bf16[8,128,512]{2,1,0:T(8,128)(2,1)} %fusion.74) | copy-start | bytes 3145732
  1900.6 201.8 %reduce-scatter.25.cloned.1.call-start = ((), (), s32[]{:S(2)}) async-start(), calls=%async_computation.28 | async-start | bytes 8912896 | tf_op jit(solution)/shard_map/reduce_scatter | solution.py:251
  1907.9 367.4 %reduce-scatter.21.cloned.1.call-start = ((), (), s32[]{:S(2)}) async-start(), calls=%async_computation.26 | async-start | bytes 8912896 | tf_op jit(solution)/shard_map/reduce_scatter | solution.py:249
  1915.8 542.6 %reduce-scatter.19.cloned.1.call-start = ((), (), s32[]{:S(2)}) async-start(), calls=%async_computation.25 | async-start | bytes 8912896 | tf_op jit(solution)/shard_map/reduce_scatter | solution.py:248
  1923.2 718.2 %reduce-scatter.23.cloned.1.call-start = ((), (), s32[]{:S(2)}) async-start(), calls=%async_computation.27 | async-start | bytes 8912896 | tf_op jit(solution)/shard_map/reduce_scatter | solution.py:250
  1931.7 1398.5 %reduce-scatter.27.cloned.1.call-start = ((), (), s32[]{:S(2)}) async-start(), calls=%async_computation.29 | async-start | bytes 35651584 | tf_op jit(solution)/shard_map/reduce_scatter | solution.py:252
  1949.9 2072.1 %reduce-scatter.29.cloned.1.call-start = ((), (), s32[]{:S(2)}) async-start(), calls=%async_computation.30 | async-start | bytes 35651584 | tf_op jit(solution)/shard_map/reduce_scatter | solution.py:253
  1968.7 86.3 %copy-start.9 = (f32[2048,100]{0,1:T(8,128)S(1)}, f32[2048,100]{0,1:T(8,128)}, u32[]{:S(2)}) copy-start(f32[2048,100]{0,1:T(8,128)} %get-tuple-element.40) | copy-start | bytes 2457604
  1968.7 2175.0 %all-reduce.11.cloned.1.call-start = ((), (), s32[]{:S(2)}) async-start(), calls=%async_computation.24 | async-start | bytes 1703936 | tf_op jit(solution)/shard_map/psum | solution.py:289
  (42 other events, 397.4 us)
Sparse Core Ops, SparseCore 0:
  22.3 47.1 all-reduce.6
  97.7 632.3 reduce-scatter.12
  1900.7 77.5 all-reduce.8
Sparse Core Ops, SparseCore 1:
  25.8 78.5 all-gather.15
  107.4 99.3 all-gather.13
  209.8 97.0 all-gather.9
  310.0 101.9 all-gather.19
  762.6 52.4 all-gather.17
  817.6 52.4 all-gather.11
  873.0 191.1 all-gather.21
  1067.2 247.4 all-gather.23
  1317.7 50.7 reduce-scatter.14
  1371.5 52.5 reduce-scatter.16
  1436.6 40.4 all-reduce.12
  1519.0 298.3 all-gather.25
  1819.6 77.6 reduce-scatter.30
  1908.0 185.0 reduce-scatter.24
  2095.9 179.3 reduce-scatter.20
  2278.2 180.1 reduce-scatter.18
  2461.3 180.1 reduce-scatter.22
  2644.4 685.7 reduce-scatter.26
  3333.0 688.9 reduce-scatter.28
  4027.9 115.8 all-reduce.10
where the time goes:
time: 4160 us; the launch traced here: 4150 us
  waiting for transfers between devices  3410 us (82%)
  matrix products  396 us (10%)
  other arithmetic  169 us (4%)
  blocking collectives  117 us (3%)
    reduce_scatter x1, waiting for transfers between devices, shards(): lax.psum_scatter(down_part, ('dp', 'hist'), scatter_dimension=1, tiled=True)  692 us
    reduce_scatter x1, waiting for transfers between devices, shards(): lax.psum_scatter(up_part, ('dp', 'hist'), scatter_dimension=0, tiled=True)  689 us
    reduce_scatter x1, waiting for transfers between devices, shards(): streams = lax.psum_scatter(total, 'hist', scatter_dimension=0, tiled=True)  517 us
    all_gather x1, waiting for transfers between devices, shards(): stream_all = lax.all_gather(stream_low, 'hist', axis=0, tiled=True)  296 us
    all_gather x1, waiting for transfers between devices, shards(): lax.all_gather(down_weight, ('dp', 'hist'), axis=1, tiled=True)  220 us
    reduce_scatter x1, waiting for transfers between devices, shards(): lax.psum_scatter(query_part, ('dp', 'hist'), scatter_dimension=0, tiled=T...  183 us
    reduce_scatter x1, waiting for transfers between devices, shards(): lax.psum_scatter(value_part, ('dp', 'hist'), scatter_dimension=0, tiled=T...  183 us
    reduce_scatter x1, waiting for transfers between devices, shards(): lax.psum_scatter(key_part, ('dp', 'hist'), scatter_dimension=0, tiled=True)  173 us
  transfers between devices with their start and end apart: 23, of which 15 were waited for; matrix products, arithmetic and copies ran while one was open for 13% of the time, Pallas kernels for 0%

commit v1 on v0

v1 whole, which is shorter than its diff:
```python
import jax
import jax.numpy as jnp
from jax import lax
from jax.experimental import pallas as pl
from jax.experimental.pallas import tpu as pltpu
from jax.sharding import PartitionSpec as P

HD = 128
ROT = 32
STREAMS = 4
LANES = 128
GROUP = 16

HIGHEST = lax.Precision.HIGHEST
EPS_NORM = 1e-05
EPS_RMS = 1e-06
ROPE_BASE = 10000.0
VMEM = 56 * 2**20
PLANE = ("hist", "mp")


def dot(left, right, contract):
    return lax.dot_general(
        left, right, (((contract[0],), (contract[1],)), ((), ())), preferred_element_type=jnp.float32
    )


def gelu_exact(value):
    return 0.5 * value * (1.0 + lax.erf(value * 0.7071067811865476))


def gelu_slope(value):
    return (
        0.5 * (1.0 + lax.erf(value * 0.7071067811865476))
        + value * jnp.exp(-0.5 * value * value) * 0.3989422804014327
    )


class Plane:
    def __init__(self):
        self.size = lax.axis_size("hist")
        self.cores = lax.axis_size("mp")
        self.bits = self.size.bit_length() - 1
        assert self.size == 1 << self.bits
        self.h = lax.axis_index("hist")
        self.m = lax.axis_index("mp")

    def turned(self, j):
        return sum(((j >> b) & 1) << (self.bits - 1 - b) for b in range(self.bits))

    def place(self, j):
        return jnp.where(self.m % 2 == 0, j, self.turned(j))

    def step(self, value, i):
        pairs = []
        for h in range(self.size):
            for m in range(self.cores):
                bit = 1 << (i if m % 2 == 0 else self.bits - 1 - i)
                pairs.append((h * self.cores + m, (h ^ bit) * self.cores + m))
        return lax.ppermute(value, PLANE, pairs)

    def gather(self, value):
        slots = [value]
        for i in range(self.bits):
            slots = slots + [self.step(s, i) for s in slots]
        return slots

    def scatter(self, held):
        for i in reversed(range(self.bits)):
            got = [self.step(x, i) for x in held[1 << i :]]
            held = [
                (x.astype(jnp.float32) + y.astype(jnp.float32)).astype(jnp.bfloat16)
                for x, y in zip(held[: 1 << i], got)
            ]
        return held[0]

    def ordered(self, slots):
        rows = slots[0].shape[0]
        out = jnp.zeros((self.size * rows,) + slots[0].shape[1:], slots[0].dtype)
        for j, slot in enumerate(slots):
            out = lax.dynamic_update_slice_in_dim(out, slot, (self.h ^ self.place(j)) * rows, 0)
        return out

    def trade(self, wide):
        cols = wide.shape[1] // self.size
        block = lambda r: lax.dynamic_slice_in_dim(wide, (self.h ^ r) * cols, cols, 1)
        return [block(0)] + [
            lax.ppermute(block(r), "hist", [(h, h ^ r) for h in range(self.size)]) for r in range(1, self.size)
        ]

    def trade_rows(self, tall):
        rows = tall.shape[0] // self.size
        block = lambda r: lax.dynamic_slice_in_dim(tall, (self.h ^ r) * rows, rows, 0)
        return [block(0)] + [
            lax.ppermute(block(r), "hist", [(h, h ^ r) for h in range(self.size)]) for r in range(1, self.size)
        ]

    def stacked(self, entries):
        rows = entries[0].shape[0]
        out = jnp.zeros((self.size * rows,) + entries[0].shape[1:], entries[0].dtype)
        for r, entry in enumerate(entries):
            out = lax.dynamic_update_slice_in_dim(out, entry, (self.h ^ r) * rows, 0)
        return out

    def swap(self, value):
        return lax.ppermute(value, "mp", [(m, m ^ 1) for m in range(self.cores)])

    def both(self, own, sibling, axis):
        first = self.m % 2 == 0
        return jnp.stack([jnp.where(first, own, sibling), jnp.where(first, sibling, own)], axis)


def forward_kernel(count, pick, *refs):
    slots = refs[:count]
    in_ref, out_ref, bias_ref, gain_ref = refs[count : count + 4]
    normed = refs[count + 4 : count + 4 + STREAMS]
    mix_ref, pre_ref, stat_ref, last_ref = refs[count + 4 + STREAMS :]
    for j in range(count):

        @pl.when(pick[0] == j)
        def _(j=j):
            last_ref[...] = slots[j][...]

    tile = last_ref.shape[0]
    last = last_ref[...].astype(jnp.float32)
    inverse = lax.rsqrt(jnp.mean(last * last, -1, keepdims=True) + EPS_RMS)
    unit = (last * inverse).astype(jnp.bfloat16)
    pre = jnp.dot(unit, in_ref[...], preferred_element_type=jnp.float32)
    pre_ref[...] = pre
    hidden = gelu_exact(pre).astype(jnp.bfloat16)
    mix_ref[...] = (
        jnp.dot(hidden, out_ref[...], preferred_element_type=jnp.float32) + bias_ref[...]
    )
    lane = lax.broadcasted_iota(jnp.int32, (GROUP, LANES), 1)

    def group(g, carry):
        rows = pl.ds(pl.multiple_of(g * GROUP, GROUP), GROUP)
        mix = mix_ref[rows, :]
        parts = [s[rows, :].astype(jnp.float32) for s in slots]
        stat = jnp.zeros((GROUP, LANES), jnp.float32)
        for c in range(STREAMS):
            stream = mix[:, c * count : c * count + 1] * parts[0]
            for j in range(1, count):
                stream = stream + mix[:, c * count + j : c * count + j + 1] * parts[j]
            centered = stream - jnp.mean(stream, -1, keepdims=True)
            scale = lax.rsqrt(jnp.mean(centered * centered, -1, keepdims=True) + EPS_NORM)
            normed[c][rows, :] = (centered * scale * gain_ref[c : c + 1, :]).astype(jnp.bfloat16)
            stat = jnp.where(lane == c, scale, stat)
        stat_ref[rows, :] = stat
        return carry

    lax.fori_loop(0, tile // GROUP, group, 0)


def forward_streams(slots, pick, mixer_in, mixer_out, bias, gain):
    count = len(slots)
    rows, width = slots[0].shape
    tile = min(128, rows)
    whole = lambda shape: pl.BlockSpec(shape, lambda i: (0,) * len(shape))
    by_row = lambda cols: pl.BlockSpec((tile, cols), lambda i: (i, 0))
    return pl.pallas_call(
        lambda *refs: forward_kernel(count, *refs),
        grid=(rows // tile,),
        in_specs=[pl.BlockSpec(memory_space=pltpu.SMEM)]
        + [by_row(width)] * count
        + [whole(mixer_in.shape), whole(mixer_out.shape), whole(bias.shape), whole(gain.shape)],
        out_specs=[by_row(width)] * STREAMS + [by_row(LANES)] * 3,
        out_shape=[jax.ShapeDtypeStruct((rows, width), jnp.bfloat16)] * STREAMS
        + [jax.ShapeDtypeStruct((rows, LANES), jnp.float32)] * 3,
        scratch_shapes=[pltpu.VMEM((tile, width), jnp.bfloat16)],
        compiler_params=pltpu.CompilerParams(vmem_limit_bytes=VMEM),
        cost_estimate=pl.CostEstimate(
            flops=rows * width * 80, bytes_accessed=rows * width * 2 * (count + STREAMS), transcendentals=0
        ),
        name="forward_streams",
    )(pick, *slots, mixer_in, mixer_out, bias, gain)


def split_dot(left, right, contract):
    high = right.astype(jnp.bfloat16)
    low = (right - high.astype(jnp.float32)).astype(jnp.bfloat16)
    return dot(left, high, contract) + dot(left, low, contract)


def backward_kernel(count, pick, *refs):
    slots, refs = refs[:count], refs[count:]
    mine, refs = refs[:STREAMS], refs[STREAMS:]
    theirs, refs = refs[:STREAMS], refs[STREAMS:]
    normed, refs = refs[:STREAMS], refs[STREAMS:]
    mix_ref, pre_ref, stat_ref, target_ref, scale_ref, refs = *refs[:5], refs[5:]
    in_ref, out_ref, gain_ref, inverse_gain_ref, refs = *refs[:4], refs[4:]
    grads, refs = refs[:count], refs[count:]
    gain_grad_ref, in_grad_ref, out_grad_ref, bias_grad_ref, last_ref, dmix_ref, gain_sum = refs
    tile = last_ref.shape[0]

    @pl.when(pl.program_id(0) == 0)
    def _():
        gain_sum[...] = jnp.zeros_like(gain_sum)
        in_grad_ref[...] = jnp.zeros_like(in_grad_ref)
        out_grad_ref[...] = jnp.zeros_like(out_grad_ref)
        bias_grad_ref[...] = jnp.zeros_like(bias_grad_ref)

    for j in range(count):

        @pl.when(pick[0] == j)
        def _(j=j):
            last_ref[...] = slots[j][...]

    lane = lax.broadcasted_iota(jnp.int32, (GROUP, LANES), 1)

    def group(g, carry):
        rows = pl.ds(pl.multiple_of(g * GROUP, GROUP), GROUP)
        mix = mix_ref[rows, :]
        stat = stat_ref[rows, :]
        dmix = jnp.zeros((GROUP, LANES), jnp.float32)
        grad = []
        for c in range(STREAMS):
            total = mine[c][rows, :].astype(jnp.float32) + theirs[c][rows, :].astype(jnp.float32)
            unit = normed[c][rows, :].astype(jnp.float32) * inverse_gain_ref[c : c + 1, :]
            product = total * unit
            gain_sum[c] += product[:8] + product[8:]
            scaled = total * gain_ref[c : c + 1, :]
            mean = jnp.mean(scaled, -1, keepdims=True)
            along = jnp.mean(product * gain_ref[c : c + 1, :], -1, keepdims=True)
            one = stat[:, c : c + 1] * (scaled - mean - unit * along)
            if c == STREAMS - 1:
                one = one + target_ref[rows, :].astype(jnp.float32) * scale_ref[rows, :1]
            grad.append(one)
        for j in range(count):
            part = slots[j][rows, :].astype(jnp.float32)
            total = mix[:, j : j + 1] * grad[0]
            for c in range(1, STREAMS):
                total = total + mix[:, c * count + j : c * count + j + 1] * grad[c]
            grads[j][rows, :] = total.astype(jnp.bfloat16)
            for c in range(STREAMS):
                value = jnp.sum(grad[c] * part, -1, keepdims=True)
                dmix = jnp.where(lane == c * count + j, value, dmix)
        dmix_ref[rows, :] = dmix
        return carry

    lax.fori_loop(0, tile // GROUP, group, 0)
    dmix = dmix_ref[...]
    last = last_ref[...].astype(jnp.float32)
    inverse = lax.rsqrt(jnp.mean(last * last, -1, keepdims=True) + EPS_RMS)
    unit = (last * inverse).astype(jnp.bfloat16)
    pre = pre_ref[...]
    hidden = gelu_exact(pre).astype(jnp.bfloat16)
    hidden_grad = lax.dot_general(
        dmix,
        out_ref[...].astype(jnp.float32),
        (((1,), (1,)), ((), ())),
        precision=HIGHEST,
        preferred_element_type=jnp.float32,
    )
    pre_grad = hidden_grad * gelu_slope(pre)
    in_grad_ref[...] += split_dot(unit, pre_grad, (0, 0))
    out_grad_ref[...] += split_dot(hidden, dmix, (0, 0))
    bias_grad_ref[...] += jnp.sum(dmix, 0, keepdims=True)
    high = pre_grad.astype(jnp.bfloat16)
    low = (pre_grad - high.astype(jnp.float32)).astype(jnp.bfloat16)
    unit_grad = dot(high, in_ref[...], (1, 1)) + dot(low, in_ref[...], (1, 1))
    cube = inverse * inverse * inverse * jnp.mean(unit_grad * last, -1, keepdims=True)
    extra = inverse * unit_grad - last * cube
    for j in range(count):

        @pl.when(pick[0] == j)
        def _(j=j):
            grads[j][...] = (grads[j][...].astype(jnp.float32) + extra).astype(jnp.bfloat16)

    @pl.when(pl.program_id(0) == pl.num_programs(0) - 1)
    def _():
        gain_grad_ref[...] = jnp.sum(gain_sum[...], 1)


def backward_streams(slots, mine, theirs, at, normed, mix, pre, stat, target, scale, pick, mixer_in, mixer_out, gain):
    count = len(slots)
    rows, width = slots[0].shape
    tile = min(128, rows)
    steps = rows // tile
    whole = lambda shape: pl.BlockSpec(shape, lambda i: (0,) * len(shape))
    by_row = lambda cols: pl.BlockSpec((tile, cols), lambda i: (i, 0))
    shifted = pl.BlockSpec((tile, width), lambda i: (at * steps + i, 0))
    hidden = mixer_in.shape[1]
    return pl.pallas_call(
        lambda *refs: backward_kernel(count, *refs),
        grid=(steps,),
        in_specs=[pl.BlockSpec(memory_space=pltpu.SMEM)]
        + [by_row(width)] * count
        + [shifted] * (2 * STREAMS)
        + [by_row(width)] * STREAMS
        + [by_row(LANES)] * 3
        + [by_row(width), by_row(LANES)]
        + [whole(mixer_in.shape), whole(mixer_out.shape), whole(gain.shape), whole(gain.shape)],
        out_specs=[by_row(width)] * count
        + [whole((STREAMS, width)), whole((width, hidden)), whole((hidden, LANES)), whole((1, LANES))],
        out_shape=[jax.ShapeDtypeStruct((rows, width), jnp.bfloat16)] * count
        + [
            jax.ShapeDtypeStruct((STREAMS, width), jnp.float32),
            jax.ShapeDtypeStruct((width, hidden), jnp.float32),
            jax.ShapeDtypeStruct((hidden, LANES), jnp.float32),
            jax.ShapeDtypeStruct((1, LANES), jnp.float32),
        ],
        scratch_shapes=[
            pltpu.VMEM((tile, width), jnp.bfloat16),
            pltpu.VMEM((tile, LANES), jnp.float32),
            pltpu.VMEM((STREAMS, 8, width), jnp.float32),
        ],
        compiler_params=pltpu.CompilerParams(vmem_limit_bytes=VMEM),
        cost_estimate=pl.CostEstimate(
            flops=rows * width * 160,
            bytes_accessed=rows * width * 2 * (2 * count + 3 * STREAMS),
            transcendentals=0,
        ),
        name="backward_streams",
    )(pick, *slots, *mine, *theirs, *normed, mix, pre, stat, target, scale, mixer_in, mixer_out, gain, 1.0 / gain)


def rope_tables(positions):
    side = ROT // 2
    freq = ROPE_BASE ** (-2.0 * jnp.arange(side, dtype=jnp.float32) / ROT)
    angle = positions.astype(jnp.float32)[:, None] * freq[None, :]
    cosine, sine = jnp.cos(angle), jnp.sin(angle)
    rest = HD - ROT
    return (
        jnp.pad(jnp.concatenate([cosine, cosine], 1), ((0, 0), (0, rest)), constant_values=1.0),
        jnp.pad(-sine, ((0, 0), (0, HD - side))),
        jnp.pad(sine, ((0, 0), (side, rest))),
    )


def turn(value, cosine, right, left, sign):
    side = ROT // 2
    moved = pltpu.roll(value, HD - side, 1) * right + pltpu.roll(value, side, 1) * left
    return value * cosine + moved * sign


def attention_kernel(count, half, heads, which, *refs):
    q_ref, k_ref, v_ref, g_ref, cos_ref, right_ref, left_ref = refs[:7]
    o_ref, dq_ref, dk_ref, dv_ref = refs[7:11]
    k_s, dk_s, dv_s, p_s, o_s, dq_s, top_s, sum_s = refs[11:]
    blocks = 2 * count
    scale = HD ** (-0.5)
    bf16, f32 = jnp.bfloat16, jnp.float32
    m = which[0]

    def at(b):
        return pl.ds(pl.multiple_of(((lax.rem(b, 2) ^ m) * count + lax.div(b, 2)) * half, half), half)

    def cols(n):
        return slice(n * HD, (n + 1) * HD)

    def prepare(b, carry):
        rows = pl.ds(pl.multiple_of(b * half, half), half)
        for n in range(heads):
            k_s[rows, cols(n)] = turn(
                k_ref[rows, cols(n)], cos_ref[rows, :], right_ref[rows, :], left_ref[rows, :], 1.0
            ).astype(bf16)
        dk_s[rows, :] = jnp.zeros((half, heads * HD), f32)
        dv_s[rows, :] = jnp.zeros((half, heads * HD), f32)
        return carry

    lax.fori_loop(0, blocks, prepare, 0)
    later = lax.broadcasted_iota(jnp.int32, (half, half), 1) > lax.broadcasted_iota(jnp.int32, (half, half), 0)

    def lanes(value, op):
        parts = [value[:, i : i + LANES] for i in range(0, value.shape[1], LANES)]
        out = parts[0]
        for part in parts[1:]:
            out = op(out, part)
        return out

    def query_block(i, carry):
        here = at(i)
        queries = [
            turn(
                q_ref[here, cols(n)], cos_ref[here, :], right_ref[here, :], left_ref[here, :], 1.0
            ).astype(bf16)
            for n in range(heads)
        ]
        grads = [g_ref[here, cols(n)] for n in range(heads)]

        def scores(j, last):
            there = at(j)
            for n in range(heads):
                s = dot(queries[n], k_s[there, cols(n)], (1, 1)) * scale
                if last:
                    s = jnp.where(later, -1e30, s)
                p_s[n, :, pl.ds(pl.multiple_of(j * half, half), half)] = s
                top = lanes(s, jnp.maximum)
                top_s[n] = jnp.maximum(top_s[n], top)

        top_s[...] = jnp.full(top_s.shape, -1e30, f32)
        lax.fori_loop(0, i, lambda j, c: (scores(j, False), c)[1], 0)
        scores(i, True)
        tops = [jnp.max(top_s[n], -1, keepdims=True) for n in range(heads)]
        o_s[...] = jnp.zeros(o_s.shape, f32)
        dq_s[...] = jnp.zeros(dq_s.shape, f32)
        sum_s[...] = jnp.zeros(sum_s.shape, f32)

        def mixing(j, c):
            there = at(j)
            spot = pl.ds(pl.multiple_of(j * half, half), half)
            for n in range(heads):
                p = jnp.exp(p_s[n, :, spot] - tops[n])
                p_s[n, :, spot] = p
                sum_s[n] += lanes(p, jnp.add)
                o_s[n] += dot(p.astype(bf16), v_ref[there, cols(n)], (1, 0))
            return c

        lax.fori_loop(0, i + 1, mixing, 0)
        shares, deltas = [], []
        for n in range(heads):
            share = 1.0 / jnp.sum(sum_s[n], -1, keepdims=True)
            found = o_s[n] * share
            o_ref[here, cols(n)] = found.astype(bf16)
            shares.append(share)
            deltas.append(jnp.sum(found * grads[n].astype(f32), -1, keepdims=True))

        def back(j, c):
            there = at(j)
            spot = pl.ds(pl.multiple_of(j * half, half), half)
            for n in range(heads):
                p = p_s[n, :, spot] * shares[n]
                dp = dot(grads[n], v_ref[there, cols(n)], (1, 1))
                ds = (p * (dp - deltas[n])).astype(bf16)
                dq_s[n] += dot(ds, k_s[there, cols(n)], (1, 0))
                dk_s[there, cols(n)] += dot(ds, queries[n], (0, 0))
                dv_s[there, cols(n)] += dot(p.astype(bf16), grads[n], (0, 0))
            return c

        lax.fori_loop(0, i + 1, back, 0)
        for n in range(heads):
            dq_ref[here, cols(n)] = turn(
                dq_s[n] * scale, cos_ref[here, :], right_ref[here, :], left_ref[here, :], -1.0
            ).astype(bf16)
        return carry

    lax.fori_loop(0, blocks, query_block, 0)

    def finish(b, carry):
        rows = pl.ds(pl.multiple_of(b * half, half), half)
        for n in range(heads):
            dk_ref[rows, cols(n)] = turn(
                dk_s[rows, cols(n)] * scale, cos_ref[rows, :], right_ref[rows, :], left_ref[rows, :], -1.0
            ).astype(bf16)
        dv_ref[rows, :] = dv_s[rows, :].astype(bf16)
        return carry

    lax.fori_loop(0, blocks, finish, 0)


def attention(query, keys, values, grad, positions, which, count):
    rows, piece = query.shape
    heads, half = piece // HD, rows // (2 * count)
    vmem = pl.BlockSpec(memory_space=pltpu.VMEM)
    out = jax.ShapeDtypeStruct((rows, piece), jnp.bfloat16)
    wide = lambda *shape: pltpu.VMEM(shape, jnp.float32)
    return pl.pallas_call(
        lambda *refs: attention_kernel(count, half, heads, *refs),
        in_specs=[pl.BlockSpec(memory_space=pltpu.SMEM)] + [vmem] * 7,
        out_specs=[vmem] * 4,
        out_shape=[out] * 4,
        scratch_shapes=[
            pltpu.VMEM((rows, piece), jnp.bfloat16),
            wide(rows, piece),
            wide(rows, piece),
            wide(heads, half, rows),
            wide(heads, half, HD),
            wide(heads, half, HD),
            wide(heads, half, LANES),
            wide(heads, half, LANES),
        ],
        compiler_params=pltpu.CompilerParams(vmem_limit_bytes=VMEM),
        cost_estimate=pl.CostEstimate(
            flops=6 * rows * rows * piece, bytes_accessed=rows * piece * 20, transcendentals=rows * rows * heads // 2
        ),
        name="attention",
    )(which, query, keys, values, grad, *rope_tables(positions))


def interleave(own, sibling, m):
    count = len(own)
    half, width = own[0].shape

    def kernel(which, *refs):
        out, sems = refs[2 * count], refs[2 * count + 1]
        copies = []
        for a in range(count):
            copies.append(pltpu.make_async_copy(refs[a], out.at[a, which[0]], sems.at[a]))
            copies.append(pltpu.make_async_copy(refs[count + a], out.at[a, 1 - which[0]], sems.at[count + a]))
        for copy in copies:
            copy.start()
        for copy in copies:
            copy.wait()

    return pl.pallas_call(
        kernel,
        in_specs=[pl.BlockSpec(memory_space=pltpu.SMEM)] + [pl.BlockSpec(memory_space=pl.ANY)] * (2 * count),
        out_specs=pl.BlockSpec(memory_space=pl.ANY),
        out_shape=jax.ShapeDtypeStruct((count, 2, half, width), own[0].dtype),
        scratch_shapes=[pltpu.SemaphoreType.DMA((2 * count,))],
        name="interleave",
    )(m, *own, *sibling)


def place_wide(entries, h, out_type, pieces, turned):
    count = len(entries)
    depth, cols = entries[0].shape
    size = cols // pieces

    def kernel(which, *refs):
        a = pl.program_id(0)
        for r in range(count):

            @pl.when((which[0] ^ a) == r)
            def _(r=r):
                for i in range(pieces):
                    block = refs[r][:, i * size : (i + 1) * size].astype(jnp.float32)
                    refs[count + i][...] = block.T if turned[i] else block

    return pl.pallas_call(
        kernel,
        grid=(count,),
        in_specs=[pl.BlockSpec(memory_space=pltpu.SMEM)] + [pl.BlockSpec((depth, cols), lambda a: (0, 0))] * count,
        out_specs=[
            pl.BlockSpec((size, depth), lambda a: (a, 0)) if t else pl.BlockSpec((depth, size), lambda a: (0, a))
            for t in turned
        ],
        out_shape=[
            jax.ShapeDtypeStruct((count * size, depth) if t else (depth, count * size), out_type) for t in turned
        ],
        compiler_params=pltpu.CompilerParams(vmem_limit_bytes=VMEM),
        name="place_wide",
    )(h, *entries)


def after(value, *others):
    return lax.optimization_barrier((value,) + others)[0]


def shards(
    history,
    mixer_in,
    mixer_out,
    mixer_bias,
    norm_gain,
    query_weight,
    key_weight,
    value_weight,
    out_weight,
    up_weight,
    down_weight,
    target,
    loss_count,
    domain,
    domain_scale,
):
    plane = Plane()
    count, cores, h, m = plane.size, plane.cores, plane.h, plane.m
    layers, group_rows, width = history.shape
    rows = target.shape[0]
    half = rows // cores
    depth = query_weight.shape[0]
    assert layers == 1 and cores == 2 and domain.shape[0] == 1 and group_rows == count * rows
    hidden_units = mixer_in.shape[1]
    bf16, f32 = jnp.bfloat16, jnp.float32

    near = count * half
    which_m = m.astype(jnp.int32).reshape(1)
    which_h = h.astype(jnp.int32).reshape(1)

    z, zs = lax.axis_index("dp"), lax.axis_size("dp")
    part = plane.ordered([x[None] for x in plane.gather(norm_gain)])
    gain = lax.dynamic_update_slice_in_dim(jnp.zeros((zs,) + part.shape, bf16), part[None], z, 0)
    for k in range(1, zs):
        came = lax.ppermute(part, "dp", [(i, (i + k) % zs) for i in range(zs)])
        gain = lax.dynamic_update_slice_in_dim(gain, came[None], (z + zs - k) % zs, 0)
    gain = gain.reshape(zs * count, STREAMS, -1).transpose(1, 0, 2).reshape(STREAMS, width).astype(f32)

    parted = history.reshape(count, cores, half, width)
    own_rows = [lax.dynamic_index_in_dim(parted[a], m, 0, keepdims=False) for a in range(count)]
    up_parts = plane.trade(up_weight)
    up_full = lax.all_gather(plane.stacked(up_parts), "dp", axis=0, tiled=True)
    slots, waited = [], up_parts[-1]
    marks = []
    for a in range(count):
        found = plane.gather(after(own_rows[a], waited))
        waited = found[1]
        marks.append(waited)
        slots.append(found)
    down_parts = plane.trade(after(down_weight, marks[0]).T)
    down_full = lax.all_gather(plane.stacked(down_parts), "dp", axis=0, tiled=True)
    packed = jnp.stack(
        [query_weight, key_weight, value_weight, after(out_weight, marks[min(1, count - 1)]).T], 0
    )
    packed = packed.reshape(4, depth, count, -1).transpose(1, 2, 0, 3).reshape(depth, -1)
    narrow_full = lax.all_gather(plane.stacked(plane.trade(packed)), "dp", axis=0, tiled=True)
    piece = narrow_full.shape[1] // 4
    query_full, key_full, value_full, out_full = (
        narrow_full[:, i * piece : (i + 1) * piece] for i in range(4)
    )

    layer_of = [h ^ plane.place(j) for j in range(count)]
    pick = sum(jnp.where(layer_of[j] == count - 1, j, 0) for j in range(count)).astype(jnp.int32).reshape(1)

    def to_slots(values):
        return jnp.stack(
            [sum(jnp.where(layer_of[j] == l, values[..., l], 0) for l in range(count)) for j in range(count)], -1
        )

    def from_slots(values):
        return jnp.stack(
            [sum(jnp.where(layer_of[j] == l, values[..., j], 0) for j in range(count)) for l in range(count)], -1
        )

    pairs = STREAMS * count
    in_wide = jnp.pad(mixer_in, ((0, 0), (0, LANES - hidden_units)))
    out_wide = jnp.pad(
        to_slots(mixer_out).reshape(hidden_units, pairs), ((0, LANES - hidden_units), (0, LANES - pairs))
    )
    bias_wide = jnp.pad(to_slots(mixer_bias).reshape(1, pairs), ((0, 0), (0, LANES - pairs)))

    normed, mixes, pres, stats, others = [], [], [], [], []
    for a in range(count):
        *one, mix, pre, stat = forward_streams(slots[a], pick, in_wide, out_wide, bias_wide, gain)
        normed.append(one)
        mixes.append(mix)
        pres.append(pre)
        stats.append(stat)
        others.append([plane.swap(x) for x in one])
    streams = [jnp.concatenate([x[c] for x in normed + others], 0) for c in range(STREAMS)]
    block = jnp.arange(count)[:, None] * rows + jnp.arange(half)[None, :]
    positions = jnp.concatenate([(block + m * half).reshape(-1), (block + (1 - m) * half).reshape(-1)])

    domain_one = jnp.sum(jnp.where(jnp.arange(domain_scale.shape[0]) == domain[0], domain_scale, 0.0))
    own_target = lax.dynamic_slice_in_dim(target, m * half, half, 0)
    own_scale = lax.dynamic_slice_in_dim(loss_count, m * half, half, 0).astype(f32) * domain_one
    branch_own = (own_target.astype(f32) * own_scale[:, None]).astype(bf16)
    branch_near = plane.ordered(plane.gather(after(branch_own, marks[-1])))
    branch_grad = jnp.concatenate([branch_near, plane.swap(branch_near)], 0)

    hidden_pre = dot(streams[3], up_full, (1, 0))
    hidden = gelu_exact(hidden_pre).astype(bf16)
    act_grad = dot(branch_grad, down_full, (1, 0))
    pre_grad = (act_grad * gelu_slope(hidden_pre)).astype(bf16)
    down_part = dot(branch_grad, hidden, (0, 0)).astype(bf16)
    up_part = dot(streams[3], pre_grad, (0, 0)).astype(bf16)

    streams[0], streams[1], streams[2] = lax.optimization_barrier(
        (streams[0], streams[1], streams[2], up_part, down_part)
    )[:3]
    query = dot(streams[0], query_full, (1, 0))
    keys = dot(streams[1], key_full, (1, 0))
    values = dot(streams[2], value_full, (1, 0)).astype(bf16)
    attended_grad = dot(branch_grad, out_full, (1, 0)).astype(bf16)
    attended, query_back, key_back, value_back = attention(
        query, keys, values, attended_grad, positions, which_m, count
    )

    branch_far = (
        dot(attended[near:], out_full, (1, 1)) + dot(hidden[near:], down_full, (1, 1))
    ).astype(bf16)
    query_back, key_back, value_back, branch_far = lax.optimization_barrier(
        (query_back, key_back, value_back, branch_far)
    )
    branch = dot(attended[:near], out_full, (1, 1)) + dot(hidden[:near], down_full, (1, 1))
    branch_sum = (branch + plane.swap(branch_far).astype(f32)).astype(bf16)
    branch_rows = plane.scatter(
        [lax.dynamic_slice_in_dim(branch_sum, layer_of[j] * half, half, 0) for j in range(count)]
    ).astype(f32)
    own_mix = lax.dynamic_index_in_dim(jnp.stack(mixes, 0), h, 0, keepdims=False)[:, :pairs]
    own_mix = own_mix.reshape(half, STREAMS, count)
    own_layers = [lax.dynamic_index_in_dim(jnp.stack([s[j] for s in slots], 0), h, 0, keepdims=False) for j in range(count)]
    residual = sum(own_mix[:, STREAMS - 1, j, None] * own_layers[j].astype(f32) for j in range(count))
    output_own = (residual + branch_rows).astype(bf16)
    output = plane.both(output_own, plane.swap(output_own), 0).reshape(rows, width)
    mix_own = from_slots(own_mix)
    mix_rows = plane.both(mix_own, plane.swap(mix_own), 0).reshape(rows, STREAMS, count)

    tails = [
        (query_back, query_full),
        (key_back, key_full),
        (value_back, value_full),
        (pre_grad, up_full),
    ]
    theirs = [plane.swap(dot(x[near:], w, (1, 1)).astype(bf16)) for x, w in tails]
    mine = [dot(x[:near], w, (1, 1)).astype(bf16) for x, w in tails]

    narrow_part = jnp.concatenate(
        [
            dot(streams[0], query_back, (0, 0)),
            dot(streams[1], key_back, (0, 0)),
            dot(streams[2], value_back, (0, 0)),
            dot(branch_grad, attended, (0, 0)),
        ],
        1,
    ).astype(bf16)

    def spread(part, turned):
        summed = lax.psum_scatter(part, "dp", scatter_dimension=0, tiled=True)
        return place_wide(plane.trade_rows(summed), which_h, f32, len(turned), turned)

    (up_grad,) = spread(up_part, (False,))
    (down_grad,) = spread(down_part, (True,))
    query_grad, key_grad, value_grad, out_grad = spread(narrow_part, (False, False, False, True))

    scale_wide = after(jnp.broadcast_to(own_scale[:, None], (half, LANES)), narrow_part)
    finals, sums = [], None
    for a in range(count):
        scale = jnp.where(h == a, scale_wide, 0.0)
        found = backward_streams(
            slots[a], mine, theirs, a, normed[a], mixes[a], pres[a], stats[a], own_target, scale, pick, in_wide, out_wide, gain
        )
        held, rest = list(found[:count]), found[count:]
        sums = rest if sums is None else tuple(x + y for x, y in zip(sums, rest))
        finals.append(plane.scatter(held))
    history_grad = interleave(finals, [plane.swap(x) for x in finals], which_m).reshape(history.shape)

    gain_sum, in_sum, out_sum, bias_sum = sums
    out_sum = from_slots(out_sum[:, :pairs].reshape(LANES, STREAMS, count)).reshape(LANES, pairs)
    bias_sum = from_slots(bias_sum[:, :pairs].reshape(1, STREAMS, count)).reshape(1, pairs)
    small = jnp.concatenate(
        [in_sum, gain_sum.T, jnp.pad(jnp.concatenate([out_sum, bias_sum], 0), ((0, width - LANES - 1), (0, 0)))], 1
    )
    small = lax.psum(small, ("dp", "hist", "mp"))
    mixer_in_grad = small[:, :hidden_units]
    gain_all = small[:, LANES : LANES + STREAMS].T
    place = (lax.axis_index("dp") * count + h) * norm_gain.shape[1]
    norm_gain_grad = lax.dynamic_slice_in_dim(gain_all, place, norm_gain.shape[1], 1)
    tail = small[:, LANES + STREAMS :]
    mixer_out_grad = tail[:hidden_units].reshape(hidden_units, STREAMS, count)
    mixer_bias_grad = tail[LANES].reshape(STREAMS, count)
    return (
        output,
        mix_rows,
        history_grad,
        mixer_in_grad,
        mixer_out_grad,
        mixer_bias_grad,
        norm_gain_grad,
        query_grad,
        key_grad,
        value_grad,
        out_grad,
        up_grad,
        down_grad,
    )


def solution(mesh):
    in_specs = (
        P("hist", "dp", None),
        P(),
        P(),
        P(),
        P(None, ("dp", "hist")),
        P(("dp", "hist"), "mp"),
        P(("dp", "hist"), "mp"),
        P(("dp", "hist"), "mp"),
        P("mp", ("dp", "hist")),
        P(("dp", "hist"), "mp"),
        P("mp", ("dp", "hist")),
        P(("dp", "hist"), None),
        P(("dp", "hist")),
        P("dp"),
        P(),
    )
    out_specs = (
        P(("dp", "hist"), None),
        P(("dp", "hist"), None, None),
        P("hist", "dp", None),
        P(),
        P(),
        P(),
        P(None, ("dp", "hist")),
        P(("dp", "hist"), "mp"),
        P(("dp", "hist"), "mp"),
        P(("dp", "hist"), "mp"),
        P("mp", ("dp", "hist")),
        P(("dp", "hist"), "mp"),
        P("mp", ("dp", "hist")),
    )
    return jax.shard_map(shards, mesh=mesh, in_specs=in_specs, out_specs=out_specs, check_vma=False)
```

time: 4160 us -> 1220 us (0.29)
  waiting for transfers between devices: 3410 us -> 339 us
  Pallas kernels: 0 us -> 455 us
  matrix products: 396 us -> 176 us
  other arithmetic: 169 us -> 34.7 us
  blocking collectives: 117 us -> 0 us
  starting transfers between devices: 1.95 us -> 88.1 us
  local copies, waits for them, and re-layouts: 40.2 us -> 108 us
    reduce_scatter x9 -> x3, waiting for transfers between devices: 2440 us -> 80.4 us  [spread(): summed = lax.psum_scatter(part, 'dp', scatter_dimension=0, tiled=True)]
    all_gather x9 -> x3, waiting for transfers between devices: 775 us -> 0.02 us  [the longest x1 0.02 us: shards(): lax.all_gather(plane.stacked(down_parts), 'dp', axis=0, tiled=True)]
    pallas_call x0 -> x13, Pallas kernels: none -> 455 us  [the longest x1 255 us: interleave(): pl.pallas_call(kernel, in_specs=[pl.BlockSpec(memory_space=pltpu.SMEM)] +...]
    ppermute x0 -> x82, waiting for transfers between devices: none -> 258 us  [the longest x33 214 us: step(): return lax.ppermute(value, PLANE, pairs)]
    dot_general x31 -> x24, matrix products: 378 us -> 176 us  [dot(): lax.dot_general(left, right, (((contract[0],), (contract[1],)), ((), ()))...]
    psum x4 -> x1, waiting for transfers between devices: 197 us -> 0.01 us  [shards(): small = lax.psum(small, ('dp', 'hist', 'mp'))]
    ppermute x0 -> x82, starting transfers between devices: none -> 87.8 us  [the longest x33 36.6 us: step(): return lax.ppermute(value, PLANE, pairs)]
    psum x1 -> x0, blocking collectives: 77 us -> none  [shards(): lax.psum((in_grad, cols_grad, bias_grad), ('dp', 'hist'))]
  transfers between devices with their start and end apart: 23 -> 89, of which waited for: 15 -> 30; matrix products, arithmetic and copies ran while one was open for 13% -> 25% of each run, Pallas kernels for 0% -> 30%
where the time goes in v1:
time: 1220 us
  Pallas kernels  455 us (37%)
  waiting for transfers between devices  339 us (28%)
  matrix products  176 us (14%)
  local copies, waits for them, and re-layouts  108 us (9%)
  starting transfers between devices  88.1 us (7%)
  other arithmetic  34.7 us (3%)
  between operations  16.6 us (1%)
    pallas_call x1, Pallas kernels, interleave(): pl.pallas_call(kernel, in_specs=[pl.BlockSpec(memory_space=pltpu.SMEM)] +...  255 us
    ppermute x33, waiting for transfers between devices, step(): return lax.ppermute(value, PLANE, pairs)  214 us
    dot_general x24, matrix products, dot(): lax.dot_general(left, right, (((contract[0],), (contract[1],)), ((), ()))...  176 us
    pallas_call x4, Pallas kernels, backward_streams(): pl.pallas_call(lambda *refs: backward_kernel(count, *refs), grid=(steps,)...  85.6 us
    reduce_scatter x3, waiting for transfers between devices, spread(): summed = lax.psum_scatter(part, 'dp', scatter_dimension=0, tiled=True)  80.4 us
    pallas_call x1, Pallas kernels, attention(): pl.pallas_call(lambda *refs: attention_kernel(count, half, heads, *refs),...  60.7 us
    unnamed x246, local copies, waits for them, and re-layouts  57.4 us
    pallas_call x4, Pallas kernels, forward_streams(): pl.pallas_call(lambda *refs: forward_kernel(count, *refs), grid=(rows //...  44.2 us
  transfers between devices with their start and end apart: 89, of which 30 were waited for; matrix products, arithmetic and copies ran while one was open for 25% of the time, Pallas kernels for 30%

profile of v1, /device:TPU:0, one launch (start us, length us, event | category | flops | bytes accessed | tf_op | source)
XLA Modules:
  0.0 1217.9 jit_solution(13857833313239747001)
XLA Ops:
  35.9 10.9 collective-permute-done.1.refs_2_
  103.8 19.8 %collective-permute-done.10.refs_2_ = bf16[256,2048]{1,0:T(8,128)(2,1)} collective-permute-done((bf16[256,2048]{1,0:T(8,128)(2,1)S(1)}, bf16[256,2048]{1,0:T(8,128)(2,1)}, u32[]{:S(2)}, u32[]{:S(2)}) %collective-permute-start.10) | collective-permute-done | bytes 1048608 | tf_op jit(solution)/shard_map/ppermute | solution.py:60
  130.3 9.3 collective-permute-done.3.refs_4_
  141.1 11.0 forward_streams.4
  172.7 15.0 %collective-permute-start.19 = (bf16[256,2048]{1,0:T(8,128)(2,1)}, bf16[256,2048]{1,0:T(8,128)(2,1)}, u32[]{:S(2)}, u32[]{:S(2)}) collective-permute-start(bf16[256,2048]{1,0:T(8,128)(2,1)} %get-tuple-element.104.refs_13_), channel_id=1, source_target_pairs={{0,1},{1,0},{2,3},{3,2},{4,5},{5,4},{6,7},{7,6},{8,9},{9,8},{10,11... | collective-permute-start | bytes 3145736 | tf_op jit(solution)/shard_map/ppermute | solution.py:106
  187.8 11.0 forward_streams.5
  210.0 11.1 forward_streams.6
  233.6 11.1 forward_streams.7
  290.5 10.2 collective-permute-done.37
  305.9 25.9 %multiply_convert_fusion = (bf16[2048,1024]{1,0:T(8,128)(2,1)}, f32[2048,1024]{1,0:T(8,128)}) fusion(bf16[2048,2048]{1,0:T(8,128)(2,1)} %constant_dynamic-update-slice_fusion.24, bf16[2048,1024]{0,1:T(8,128)(2,1)} %all-gather.6.cloned.1.call-done), kind=kOutput, calls=%fused_computation.10 | convolution fusion | flops 8600420352 | bytes 25165824 | tf_op jit(solution)/shard_map/dot_general | solution.py:23
  331.8 10.7 fusion.8
  342.5 12.8 %convolution_convert_fusion.8 = bf16[2048,1024]{1,0:T(8,128)(2,1)} fusion(bf16[2048,1024]{1,0:T(8,128)(2,1)S(1)} %copy-done.98, bf16[1024,2048]{1,0:T(8,128)(2,1)} %collective-permute-done.38, bf16[1024,2048]{1,0:T(8,128)(2,1)} %constant_dynamic-update-slice_fusion.42), kind=kOutput, calls=%fused_computation.37 | convolution fusion | flops 8608808960 | bytes 16777216 | tf_op jit(solution)/shard_map/dot_general | solution.py:23
  355.2 15.5 %fusion.5 = bf16[2048,1024]{1,0:T(8,128)(2,1)S(1)} fusion(f32[2048,1024]{1,0:T(8,128)} %get-tuple-element.326, bf16[2048,1024]{0,1:T(8,128)(2,1)} %all-gather.4.cloned.1.call-done, bf16[1024,2048]{1,0:T(8,128)(2,1)} %collective-permute-done.38, bf16[1024,2048]{1,0:T(8,128)(2,1)} %constant_dynamic-update-slice_fusion.42), kind=kOutput, calls=%fused_computation.6 | convolution fusion | flops 8627683328 | bytes 25165824 | tf_op jit(solution)/shard_map/dot_general | solution.py:23
  372.8 13.2 %convolution_convert_fusion.9 = bf16[2048,1024]{1,0:T(8,128)(2,1)} fusion(bf16[2048,2048]{1,0:T(8,128)(2,1)} %constant_dynamic-update-slice_fusion.24, bf16[2048,1024]{1,0:T(8,128)(2,1)S(1)} %fusion.5), kind=kOutput, calls=%fused_computation.38 | convolution fusion | flops 8592031744 | bytes 16777216 | tf_op jit(solution)/shard_map/dot_general | solution.py:23
  386.0 9.4 convolution_convert_fusion.6
  395.9 7.2 convolution_convert_fusion.14.refs_4_
  421.2 60.7 %attention.1 = (bf16[2048,256]{1,0:T(8,128)(2,1)}, bf16[2048,256]{1,0:T(8,128)(2,1)}, bf16[2048,256]{1,0:T(8,128)(2,1)}, bf16[2048,256]{1,0:T(8,128)(2,1)}) custom-call(s32[1]{0:T(128)} %bitcast.49.refs_0_.which, f32[2048,256]{1,0:T(8,128)} %fusion.45.refs_1_, f32[2048,256]{1,0:T(8,128)} %fusion.41.refs_2_, ...), custom_call_target="tpu_custom_call" | custom-call | flops 6442450944 | bytes 10485760 | tf_op jit(solution)/shard_map/attention/pallas_call | solution.py:458
  537.5 21.6 %backward_streams.7 = (bf16[256,2048]{1,0:T(8,128)(2,1)}, bf16[256,2048]{1,0:T(8,128)(2,1)}, bf16[256,2048]{1,0:T(8,128)(2,1)}, bf16[256,2048]{1,0:T(8,128)(2,1)...) custom-call(s32[1]{0:T(128)} %bitcast.refs_0_, ...), custom_call_target="tpu_custom_call" | custom-call | flops 83886080 | bytes 20971520 | tf_op jit(solution)/shard_map/backward_streams/pallas_call | solution.py:284
  559.1 21.3 %backward_streams.6 = (bf16[256,2048]{1,0:T(8,128)(2,1)}, bf16[256,2048]{1,0:T(8,128)(2,1)}, bf16[256,2048]{1,0:T(8,128)(2,1)}, bf16[256,2048]{1,0:T(8,128)(2,1)...) custom-call(s32[1]{0:T(128)} %bitcast.refs_0_, ...), custom_call_target="tpu_custom_call" | custom-call | flops 83886080 | bytes 20971520 | tf_op jit(solution)/shard_map/backward_streams/pallas_call | solution.py:284
  580.4 21.4 %backward_streams.5 = (bf16[256,2048]{1,0:T(8,128)(2,1)}, bf16[256,2048]{1,0:T(8,128)(2,1)}, bf16[256,2048]{1,0:T(8,128)(2,1)}, bf16[256,2048]{1,0:T(8,128)(2,1)...) custom-call(s32[1]{0:T(128)} %bitcast.refs_0_, ...), custom_call_target="tpu_custom_call" | custom-call | flops 83886080 | bytes 20971520 | tf_op jit(solution)/shard_map/backward_streams/pallas_call | solution.py:284
  601.9 21.4 %backward_streams.4 = (bf16[256,2048]{1,0:T(8,128)(2,1)}, bf16[256,2048]{1,0:T(8,128)(2,1)}, bf16[256,2048]{1,0:T(8,128)(2,1)}, bf16[256,2048]{1,0:T(8,128)(2,1)...) custom-call(s32[1]{0:T(128)} %bitcast.refs_0_, bf16[256,2048]{1,0:T(8,128)(2,1)} %copy-done, ...), custom_call_target="tpu_custom_call" | custom-call | flops 83886080 | bytes 20971520 | tf_op jit(solution)/shard_map/backward_streams/pallas_call | solution.py:284
  639.6 7.4 fusion.10
  655.9 18.7 %collective-permute-done.61 = bf16[256,2048]{1,0:T(8,128)(2,1)S(1)} collective-permute-done((bf16[256,2048]{1,0:T(8,128)(2,1)S(1)}, bf16[256,2048]{1,0:T(8,128)(2,1)S(1)}, u32[]{:S(2)}, u32[]{:S(2)}) %collective-permute-start.61) | collective-permute-done | bytes 1048608 | tf_op jit(solution)/shard_map/ppermute | solution.py:60
  675.7 22.1 %collective-permute-done.58 = bf16[256,2048]{1,0:T(8,128)(2,1)S(1)} collective-permute-done((bf16[256,2048]{1,0:T(8,128)(2,1)S(1)}, bf16[256,2048]{1,0:T(8,128)(2,1)S(1)}, u32[]{:S(2)}, u32[]{:S(2)}) %collective-permute-start.58) | collective-permute-done | bytes 1048608 | tf_op jit(solution)/shard_map/ppermute | solution.py:60
  698.9 10.9 collective-permute-done.64
  711.2 21.1 %collective-permute-done.67 = bf16[256,2048]{1,0:T(8,128)(2,1)S(1)} collective-permute-done((bf16[256,2048]{1,0:T(8,128)(2,1)S(1)}, bf16[256,2048]{1,0:T(8,128)(2,1)S(1)}, u32[]{:S(2)}, u32[]{:S(2)}) %collective-permute-start.67) | collective-permute-done | bytes 1048608 | tf_op jit(solution)/shard_map/ppermute | solution.py:60
  733.0 14.5 %collective-permute-done.49 = bf16[256,2048]{1,0:T(8,128)(2,1)S(1)} collective-permute-done((bf16[256,2048]{1,0:T(8,128)(2,1)S(1)}, bf16[256,2048]{1,0:T(8,128)(2,1)S(1)}, u32[]{:S(2)}, u32[]{:S(2)}) %collective-permute-start.49) | collective-permute-done | bytes 1048608 | tf_op jit(solution)/shard_map/ppermute | solution.py:60
  752.7 21.8 %collective-permute-done.59 = bf16[256,2048]{1,0:T(8,128)(2,1)S(1)} collective-permute-done((bf16[256,2048]{1,0:T(8,128)(2,1)S(1)}, bf16[256,2048]{1,0:T(8,128)(2,1)S(1)}, u32[]{:S(2)}, u32[]{:S(2)}) %collective-permute-start.59) | collective-permute-done | bytes 1048608 | tf_op jit(solution)/shard_map/ppermute | solution.py:60
  777.2 19.7 %collective-permute-done.65 = bf16[256,2048]{1,0:T(8,128)(2,1)S(1)} collective-permute-done((bf16[256,2048]{1,0:T(8,128)(2,1)S(1)}, bf16[256,2048]{1,0:T(8,128)(2,1)S(1)}, u32[]{:S(2)}, u32[]{:S(2)}) %collective-permute-start.65) | collective-permute-done | bytes 1048608 | tf_op jit(solution)/shard_map/ppermute | solution.py:60
  798.5 17.1 %collective-permute-done.48 = bf16[256,2048]{1,0:T(8,128)(2,1)S(1)} collective-permute-done((bf16[256,2048]{1,0:T(8,128)(2,1)S(1)}, bf16[256,2048]{1,0:T(8,128)(2,1)S(1)}, u32[]{:S(2)}, u32[]{:S(2)}) %collective-permute-start.48) | collective-permute-done | bytes 1048608 | tf_op jit(solution)/shard_map/ppermute | solution.py:60
  844.5 77.3 %reduce-scatter.8.cloned.1.call-done = bf16[512,1024]{1,0:T(8,128)(2,1)} async-done(((bf16[2048,1024]{1,0:T(8,128)(2,1)}), bf16[512,1024]{1,0:T(8,128)(2,1)}) %reduce-scatter.8.cloned.1.call-update) | async-done | bytes 1048592 | tf_op jit(solution)/shard_map/reduce_scatter | solution.py:700
  931.4 255.3 %interleave.1 = bf16[4,2,256,2048]{3,2,1,0:T(8,128)(2,1)} custom-call(s32[1]{0:T(128)} %bitcast.49.refs_0_.which, bf16[256,2048]{1,0:T(8,128)(2,1)} %copy-done.44, bf16[256,2048]{1,0:T(8,128)(2,1)} %copy-done.43, bf16[256,2048]{1,0:T(8,128)(2,1)} %add_convert_fusion.5.refs_2_, bf16[256,2048]{1,0:T(8,128)(2,1)} %add_convert_fusion.2.refs_3_, ...), custom_call_target="tpu_custom_call" | custom-call | tf_op jit(solution)/shard_map/interleave/pallas_call | solution.py:496
  (567 shorter events, 365.3 us)
Async XLA Ops:
  7.2 298.7 %all-gather.6.cloned.1.call-start = ((), (), s32[]{:S(2)}) async-start(), calls=%async_computation.4 | async-start | bytes 5242880 | tf_op jit(solution)/shard_map/all_gather | solution.py:583
  26.0 305.8 %all-gather.4.cloned.1.call-start = ((), (), s32[]{:S(2)}) async-start(), calls=%async_computation.3 | async-start | bytes 5242880 | tf_op jit(solution)/shard_map/all_gather | solution.py:592
  33.7 52.1 %collective-permute-start.5 = (bf16[4,128]{1,0:T(4,128)(2,1)S(1)}, bf16[4,128]{1,0:T(4,128)(2,1)S(1)}, u32[]{:S(2)}, u32[]{:S(2)}) collective-permute-start(bf16[4,128]{1,0:T(4,128)(2,1)S(1)} %copy-done.83), channel_id=1, source_target_pairs={{0,4},{1,3},{2,6},{3,1},{4,0},{5,7},{6,2},{7,5},{8,12},{9,11},{10,... | collective-permute-start | bytes 3080 | tf_op jit(solution)/shard_map/ppermute | solution.py:60
  35.2 49.2 %collective-permute-start.4 = (bf16[4,128]{1,0:T(4,128)(2,1)S(1)}, bf16[4,128]{1,0:T(4,128)(2,1)S(1)}, u32[]{:S(2)}, u32[]{:S(2)}) collective-permute-start(bf16[4,128]{1,0:T(4,128)(2,1)S(1)} %copy-done.83), channel_id=1, source_target_pairs={{0,2},{1,5},{2,0},{3,7},{4,6},{5,1},{6,4},{7,3},{8,10},{9,13},{10,... | collective-permute-start | bytes 3080 | tf_op jit(solution)/shard_map/ppermute | solution.py:60
  61.3 334.6 %all-gather.8.cloned.1.call-start = ((), (), s32[]{:S(2)}) async-start(), calls=%async_computation.5 | async-start | bytes 5242880 | tf_op jit(solution)/shard_map/all_gather | solution.py:597
  102.3 70.4 %collective-permute-start.11 = (bf16[256,2048]{1,0:T(8,128)(2,1)S(1)}, bf16[256,2048]{1,0:T(8,128)(2,1)}, u32[]{:S(2)}, u32[]{:S(2)}) collective-permute-start(bf16[256,2048]{1,0:T(8,128)(2,1)S(1)} %dynamic-slice_bitcast_fusion.2.refs_1_), channel_id=1, source_target_pairs={{0,4},{1,3},{2,6},{3,1},{4,0},{5,7},{6,2},{7,5},{8,12},{9,11},{10,... | collective-permute-start | bytes 3145736 | tf_op jit(solution)/shard_map/ppermute | solution.py:60
  126.4 61.3 %collective-permute-start.12 = (bf16[256,2048]{1,0:T(8,128)(2,1)}, bf16[256,2048]{1,0:T(8,128)(2,1)}, u32[]{:S(2)}, u32[]{:S(2)}) collective-permute-start(bf16[256,2048]{1,0:T(8,128)(2,1)} %collective-permute-done.10.refs_2_), channel_id=1, source_target_pairs={{0,4},{1,3},{2,6},{3,1},{4,0},{5,7},{6,2},{7,5},{8,12},{9,11},{10,... | collective-permute-start | bytes 3145736 | tf_op jit(solution)/shard_map/ppermute | solution.py:60
  172.7 656.8 %all-reduce.9.cloned.1.call-start = ((), (), s32[]{:S(2)}) async-start(), calls=%async_computation.6 | async-start | bytes 4194304 | tf_op jit(solution)/shard_map/psum | solution.py:725
  172.7 79.0 %collective-permute-start.19 = (bf16[256,2048]{1,0:T(8,128)(2,1)}, bf16[256,2048]{1,0:T(8,128)(2,1)}, u32[]{:S(2)}, u32[]{:S(2)}) collective-permute-start(bf16[256,2048]{1,0:T(8,128)(2,1)} %get-tuple-element.104.refs_13_), channel_id=1, source_target_pairs={{0,1},{1,0},{2,3},{3,2},{4,5},{5,4},{6,7},{7,6},{8,9},{9,8},{10,11... | collective-permute-start | bytes 3145736 | tf_op jit(solution)/shard_map/ppermute | solution.py:106
  187.7 72.0 %collective-permute-start.23 = (bf16[256,2048]{1,0:T(8,128)(2,1)}, bf16[256,2048]{1,0:T(8,128)(2,1)}, u32[]{:S(2)}, u32[]{:S(2)}) collective-permute-start(bf16[256,2048]{1,0:T(8,128)(2,1)} %get-tuple-element.108.refs_14_), channel_id=1, source_target_pairs={{0,1},{1,0},{2,3},{3,2},{4,5},{5,4},{6,7},{7,6},{8,9},{9,8},{10,11... | collective-permute-start | bytes 3145736 | tf_op jit(solution)/shard_map/ppermute | solution.py:106
  395.4 142.1 %collective-permute-start.56 = (bf16[1024,2048]{1,0:T(8,128)(2,1)}, bf16[1024,2048]{1,0:T(8,128)(2,1)}, u32[]{:S(2)}, u32[]{:S(2)}) collective-permute-start(bf16[1024,2048]{1,0:T(8,128)(2,1)} %convolution_convert_fusion.6), channel_id=1, source_target_pairs={{0,1},{1,0},{2,3},{3,2},{4,5},{5,4},{6,7},{7,6},{8,9},{9,8},{10,11... | collective-permute-start | bytes 12582920 | tf_op jit(solution)/shard_map/ppermute | solution.py:106
  630.3 212.0 %reduce-scatter.6.cloned.1.call-start = ((), (), s32[]{:S(2)}) async-start(), calls=%async_computation.8 | async-start | bytes 5242880 | tf_op jit(solution)/shard_map/reduce_scatter | solution.py:700
  630.9 290.9 %reduce-scatter.8.cloned.1.call-start = ((), (), s32[]{:S(2)}) async-start(), calls=%async_computation.9 | async-start | bytes 5242880 | tf_op jit(solution)/shard_map/reduce_scatter | solution.py:700
  631.4 555.6 %reduce-scatter.4.cloned.1.call-start = ((), (), s32[]{:S(2)}) async-start(), calls=%async_computation.7 | async-start | bytes 5242880 | tf_op jit(solution)/shard_map/reduce_scatter | solution.py:700
  647.0 102.1 %collective-permute-start.60 = (bf16[256,2048]{1,0:T(8,128)(2,1)S(1)}, bf16[256,2048]{1,0:T(8,128)(2,1)S(1)}, u32[]{:S(2)}, u32[]{:S(2)}) collective-permute-start(bf16[256,2048]{1,0:T(8,128)(2,1)S(1)} %copy-done.93), channel_id=1, source_target_pairs={{0,4},{1,3},{2,6},{3,1},{4,0},{5,7},{6,2},{7,5},{8,12},{9,11},{10,... | collective-permute-start | bytes 3145736 | tf_op jit(solution)/shard_map/ppermute | solution.py:60
  649.1 102.4 %collective-permute-start.57 = (bf16[256,2048]{1,0:T(8,128)(2,1)S(1)}, bf16[256,2048]{1,0:T(8,128)(2,1)S(1)}, u32[]{:S(2)}, u32[]{:S(2)}) collective-permute-start(bf16[256,2048]{1,0:T(8,128)(2,1)S(1)} %copy-done.92), channel_id=1, source_target_pairs={{0,4},{1,3},{2,6},{3,1},{4,0},{5,7},{6,2},{7,5},{8,12},{9,11},{10,... | collective-permute-start | bytes 3145736 | tf_op jit(solution)/shard_map/ppermute | solution.py:60
  649.7 48.1 %collective-permute-start.58 = (bf16[256,2048]{1,0:T(8,128)(2,1)S(1)}, bf16[256,2048]{1,0:T(8,128)(2,1)S(1)}, u32[]{:S(2)}, u32[]{:S(2)}) collective-permute-start(bf16[256,2048]{1,0:T(8,128)(2,1)S(1)} %copy-done.96), channel_id=1, source_target_pairs={{0,4},{1,3},{2,6},{3,1},{4,0},{5,7},{6,2},{7,5},{8,12},{9,11},{10,... | collective-permute-start | bytes 3145736 | tf_op jit(solution)/shard_map/ppermute | solution.py:60
  651.1 58.7 %collective-permute-start.64 = (bf16[256,2048]{1,0:T(8,128)(2,1)S(1)}, bf16[256,2048]{1,0:T(8,128)(2,1)S(1)}, u32[]{:S(2)}, u32[]{:S(2)}) collective-permute-start(bf16[256,2048]{1,0:T(8,128)(2,1)S(1)} %copy-done.94), channel_id=1, source_target_pairs={{0,4},{1,3},{2,6},{3,1},{4,0},{5,7},{6,2},{7,5},{8,12},{9,11},{10,... | collective-permute-start | bytes 3145736 | tf_op jit(solution)/shard_map/ppermute | solution.py:60
  674.7 57.6 %collective-permute-start.67 = (bf16[256,2048]{1,0:T(8,128)(2,1)S(1)}, bf16[256,2048]{1,0:T(8,128)(2,1)S(1)}, u32[]{:S(2)}, u32[]{:S(2)}) collective-permute-start(bf16[256,2048]{1,0:T(8,128)(2,1)S(1)} %copy-done.91), channel_id=1, source_target_pairs={{0,4},{1,3},{2,6},{3,1},{4,0},{5,7},{6,2},{7,5},{8,12},{9,11},{10,... | collective-permute-start | bytes 3145736 | tf_op jit(solution)/shard_map/ppermute | solution.py:60
  697.8 49.7 %collective-permute-start.49 = (bf16[256,2048]{1,0:T(8,128)(2,1)S(1)}, bf16[256,2048]{1,0:T(8,128)(2,1)S(1)}, u32[]{:S(2)}, u32[]{:S(2)}) collective-permute-start(bf16[256,2048]{1,0:T(8,128)(2,1)S(1)} %get-tuple-element.264), channel_id=1, source_target_pairs={{0,4},{1,3},{2,6},{3,1},{4,0},{5,7},{6,2},{7,5},{8,12},{9,11},{10,... | collective-permute-start | bytes 3145736 | tf_op jit(solution)/shard_map/ppermute | solution.py:60
  749.1 73.4 %collective-permute-start.66 = (bf16[256,2048]{1,0:T(8,128)(2,1)S(1)}, bf16[256,2048]{1,0:T(8,128)(2,1)S(1)}, u32[]{:S(2)}, u32[]{:S(2)}) collective-permute-start(bf16[256,2048]{1,0:T(8,128)(2,1)S(1)} %copy-done.89), channel_id=1, source_target_pairs={{0,4},{1,3},{2,6},{3,1},{4,0},{5,7},{6,2},{7,5},{8,12},{9,11},{10,... | collective-permute-start | bytes 3145736 | tf_op jit(solution)/shard_map/ppermute | solution.py:60
  751.4 64.1 %collective-permute-start.48 = (bf16[256,2048]{1,0:T(8,128)(2,1)S(1)}, bf16[256,2048]{1,0:T(8,128)(2,1)S(1)}, u32[]{:S(2)}, u32[]{:S(2)}) collective-permute-start(bf16[256,2048]{1,0:T(8,128)(2,1)S(1)} %get-tuple-element.263), channel_id=1, source_target_pairs={{0,4},{1,3},{2,6},{3,1},{4,0},{5,7},{6,2},{7,5},{8,12},{9,11},{10,... | collective-permute-start | bytes 3145736 | tf_op jit(solution)/shard_map/ppermute | solution.py:60
  775.9 50.4 %collective-permute-start.68 = (bf16[256,2048]{1,0:T(8,128)(2,1)S(1)}, bf16[256,2048]{1,0:T(8,128)(2,1)S(1)}, u32[]{:S(2)}, u32[]{:S(2)}) collective-permute-start(bf16[256,2048]{1,0:T(8,128)(2,1)S(1)} %add_convert_fusion.3), channel_id=1, source_target_pairs={{0,2},{1,5},{2,0},{3,7},{4,6},{5,1},{6,4},{7,3},{8,10},{9,13},{10,... | collective-permute-start | bytes 3145736 | tf_op jit(solution)/shard_map/ppermute | solution.py:60
  797.0 126.9 %collective-permute-start.70 = (bf16[256,2048]{1,0:T(8,128)(2,1)S(1)}, bf16[256,2048]{1,0:T(8,128)(2,1)}, u32[]{:S(2)}, u32[]{:S(2)}) collective-permute-start(bf16[256,2048]{1,0:T(8,128)(2,1)S(1)} %add_convert_fusion.8.refs_1_), channel_id=1, source_target_pairs={{0,1},{1,0},{2,3},{3,2},{4,5},{5,4},{6,7},{7,6},{8,9},{9,8},{10,11... | collective-permute-start | bytes 3145736 | tf_op jit(solution)/shard_map/ppermute | solution.py:106
  815.5 110.7 %collective-permute-start.69 = (bf16[256,2048]{1,0:T(8,128)(2,1)S(1)}, bf16[256,2048]{1,0:T(8,128)(2,1)}, u32[]{:S(2)}, u32[]{:S(2)}) collective-permute-start(bf16[256,2048]{1,0:T(8,128)(2,1)S(1)} %add_convert_fusion.11.refs_0_), channel_id=1, source_target_pairs={{0,1},{1,0},{2,3},{3,2},{4,5},{5,4},{6,7},{7,6},{8,9},{9,8},{10,11... | collective-permute-start | bytes 3145736 | tf_op jit(solution)/shard_map/ppermute | solution.py:106
  815.5 111.3 %collective-permute-start.71 = (bf16[256,2048]{1,0:T(8,128)(2,1)}, bf16[256,2048]{1,0:T(8,128)(2,1)}, u32[]{:S(2)}, u32[]{:S(2)}) collective-permute-start(bf16[256,2048]{1,0:T(8,128)(2,1)} %add_convert_fusion.5.refs_2_), channel_id=1, source_target_pairs={{0,1},{1,0},{2,3},{3,2},{4,5},{5,4},{6,7},{7,6},{8,9},{9,8},{10,11... | collective-permute-start | bytes 3145736 | tf_op jit(solution)/shard_map/ppermute | solution.py:106
  822.5 104.8 %collective-permute-start.51 = (bf16[256,2048]{1,0:T(8,128)(2,1)S(1)}, bf16[256,2048]{1,0:T(8,128)(2,1)}, u32[]{:S(2)}, u32[]{:S(2)}) collective-permute-start(bf16[256,2048]{1,0:T(8,128)(2,1)S(1)} %fusion.14), channel_id=1, source_target_pairs={{0,1},{1,0},{2,3},{3,2},{4,5},{5,4},{6,7},{7,6},{8,9},{9,8},{10,11... | collective-permute-start | bytes 3145736 | tf_op jit(solution)/shard_map/ppermute | solution.py:106
  827.8 103.6 %collective-permute-start.72 = (bf16[256,2048]{1,0:T(8,128)(2,1)}, bf16[256,2048]{1,0:T(8,128)(2,1)}, u32[]{:S(2)}, u32[]{:S(2)}) collective-permute-start(bf16[256,2048]{1,0:T(8,128)(2,1)} %add_convert_fusion.2.refs_3_), channel_id=1, source_target_pairs={{0,1},{1,0},{2,3},{3,2},{4,5},{5,4},{6,7},{7,6},{8,9},{9,8},{10,11... | collective-permute-start | bytes 3145736 | tf_op jit(solution)/shard_map/ppermute | solution.py:106
  923.9 265.2 %collective-permute-start.78 = (bf16[128,1024]{1,0:T(8,128)(2,1)}, bf16[128,1024]{1,0:T(8,128)(2,1)}, u32[]{:S(2)}, u32[]{:S(2)}) collective-permute-start(bf16[128,1024]{1,0:T(8,128)(2,1)} %get-tuple-element.271), channel_id=1, source_target_pairs={{0,6},{2,4},{4,2},{6,0},{1,7},{3,5},{5,3},{7,1},{8,14},{10,12},{12... | collective-permute-start | bytes 786440 | tf_op jit(solution)/shard_map/ppermute | solution.py:95
  926.2 263.3 %collective-permute-start.77 = (bf16[128,1024]{1,0:T(8,128)(2,1)}, bf16[128,1024]{1,0:T(8,128)(2,1)}, u32[]{:S(2)}, u32[]{:S(2)}) collective-permute-start(bf16[128,1024]{1,0:T(8,128)(2,1)} %get-tuple-element.272), channel_id=1, source_target_pairs={{0,4},{2,6},{4,0},{6,2},{1,5},{3,7},{5,1},{7,3},{8,12},{10,14},{12... | collective-permute-start | bytes 786440 | tf_op jit(solution)/shard_map/ppermute | solution.py:95
  926.8 265.4 %collective-permute-start.76 = (bf16[128,1024]{1,0:T(8,128)(2,1)}, bf16[128,1024]{1,0:T(8,128)(2,1)}, u32[]{:S(2)}, u32[]{:S(2)}) collective-permute-start(bf16[128,1024]{1,0:T(8,128)(2,1)} %get-tuple-element.273), channel_id=1, source_target_pairs={{0,2},{2,0},{4,6},{6,4},{1,3},{3,1},{5,7},{7,5},{8,10},{10,8},{12,... | collective-permute-start | bytes 786440 | tf_op jit(solution)/shard_map/ppermute | solution.py:95
  927.4 265.2 %collective-permute-start.81 = (bf16[128,1024]{1,0:T(8,128)(2,1)}, bf16[128,1024]{1,0:T(8,128)(2,1)}, u32[]{:S(2)}, u32[]{:S(2)}) collective-permute-start(bf16[128,1024]{1,0:T(8,128)(2,1)} %get-tuple-element.267), channel_id=1, source_target_pairs={{0,6},{2,4},{4,2},{6,0},{1,7},{3,5},{5,3},{7,1},{8,14},{10,12},{12... | collective-permute-start | bytes 786440 | tf_op jit(solution)/shard_map/ppermute | solution.py:95
  (164 other events, 3472.5 us)
Sparse Core Ops, SparseCore 0:
  26.2 82.4 all-gather.5
  110.2 79.2 all-gather.3
  191.6 79.2 all-gather.7
  630.4 133.9 all-reduce.8
  766.6 75.7 reduce-scatter.5
  844.5 77.2 reduce-scatter.7
  924.2 77.2 reduce-scatter.3

commit v2 on v1

--- a/solution.py
+++ b/solution.py
@@ -69,7 +69,7 @@
         for i in reversed(range(self.bits)):
             got = [self.step(x, i) for x in held[1 << i :]]
             held = [
-                (x.astype(jnp.float32) + y.astype(jnp.float32)).astype(jnp.bfloat16)
+                (x.astype(jnp.float32) + y.astype(jnp.float32)).astype(x.dtype)
                 for x, y in zip(held[: 1 << i], got)
             ]
         return held[0]
@@ -478,29 +478,24 @@
     )(which, query, keys, values, grad, *rope_tables(positions))
 
 
-def interleave(own, sibling, m):
-    count = len(own)
-    half, width = own[0].shape
-
-    def kernel(which, *refs):
-        out, sems = refs[2 * count], refs[2 * count + 1]
-        copies = []
-        for a in range(count):
-            copies.append(pltpu.make_async_copy(refs[a], out.at[a, which[0]], sems.at[a]))
-            copies.append(pltpu.make_async_copy(refs[count + a], out.at[a, 1 - which[0]], sems.at[count + a]))
-        for copy in copies:
-            copy.start()
-        for copy in copies:
-            copy.wait()
-
-    return pl.pallas_call(
-        kernel,
-        in_specs=[pl.BlockSpec(memory_space=pltpu.SMEM)] + [pl.BlockSpec(memory_space=pl.ANY)] * (2 * count),
-        out_specs=pl.BlockSpec(memory_space=pl.ANY),
-        out_shape=jax.ShapeDtypeStruct((count, 2, half, width), own[0].dtype),
-        scratch_shapes=[pltpu.SemaphoreType.DMA((2 * count,))],
-        name="interleave",
-    )(m, *own, *sibling)
+def total(value, plane):
+    z, zs = lax.axis_index("dp"), lax.axis_size("dp")
+    rows = value.shape[0]
+    side = rows // plane.cores
+    block = side // plane.size
+    part = block // zs
+    cut = lambda x, at, size: lax.dynamic_slice_in_dim(x, at * size, size, 0)
+    value = cut(value, plane.m, side) + plane.swap(cut(value, 1 - plane.m, side))
+    value = plane.scatter([cut(value, plane.h ^ plane.place(j), block) for j in range(plane.size)])
+    ring = lambda x, k: lax.ppermute(x, "dp", [(i, (i + k) % zs) for i in range(zs)])
+    mine = cut(value, z, part)
+    for k in range(1, zs):
+        mine = mine + ring(cut(value, (z + k) % zs, part), k)
+    out = lax.dynamic_update_slice_in_dim(jnp.zeros((block,) + value.shape[1:], value.dtype), mine, z * part, 0)
+    for k in range(1, zs):
+        out = lax.dynamic_update_slice_in_dim(out, ring(mine, k), (z + zs - k) % zs * part, 0)
+    out = plane.ordered(plane.gather(out))
+    return plane.both(out, plane.swap(out), 0).reshape((rows,) + value.shape[1:])
 
 
 def place_wide(entries, h, out_type, pieces, turned):
@@ -585,8 +580,7 @@
     marks = []
     for a in range(count):
         found = plane.gather(after(own_rows[a], waited))
-        waited = found[1]
-        marks.append(waited)
+        marks.append(found[1])
         slots.append(found)
     down_parts = plane.trade(after(down_weight, marks[0]).T)
     down_full = lax.all_gather(plane.stacked(down_parts), "dp", axis=0, tiled=True)
@@ -704,8 +698,9 @@
     (down_grad,) = spread(down_part, (True,))
     query_grad, key_grad, value_grad, out_grad = spread(narrow_part, (False, False, False, True))
 
-    scale_wide = after(jnp.broadcast_to(own_scale[:, None], (half, LANES)), narrow_part)
-    finals, sums = [], None
+    scale_wide = after(jnp.broadcast_to(own_scale[:, None], (half, LANES)), narrow_part, branch_sum)
+    sums = None
+    history_grad = jnp.zeros((group_rows, width), bf16)
     for a in range(count):
         scale = jnp.where(h == a, scale_wide, 0.0)
         found = backward_streams(
@@ -713,8 +708,10 @@
         )
         held, rest = list(found[:count]), found[count:]
         sums = rest if sums is None else tuple(x + y for x, y in zip(sums, rest))
-        finals.append(plane.scatter(held))
-    history_grad = interleave(finals, [plane.swap(x) for x in finals], which_m).reshape(history.shape)
+        final = plane.scatter(held)
+        history_grad = lax.dynamic_update_slice_in_dim(history_grad, final, a * rows + m * half, 0)
+        history_grad = lax.dynamic_update_slice_in_dim(history_grad, plane.swap(final), a * rows + (1 - m) * half, 0)
+    history_grad = history_grad.reshape(history.shape)
 
     gain_sum, in_sum, out_sum, bias_sum = sums
     out_sum = from_slots(out_sum[:, :pairs].reshape(LANES, STREAMS, count)).reshape(LANES, pairs)
@@ -722,7 +719,7 @@
     small = jnp.concatenate(
         [in_sum, gain_sum.T, jnp.pad(jnp.concatenate([out_sum, bias_sum], 0), ((0, width - LANES - 1), (0, 0)))], 1
     )
-    small = lax.psum(small, ("dp", "hist", "mp"))
+    small = total(small, plane)
     mixer_in_grad = small[:, :hidden_units]
     gain_all = small[:, LANES : LANES + STREAMS].T
     place = (lax.axis_index("dp") * count + h) * norm_gain.shape[1]

time: 1220 us -> 877 us (0.72)
  Pallas kernels: 455 us -> 200 us
  waiting for transfers between devices: 339 us -> 191 us
  local copies, waits for them, and re-layouts: 108 us -> 138 us
  starting transfers between devices: 88.1 us -> 115 us
  matrix products: 176 us -> 157 us
  other arithmetic: 34.7 us -> 51.3 us
    pallas_call x1 -> x0, Pallas kernels: 255 us -> none  [interleave(): pl.pallas_call(kernel, in_specs=[pl.BlockSpec(memory_space=pltpu.SMEM)] +...]
    reduce_scatter x3, waiting for transfers between devices: 80.4 us -> 0.04 us  [spread(): summed = lax.psum_scatter(part, 'dp', scatter_dimension=0, tiled=True)]
    ppermute x33 -> x39, waiting for transfers between devices: 214 us -> 135 us  [step(): return lax.ppermute(value, PLANE, pairs)]
    dot_general x24, matrix products: 176 us -> 157 us  [dot(): lax.dot_general(left, right, (((contract[0],), (contract[1],)), ((), ()))...]
    ppermute x9, waiting for transfers between devices: 27.7 us -> 43.7 us  [trade(): lax.ppermute(block(r), 'hist', [(h, h ^ r) for h in range(self.size)])]
    ppermute x33 -> x39, starting transfers between devices: 36.6 us -> 50.8 us  [step(): return lax.ppermute(value, PLANE, pairs)]
    unnamed x246 -> x208, local copies, waits for them, and re-layouts: 57.4 us -> 62.8 us
    ppermute x28 -> x30, starting transfers between devices: 24.6 us -> 22.9 us  [swap(): return lax.ppermute(value, 'mp', [(m, m ^ 1) for m in range(self.cores)])]
  transfers between devices with their start and end apart: 89 -> 102, of which waited for: 30 -> 29; matrix products, arithmetic and copies ran while one was open for 25% -> 38% of each run, Pallas kernels for 30% -> 23%
where the time goes in v2:
time: 877 us; the launch traced here: 869 us
  Pallas kernels  200 us (23%)
  waiting for transfers between devices  191 us (22%)
  matrix products  157 us (18%)
  local copies, waits for them, and re-layouts  138 us (16%)
  starting transfers between devices  115 us (13%)
  other arithmetic  51.3 us (6%)
  between operations  16.6 us (2%)
    dot_general x24, matrix products, dot(): lax.dot_general(left, right, (((contract[0],), (contract[1],)), ((), ()))...  157 us
    ppermute x39, waiting for transfers between devices, step(): return lax.ppermute(value, PLANE, pairs)  135 us
    pallas_call x4, Pallas kernels, backward_streams(): pl.pallas_call(lambda *refs: backward_kernel(count, *refs), grid=(steps,)...  85.6 us
    unnamed x208, local copies, waits for them, and re-layouts  62.8 us
    pallas_call x1, Pallas kernels, attention(): pl.pallas_call(lambda *refs: attention_kernel(count, half, heads, *refs),...  60.6 us
    ppermute x39, starting transfers between devices, step(): return lax.ppermute(value, PLANE, pairs)  50.8 us
    pallas_call x4, Pallas kernels, forward_streams(): pl.pallas_call(lambda *refs: forward_kernel(count, *refs), grid=(rows //...  44.2 us
    ppermute x9, waiting for transfers between devices, trade(): lax.ppermute(block(r), 'hist', [(h, h ^ r) for h in range(self.size)])  43.7 us
  transfers between devices with their start and end apart: 102, of which 29 were waited for; matrix products, arithmetic and copies ran while one was open for 38% of the time, Pallas kernels for 23%

profile of v2, /device:TPU:0, one launch (start us, length us, event | category | flops | bytes accessed | tf_op | source)
XLA Modules:
  0.0 868.7 jit_solution(1116111277978296675)
XLA Ops:
  35.7 11.3 %collective-permute-done.1.refs_2_ = bf16[256,2048]{1,0:T(8,128)(2,1)} collective-permute-done((bf16[256,2048]{1,0:T(8,128)(2,1)S(1)}, bf16[256,2048]{1,0:T(8,128)(2,1)}, u32[]{:S(2)}, u32[]{:S(2)}) %collective-permute-start.1) | collective-permute-done | bytes 1048608 | tf_op jit(solution)/shard_map/ppermute | solution.py:60
  99.3 13.0 %collective-permute-done.10.refs_2_ = bf16[256,2048]{1,0:T(8,128)(2,1)} collective-permute-done((bf16[256,2048]{1,0:T(8,128)(2,1)S(1)}, bf16[256,2048]{1,0:T(8,128)(2,1)}, u32[]{:S(2)}, u32[]{:S(2)}) %collective-permute-start.10) | collective-permute-done | bytes 1048608 | tf_op jit(solution)/shard_map/ppermute | solution.py:60
  123.1 11.7 %collective-permute-done.16.refs_2_ = bf16[256,2048]{1,0:T(8,128)(2,1)S(1)} collective-permute-done((bf16[256,2048]{1,0:T(8,128)(2,1)S(1)}, bf16[256,2048]{1,0:T(8,128)(2,1)S(1)}, u32[]{:S(2)}, u32[]{:S(2)}) %collective-permute-start.16) | collective-permute-done | bytes 1048608 | tf_op jit(solution)/shard_map/ppermute | solution.py:60
  154.6 14.5 %collective-permute-done.46 = bf16[128,1024]{0,1:T(8,128)(2,1)S(1)} collective-permute-done((bf16[128,1024]{0,1:T(8,128)(2,1)S(1)}, bf16[128,1024]{0,1:T(8,128)(2,1)S(1)}, u32[]{:S(2)}, u32[]{:S(2)}) %collective-permute-start.46) | collective-permute-done | bytes 262176 | tf_op jit(solution)/shard_map/ppermute | solution.py:88
  175.6 11.1 %forward_streams.4 = (bf16[256,2048]{1,0:T(8,128)(2,1)}, bf16[256,2048]{1,0:T(8,128)(2,1)}, bf16[256,2048]{1,0:T(8,128)(2,1)}, bf16[256,2048]{1,0:T(8,128)(2,1)}...) custom-call(s32[1]{0:T(128)} %bitcast.refs_0_, bf16[256,2048]{1,0:T(8,128)(2,1)} %copy-done.2, ...), custom_call_target="tpu_custom_call" | custom-call | flops 41943040 | bytes 8388608 | tf_op jit(solution)/shard_map/forward_streams/pallas_call | solution.py:161
  193.6 11.0 %forward_streams.5 = (bf16[256,2048]{1,0:T(8,128)(2,1)}, bf16[256,2048]{1,0:T(8,128)(2,1)}, bf16[256,2048]{1,0:T(8,128)(2,1)}, bf16[256,2048]{1,0:T(8,128)(2,1)}...) custom-call(s32[1]{0:T(128)} %bitcast.refs_0_, bf16[256,2048]{1,0:T(8,128)(2,1)} %copy-done, ...), custom_call_target="tpu_custom_call" | custom-call | flops 41943040 | bytes 8388608 | tf_op jit(solution)/shard_map/forward_streams/pallas_call | solution.py:161
  208.1 16.2 %collective-permute-start.31 = (bf16[256,2048]{1,0:T(8,128)(2,1)}, bf16[256,2048]{1,0:T(8,128)(2,1)}, u32[]{:S(2)}, u32[]{:S(2)}) collective-permute-start(bf16[256,2048]{1,0:T(8,128)(2,1)} %get-tuple-element.116.refs_16_), channel_id=1, source_target_pairs={{0,1},{1,0},{2,3},{3,2},{4,5},{5,4},{6,7},{7,6},{8,9},{9,8},{10,11... | collective-permute-start | bytes 3145736 | tf_op jit(solution)/shard_map/ppermute | solution.py:106
  224.9 11.0 %forward_streams.6 = (bf16[256,2048]{1,0:T(8,128)(2,1)}, bf16[256,2048]{1,0:T(8,128)(2,1)}, bf16[256,2048]{1,0:T(8,128)(2,1)}, bf16[256,2048]{1,0:T(8,128)(2,1)}...) custom-call(s32[1]{0:T(128)} %bitcast.refs_0_, bf16[256,2048]{1,0:T(8,128)(2,1)} %get-tuple-element.100.refs_1_, ...), custom_call_target="tpu_custom_call" | custom-call | flops 41943040 | bytes 8388608 | tf_op jit(solution)/shard_map/forward_streams/pallas_call | solution.py:161
  239.7 11.1 %forward_streams.7 = (bf16[256,2048]{1,0:T(8,128)(2,1)}, bf16[256,2048]{1,0:T(8,128)(2,1)}, bf16[256,2048]{1,0:T(8,128)(2,1)}, bf16[256,2048]{1,0:T(8,128)(2,1)}...) custom-call(s32[1]{0:T(128)} %bitcast.refs_0_, bf16[256,2048]{1,0:T(8,128)(2,1)} %copy-done.4, ...), custom_call_target="tpu_custom_call" | custom-call | flops 41943040 | bytes 8388608 | tf_op jit(solution)/shard_map/forward_streams/pallas_call | solution.py:161
  277.8 15.0 %multiply_convert_fusion = (bf16[2048,1024]{1,0:T(8,128)(2,1)S(1)}, f32[2048,1024]{1,0:T(8,128)}) fusion(bf16[2048,2048]{1,0:T(8,128)(2,1)} %constant_dynamic-update-slice_fusion.24, bf16[2048,1024]{0,1:T(8,128)(2,1)} %all-gather.6.cloned.1.call-done), kind=kOutput, calls=%fused_computation.10 | convolution fusion | flops 8600420352 | bytes 25165824 | tf_op jit(solution)/shard_map/dot_general | solution.py:23
  294.9 12.5 %convolution_convert_fusion.8 = bf16[2048,1024]{1,0:T(8,128)(2,1)} fusion(bf16[2048,1024]{1,0:T(8,128)(2,1)S(1)} %get-tuple-element.262, bf16[1024,2048]{1,0:T(8,128)(2,1)} %collective-permute-done.38, bf16[1024,2048]{1,0:T(8,128)(2,1)S(1)} %copy-done.30), kind=kOutput, calls=%fused_computation.37 | convolution fusion | flops 8608808960 | bytes 16777216 | tf_op jit(solution)/shard_map/dot_general | solution.py:23
  335.4 15.8 %fusion.5 = bf16[2048,1024]{1,0:T(8,128)(2,1)S(1)} fusion(f32[2048,1024]{1,0:T(8,128)} %get-tuple-element.263, bf16[2048,1024]{0,1:T(8,128)(2,1)} %all-gather.4.cloned.1.call-done, bf16[1024,2048]{1,0:T(8,128)(2,1)} %collective-permute-done.38, bf16[1024,2048]{1,0:T(8,128)(2,1)} %constant_dynamic-update-slice_fusion.46), kind=kOutput, calls=%fused_computation.6 | convolution fusion | flops 8627683328 | bytes 25165824 | tf_op jit(solution)/shard_map/dot_general | solution.py:23
  353.2 12.8 %convolution_convert_fusion.9 = bf16[2048,1024]{1,0:T(8,128)(2,1)} fusion(bf16[2048,2048]{1,0:T(8,128)(2,1)} %constant_dynamic-update-slice_fusion.24, bf16[2048,1024]{1,0:T(8,128)(2,1)S(1)} %fusion.5), kind=kOutput, calls=%fused_computation.38 | convolution fusion | flops 8592031744 | bytes 16777216 | tf_op jit(solution)/shard_map/dot_general | solution.py:23
  366.6 7.2 convolution_convert_fusion.14.refs_4_
  373.8 6.7 convolution_convert_fusion.15.refs_3_
  380.5 7.1 fusion.41.refs_2_
  387.7 7.1 fusion.45.refs_1_
  394.8 60.6 %attention.1 = (bf16[2048,256]{1,0:T(8,128)(2,1)}, bf16[2048,256]{1,0:T(8,128)(2,1)}, bf16[2048,256]{1,0:T(8,128)(2,1)}, bf16[2048,256]{1,0:T(8,128)(2,1)}) custom-call(s32[1]{0:T(128)} %bitcast.49.refs_0_, f32[2048,256]{1,0:T(8,128)} %fusion.45.refs_1_, f32[2048,256]{1,0:T(8,128)} %fusion.41.refs_2_, bf16[2048,256]{1,0:T(8,128)(2,1)} %convolution_convert_fusion.15.refs_3_, ...), custom_call_target="tpu_custom_call" | custom-call | flops 6442450944 | bytes 10485760 | tf_op jit(solution)/shard_map/attention/pallas_call | solution.py:458
  455.4 7.2 fusion.8
  485.7 6.3 convolution_convert_fusion.6
  512.6 7.5 fusion.10
  533.1 21.3 %backward_streams.7 = (bf16[256,2048]{1,0:T(8,128)(2,1)}, bf16[256,2048]{1,0:T(8,128)(2,1)}, bf16[256,2048]{1,0:T(8,128)(2,1)}, bf16[256,2048]{1,0:T(8,128)(2,1)...) custom-call(s32[1]{0:T(128)} %bitcast.refs_0_, ...), custom_call_target="tpu_custom_call" | custom-call | flops 83886080 | bytes 20971520 | tf_op jit(solution)/shard_map/backward_streams/pallas_call | solution.py:284
  554.4 21.3 %backward_streams.6 = (bf16[256,2048]{1,0:T(8,128)(2,1)}, bf16[256,2048]{1,0:T(8,128)(2,1)}, bf16[256,2048]{1,0:T(8,128)(2,1)}, bf16[256,2048]{1,0:T(8,128)(2,1)...) custom-call(s32[1]{0:T(128)} %bitcast.refs_0_, ...), custom_call_target="tpu_custom_call" | custom-call | flops 83886080 | bytes 20971520 | tf_op jit(solution)/shard_map/backward_streams/pallas_call | solution.py:284
  575.8 21.5 %backward_streams.5 = (bf16[256,2048]{1,0:T(8,128)(2,1)}, bf16[256,2048]{1,0:T(8,128)(2,1)}, bf16[256,2048]{1,0:T(8,128)(2,1)}, bf16[256,2048]{1,0:T(8,128)(2,1)...) custom-call(s32[1]{0:T(128)} %bitcast.refs_0_, bf16[256,2048]{1,0:T(8,128)(2,1)} %copy-done, ...), custom_call_target="tpu_custom_call" | custom-call | flops 83886080 | bytes 20971520 | tf_op jit(solution)/shard_map/backward_streams/pallas_call | solution.py:284
  597.4 21.4 %backward_streams.4 = (bf16[256,2048]{1,0:T(8,128)(2,1)}, bf16[256,2048]{1,0:T(8,128)(2,1)}, bf16[256,2048]{1,0:T(8,128)(2,1)}, bf16[256,2048]{1,0:T(8,128)(2,1)...) custom-call(s32[1]{0:T(128)} %bitcast.refs_0_, ...), custom_call_target="tpu_custom_call" | custom-call | flops 83886080 | bytes 20971520 | tf_op jit(solution)/shard_map/backward_streams/pallas_call | solution.py:284
  632.2 11.7 %collective-permute-done.75 = f32[256,148]{1,0:T(8,128)S(1)} collective-permute-done((f32[256,148]{1,0:T(8,128)S(1)}, f32[256,148]{1,0:T(8,128)S(1)}, u32[]{:S(2)}, u32[]{:S(2)}) %collective-permute-start.75) | collective-permute-done | bytes 151584 | tf_op jit(solution)/shard_map/ppermute | solution.py:60
  702.2 16.2 %collective-permute-done.84 = f32[256,148]{0,1:T(8,128)S(1)} collective-permute-done((f32[256,148]{0,1:T(8,128)S(1)}, f32[256,148]{0,1:T(8,128)S(1)}, u32[]{:S(2)}, u32[]{:S(2)}) %collective-permute-start.84) | collective-permute-done | bytes 151584 | tf_op jit(solution)/shard_map/ppermute | solution.py:60
  729.7 15.5 %collective-permute-done.66 = bf16[256,2048]{1,0:T(8,128)(2,1)S(1)} collective-permute-done((bf16[256,2048]{1,0:T(8,128)(2,1)S(1)}, bf16[256,2048]{1,0:T(8,128)(2,1)S(1)}, u32[]{:S(2)}, u32[]{:S(2)}) %collective-permute-start.66) | collective-permute-done | bytes 1048608 | tf_op jit(solution)/shard_map/ppermute | solution.py:60
  745.8 21.8 %collective-permute-done.49 = bf16[256,2048]{1,0:T(8,128)(2,1)S(1)} collective-permute-done((bf16[256,2048]{1,0:T(8,128)(2,1)S(1)}, bf16[256,2048]{1,0:T(8,128)(2,1)S(1)}, u32[]{:S(2)}, u32[]{:S(2)}) %collective-permute-start.49) | collective-permute-done | bytes 1048608 | tf_op jit(solution)/shard_map/ppermute | solution.py:60
  780.6 10.7 %collective-permute-done.67 = bf16[256,2048]{1,0:T(8,128)(2,1)S(1)} collective-permute-done((bf16[256,2048]{1,0:T(8,128)(2,1)S(1)}, bf16[256,2048]{1,0:T(8,128)(2,1)S(1)}, u32[]{:S(2)}, u32[]{:S(2)}) %collective-permute-start.67) | collective-permute-done | bytes 1048608 | tf_op jit(solution)/shard_map/ppermute | solution.py:60
  798.6 6.4 collective-permute-done.50
  805.0 8.0 fusion.14
  (581 shorter events, 399.3 us)
Async XLA Ops:
  7.2 270.6 %all-gather.6.cloned.1.call-start = ((), (), s32[]{:S(2)}) async-start(), calls=%async_computation.4 | async-start | bytes 5242880 | tf_op jit(solution)/shard_map/all_gather | solution.py:578
  26.5 308.9 %all-gather.4.cloned.1.call-start = ((), (), s32[]{:S(2)}) async-start(), calls=%async_computation.3 | async-start | bytes 5242880 | tf_op jit(solution)/shard_map/all_gather | solution.py:586
  33.0 54.1 %collective-permute-start.4 = (bf16[4,128]{1,0:T(4,128)(2,1)S(1)}, bf16[4,128]{1,0:T(4,128)(2,1)S(1)}, u32[]{:S(2)}, u32[]{:S(2)}) collective-permute-start(bf16[4,128]{1,0:T(4,128)(2,1)S(1)} %copy-done.69), channel_id=1, source_target_pairs={{0,2},{1,5},{2,0},{3,7},{4,6},{5,1},{6,4},{7,3},{8,10},{9,13},{10,... | collective-permute-start | bytes 3080 | tf_op jit(solution)/shard_map/ppermute | solution.py:60
  34.2 55.5 %collective-permute-start.5 = (bf16[4,128]{1,0:T(4,128)(2,1)S(1)}, bf16[4,128]{1,0:T(4,128)(2,1)S(1)}, u32[]{:S(2)}, u32[]{:S(2)}) collective-permute-start(bf16[4,128]{1,0:T(4,128)(2,1)S(1)} %copy-done.69), channel_id=1, source_target_pairs={{0,4},{1,3},{2,6},{3,1},{4,0},{5,7},{6,2},{7,5},{8,12},{9,11},{10,... | collective-permute-start | bytes 3080 | tf_op jit(solution)/shard_map/ppermute | solution.py:60
  60.9 305.7 %all-gather.8.cloned.1.call-start = ((), (), s32[]{:S(2)}) async-start(), calls=%async_computation.5 | async-start | bytes 5242880 | tf_op jit(solution)/shard_map/all_gather | solution.py:591
  97.0 37.8 %collective-permute-start.16 = (bf16[256,2048]{1,0:T(8,128)(2,1)S(1)}, bf16[256,2048]{1,0:T(8,128)(2,1)S(1)}, u32[]{:S(2)}, u32[]{:S(2)}) collective-permute-start(bf16[256,2048]{1,0:T(8,128)(2,1)S(1)} %get-tuple-element.102.refs_1_), channel_id=1, source_target_pairs={{0,2},{1,5},{2,0},{3,7},{4,6},{5,1},{6,4},{7,3},{8,10},{9,13},{10,... | collective-permute-start | bytes 3145736 | tf_op jit(solution)/shard_map/ppermute | solution.py:60
  118.1 71.0 %collective-permute-start.11 = (bf16[256,2048]{1,0:T(8,128)(2,1)S(1)}, bf16[256,2048]{1,0:T(8,128)(2,1)}, u32[]{:S(2)}, u32[]{:S(2)}) collective-permute-start(bf16[256,2048]{1,0:T(8,128)(2,1)S(1)} %get-tuple-element.98.refs_1_), channel_id=1, source_target_pairs={{0,4},{1,3},{2,6},{3,1},{4,0},{5,7},{6,2},{7,5},{8,12},{9,11},{10,... | collective-permute-start | bytes 3145736 | tf_op jit(solution)/shard_map/ppermute | solution.py:60
  118.2 52.8 %collective-permute-start.13 = (bf16[256,2048]{1,0:T(8,128)(2,1)}, bf16[256,2048]{1,0:T(8,128)(2,1)}, u32[]{:S(2)}, u32[]{:S(2)}) collective-permute-start(bf16[256,2048]{1,0:T(8,128)(2,1)} %get-tuple-element.100.refs_1_), channel_id=1, source_target_pairs={{0,2},{1,5},{2,0},{3,7},{4,6},{5,1},{6,4},{7,3},{8,10},{9,13},{10,... | collective-permute-start | bytes 3145736 | tf_op jit(solution)/shard_map/ppermute | solution.py:60
  134.8 54.6 %collective-permute-start.12 = (bf16[256,2048]{1,0:T(8,128)(2,1)}, bf16[256,2048]{1,0:T(8,128)(2,1)}, u32[]{:S(2)}, u32[]{:S(2)}) collective-permute-start(bf16[256,2048]{1,0:T(8,128)(2,1)} %collective-permute-done.10.refs_2_), channel_id=1, source_target_pairs={{0,4},{1,3},{2,6},{3,1},{4,0},{5,7},{6,2},{7,5},{8,12},{9,11},{10,... | collective-permute-start | bytes 3145736 | tf_op jit(solution)/shard_map/ppermute | solution.py:60
  170.4 642.7 %reduce-scatter.8.cloned.1.call-start = ((), (), s32[]{:S(2)}) async-start(), calls=%async_computation.8 | async-start | bytes 5242880 | tf_op jit(solution)/shard_map/reduce_scatter | solution.py:694
  170.9 53.3 %collective-permute-start.35 = (bf16[256,2048]{1,0:T(8,128)(2,1)}, bf16[256,2048]{1,0:T(8,128)(2,1)}, u32[]{:S(2)}, u32[]{:S(2)}) collective-permute-start(bf16[256,2048]{1,0:T(8,128)(2,1)} %get-tuple-element.120), channel_id=1, source_target_pairs={{0,2},{1,5},{2,0},{3,7},{4,6},{5,1},{6,4},{7,3},{8,10},{9,13},{10,... | collective-permute-start | bytes 3145736 | tf_op jit(solution)/shard_map/ppermute | solution.py:60
  189.1 49.1 %collective-permute-start.17 = (bf16[256,2048]{1,0:T(8,128)(2,1)S(1)}, bf16[256,2048]{1,0:T(8,128)(2,1)S(1)}, u32[]{:S(2)}, u32[]{:S(2)}) collective-permute-start(bf16[256,2048]{1,0:T(8,128)(2,1)S(1)} %get-tuple-element.102.refs_1_), channel_id=1, source_target_pairs={{0,4},{1,3},{2,6},{3,1},{4,0},{5,7},{6,2},{7,5},{8,12},{9,11},{10,... | collective-permute-start | bytes 3145736 | tf_op jit(solution)/shard_map/ppermute | solution.py:60
  189.4 49.3 %collective-permute-start.18 = (bf16[256,2048]{1,0:T(8,128)(2,1)S(1)}, bf16[256,2048]{1,0:T(8,128)(2,1)S(1)}, u32[]{:S(2)}, u32[]{:S(2)}) collective-permute-start(bf16[256,2048]{1,0:T(8,128)(2,1)S(1)} %copy-done.9), channel_id=1, source_target_pairs={{0,4},{1,3},{2,6},{3,1},{4,0},{5,7},{6,2},{7,5},{8,12},{9,11},{10,... | collective-permute-start | bytes 3145736 | tf_op jit(solution)/shard_map/ppermute | solution.py:60
  206.8 51.1 %collective-permute-start.36 = (bf16[256,2048]{1,0:T(8,128)(2,1)}, bf16[256,2048]{1,0:T(8,128)(2,1)}, u32[]{:S(2)}, u32[]{:S(2)}) collective-permute-start(bf16[256,2048]{1,0:T(8,128)(2,1)} %get-tuple-element.120), channel_id=1, source_target_pairs={{0,4},{1,3},{2,6},{3,1},{4,0},{5,7},{6,2},{7,5},{8,12},{9,11},{10,... | collective-permute-start | bytes 3145736 | tf_op jit(solution)/shard_map/ppermute | solution.py:60
  208.1 61.9 %collective-permute-start.31 = (bf16[256,2048]{1,0:T(8,128)(2,1)}, bf16[256,2048]{1,0:T(8,128)(2,1)}, u32[]{:S(2)}, u32[]{:S(2)}) collective-permute-start(bf16[256,2048]{1,0:T(8,128)(2,1)} %get-tuple-element.116.refs_16_), channel_id=1, source_target_pairs={{0,1},{1,0},{2,3},{3,2},{4,5},{5,4},{6,7},{7,6},{8,9},{9,8},{10,11... | collective-permute-start | bytes 3145736 | tf_op jit(solution)/shard_map/ppermute | solution.py:106
  270.0 44.5 %collective-permute-start.27 = (bf16[256,2048]{1,0:T(8,128)(2,1)S(1)}, bf16[256,2048]{1,0:T(8,128)(2,1)}, u32[]{:S(2)}, u32[]{:S(2)}) collective-permute-start(bf16[256,2048]{1,0:T(8,128)(2,1)S(1)} %copy-done.16), channel_id=1, source_target_pairs={{0,1},{1,0},{2,3},{3,2},{4,5},{5,4},{6,7},{7,6},{8,9},{9,8},{10,11... | collective-permute-start | bytes 3145736 | tf_op jit(solution)/shard_map/ppermute | solution.py:106
  272.6 44.5 %collective-permute-start.28 = (bf16[256,2048]{1,0:T(8,128)(2,1)}, bf16[256,2048]{1,0:T(8,128)(2,1)}, u32[]{:S(2)}, u32[]{:S(2)}) collective-permute-start(bf16[256,2048]{1,0:T(8,128)(2,1)} %get-tuple-element.113.refs_15_), channel_id=1, source_target_pairs={{0,1},{1,0},{2,3},{3,2},{4,5},{5,4},{6,7},{7,6},{8,9},{9,8},{10,11... | collective-permute-start | bytes 3145736 | tf_op jit(solution)/shard_map/ppermute | solution.py:106
  275.1 44.6 %collective-permute-start.29 = (bf16[256,2048]{1,0:T(8,128)(2,1)}, bf16[256,2048]{1,0:T(8,128)(2,1)}, u32[]{:S(2)}, u32[]{:S(2)}) collective-permute-start(bf16[256,2048]{1,0:T(8,128)(2,1)} %get-tuple-element.114.refs_15_), channel_id=1, source_target_pairs={{0,1},{1,0},{2,3},{3,2},{4,5},{5,4},{6,7},{7,6},{8,9},{9,8},{10,11... | collective-permute-start | bytes 3145736 | tf_op jit(solution)/shard_map/ppermute | solution.py:106
  276.5 45.8 %collective-permute-start.30 = (bf16[256,2048]{1,0:T(8,128)(2,1)}, bf16[256,2048]{1,0:T(8,128)(2,1)}, u32[]{:S(2)}, u32[]{:S(2)}) collective-permute-start(bf16[256,2048]{1,0:T(8,128)(2,1)} %get-tuple-element.115.refs_15_), channel_id=1, source_target_pairs={{0,1},{1,0},{2,3},{3,2},{4,5},{5,4},{6,7},{7,6},{8,9},{9,8},{10,11... | collective-permute-start | bytes 3145736 | tf_op jit(solution)/shard_map/ppermute | solution.py:106
  307.4 517.7 %reduce-scatter.6.cloned.1.call-start = ((), (), s32[]{:S(2)}) async-start(), calls=%async_computation.7 | async-start | bytes 5242880 | tf_op jit(solution)/shard_map/reduce_scatter | solution.py:694
  366.1 466.8 %reduce-scatter.4.cloned.1.call-start = ((), (), s32[]{:S(2)}) async-start(), calls=%async_computation.6 | async-start | bytes 5242880 | tf_op jit(solution)/shard_map/reduce_scatter | solution.py:694
  474.8 51.4 %collective-permute-start.47 = (bf16[1024,2048]{1,0:T(8,128)(2,1)}, bf16[1024,2048]{1,0:T(8,128)(2,1)}, u32[]{:S(2)}, u32[]{:S(2)}) collective-permute-start(bf16[1024,2048]{1,0:T(8,128)(2,1)} %add_convert_fusion.1), channel_id=1, source_target_pairs={{0,1},{1,0},{2,3},{3,2},{4,5},{5,4},{6,7},{7,6},{8,9},{9,8},{10,11... | collective-permute-start | bytes 12582920 | tf_op jit(solution)/shard_map/ppermute | solution.py:106
  478.4 54.6 %collective-permute-start.55 = (bf16[1024,2048]{1,0:T(8,128)(2,1)}, bf16[1024,2048]{1,0:T(8,128)(2,1)}, u32[]{:S(2)}, u32[]{:S(2)}) collective-permute-start(bf16[1024,2048]{1,0:T(8,128)(2,1)} %convolution_convert_fusion), channel_id=1, source_target_pairs={{0,1},{1,0},{2,3},{3,2},{4,5},{5,4},{6,7},{7,6},{8,9},{9,8},{10,11... | collective-permute-start | bytes 12582920 | tf_op jit(solution)/shard_map/ppermute | solution.py:106
  481.9 51.2 %collective-permute-start.54 = (bf16[1024,2048]{1,0:T(8,128)(2,1)}, bf16[1024,2048]{1,0:T(8,128)(2,1)}, u32[]{:S(2)}, u32[]{:S(2)}) collective-permute-start(bf16[1024,2048]{1,0:T(8,128)(2,1)} %convolution_convert_fusion.1), channel_id=1, source_target_pairs={{0,1},{1,0},{2,3},{3,2},{4,5},{5,4},{6,7},{7,6},{8,9},{9,8},{10,11... | collective-permute-start | bytes 12582920 | tf_op jit(solution)/shard_map/ppermute | solution.py:106
  485.5 47.5 %collective-permute-start.53 = (bf16[1024,2048]{1,0:T(8,128)(2,1)}, bf16[1024,2048]{1,0:T(8,128)(2,1)}, u32[]{:S(2)}, u32[]{:S(2)}) collective-permute-start(bf16[1024,2048]{1,0:T(8,128)(2,1)} %convolution_convert_fusion.2), channel_id=1, source_target_pairs={{0,1},{1,0},{2,3},{3,2},{4,5},{5,4},{6,7},{7,6},{8,9},{9,8},{10,11... | collective-permute-start | bytes 12582920 | tf_op jit(solution)/shard_map/ppermute | solution.py:106
  492.0 41.1 %collective-permute-start.56 = (bf16[1024,2048]{1,0:T(8,128)(2,1)}, bf16[1024,2048]{1,0:T(8,128)(2,1)}, u32[]{:S(2)}, u32[]{:S(2)}) collective-permute-start(bf16[1024,2048]{1,0:T(8,128)(2,1)} %convolution_convert_fusion.6), channel_id=1, source_target_pairs={{0,1},{1,0},{2,3},{3,2},{4,5},{5,4},{6,7},{7,6},{8,9},{9,8},{10,11... | collective-permute-start | bytes 12582920 | tf_op jit(solution)/shard_map/ppermute | solution.py:106
  681.6 43.2 %collective-permute-start.61 = (bf16[256,2048]{1,0:T(8,128)(2,1)}, bf16[256,2048]{1,0:T(8,128)(2,1)}, u32[]{:S(2)}, u32[]{:S(2)}) collective-permute-start(bf16[256,2048]{1,0:T(8,128)(2,1)} %get-tuple-element.144), channel_id=1, source_target_pairs={{0,4},{1,3},{2,6},{3,1},{4,0},{5,7},{6,2},{7,5},{8,12},{9,11},{10,... | collective-permute-start | bytes 3145736 | tf_op jit(solution)/shard_map/ppermute | solution.py:60
  718.4 103.2 %collective-permute-start.69 = (bf16[256,2048]{1,0:T(8,128)(2,1)}, bf16[256,2048]{1,0:T(8,128)(2,1)}, u32[]{:S(2)}, u32[]{:S(2)}) collective-permute-start(bf16[256,2048]{1,0:T(8,128)(2,1)} %get-tuple-element.156), channel_id=1, source_target_pairs={{0,4},{1,3},{2,6},{3,1},{4,0},{5,7},{6,2},{7,5},{8,12},{9,11},{10,... | collective-permute-start | bytes 3145736 | tf_op jit(solution)/shard_map/ppermute | solution.py:60
  723.6 55.1 %collective-permute-start.65 = (bf16[256,2048]{1,0:T(8,128)(2,1)S(1)}, bf16[256,2048]{1,0:T(8,128)(2,1)S(1)}, u32[]{:S(2)}, u32[]{:S(2)}) collective-permute-start(bf16[256,2048]{1,0:T(8,128)(2,1)S(1)} %copy-done.76), channel_id=1, source_target_pairs={{0,4},{1,3},{2,6},{3,1},{4,0},{5,7},{6,2},{7,5},{8,12},{9,11},{10,... | collective-permute-start | bytes 3145736 | tf_op jit(solution)/shard_map/ppermute | solution.py:60
  724.8 42.8 %collective-permute-start.49 = (bf16[256,2048]{1,0:T(8,128)(2,1)S(1)}, bf16[256,2048]{1,0:T(8,128)(2,1)S(1)}, u32[]{:S(2)}, u32[]{:S(2)}) collective-permute-start(bf16[256,2048]{1,0:T(8,128)(2,1)S(1)} %get-tuple-element.194), channel_id=1, source_target_pairs={{0,4},{1,3},{2,6},{3,1},{4,0},{5,7},{6,2},{7,5},{8,12},{9,11},{10,... | collective-permute-start | bytes 3145736 | tf_op jit(solution)/shard_map/ppermute | solution.py:60
  726.7 45.4 %collective-permute-start.86 = (f32[1024,148]{0,1:T(8,128)S(1)}, f32[1024,148]{0,1:T(8,128)S(1)}, u32[]{:S(2)}, u32[]{:S(2)}) collective-permute-start(f32[1024,148]{0,1:T(8,128)S(1)} %constant_dynamic-update-slice_fusion.32), channel_id=1, source_target_pairs={{0,1},{1,0},{2,3},{3,2},{4,5},{5,4},{6,7},{7,6},{8,9},{9,8},{10,11... | collective-permute-start | bytes 1818632 | tf_op jit(solution)/shard_map/ppermute | solution.py:106
  778.6 43.0 %collective-permute-start.71 = (bf16[256,2048]{1,0:T(8,128)(2,1)}, bf16[256,2048]{1,0:T(8,128)(2,1)}, u32[]{:S(2)}, u32[]{:S(2)}) collective-permute-start(bf16[256,2048]{1,0:T(8,128)(2,1)} %add_convert_fusion.3), channel_id=1, source_target_pairs={{0,2},{1,5},{2,0},{3,7},{4,6},{5,1},{6,4},{7,3},{8,10},{9,13},{10,... | collective-permute-start | bytes 3145736 | tf_op jit(solution)/shard_map/ppermute | solution.py:60
  (157 other events, 2586.5 us)
Sparse Core Ops, SparseCore 0:
  26.6 81.4 all-gather.5
  110.2 79.1 all-gather.3
  191.6 79.2 all-gather.7
  307.5 75.9 reduce-scatter.7
  385.8 77.2 reduce-scatter.5
  666.1 77.5 reduce-scatter.3

commit v3 on v2

--- a/solution.py
+++ b/solution.py
@@ -10,6 +10,7 @@
 STREAMS = 4
 LANES = 128
 GROUP = 16
+UNROLL = 1
 
 HIGHEST = lax.Precision.HIGHEST
 EPS_NORM = 1e-05
@@ -73,6 +74,23 @@
                 for x, y in zip(held[: 1 << i], got)
             ]
         return held[0]
+
+    def scatter_packed(self, low, high):
+        for i in reversed(range(self.bits)):
+            got = self.step(high, i)
+            if i == 0:
+                return low, got
+            total = (low.astype(jnp.float32) + got.astype(jnp.float32)).astype(low.dtype)
+            side = total.shape[0] // 2
+            low, high = total[:side], total[side:]
+
+    def direct(self, value, j):
+        pairs = []
+        for h in range(self.size):
+            for m in range(self.cores):
+                place = j if m % 2 == 0 else self.turned(j)
+                pairs.append((h * self.cores + m, (h ^ place) * self.cores + m))
+        return lax.ppermute(value, PLANE, pairs)
 
     def ordered(self, slots):
         rows = slots[0].shape[0]
@@ -149,31 +167,36 @@
         stat_ref[rows, :] = stat
         return carry
 
-    lax.fori_loop(0, tile // GROUP, group, 0)
-
-
-def forward_streams(slots, pick, mixer_in, mixer_out, bias, gain):
+    lax.fori_loop(0, tile // GROUP, group, 0, unroll=UNROLL)
+
+
+def forward_streams(slots, at, blocks, before, pick, mixer_in, mixer_out, bias, gain):
     count = len(slots)
     rows, width = slots[0].shape
     tile = min(128, rows)
+    steps = rows // tile
     whole = lambda shape: pl.BlockSpec(shape, lambda i: (0,) * len(shape))
     by_row = lambda cols: pl.BlockSpec((tile, cols), lambda i: (i, 0))
+    shifted = lambda cols: pl.BlockSpec((tile, cols), lambda i: (at * steps + i, 0))
+    given = 1 + count + 4
     return pl.pallas_call(
-        lambda *refs: forward_kernel(count, *refs),
-        grid=(rows // tile,),
+        lambda *refs: forward_kernel(count, *refs[:given], *refs[given + len(before) :]),
+        grid=(steps,),
         in_specs=[pl.BlockSpec(memory_space=pltpu.SMEM)]
         + [by_row(width)] * count
-        + [whole(mixer_in.shape), whole(mixer_out.shape), whole(bias.shape), whole(gain.shape)],
-        out_specs=[by_row(width)] * STREAMS + [by_row(LANES)] * 3,
-        out_shape=[jax.ShapeDtypeStruct((rows, width), jnp.bfloat16)] * STREAMS
-        + [jax.ShapeDtypeStruct((rows, LANES), jnp.float32)] * 3,
+        + [whole(mixer_in.shape), whole(mixer_out.shape), whole(bias.shape), whole(gain.shape)]
+        + [pl.BlockSpec(memory_space=pl.ANY)] * len(before),
+        out_specs=[shifted(width)] * STREAMS + [shifted(LANES)] * 3,
+        out_shape=[jax.ShapeDtypeStruct((blocks * rows, width), jnp.bfloat16)] * STREAMS
+        + [jax.ShapeDtypeStruct((blocks * rows, LANES), jnp.float32)] * 3,
+        input_output_aliases={given + i: i for i in range(len(before))},
         scratch_shapes=[pltpu.VMEM((tile, width), jnp.bfloat16)],
         compiler_params=pltpu.CompilerParams(vmem_limit_bytes=VMEM),
         cost_estimate=pl.CostEstimate(
             flops=rows * width * 80, bytes_accessed=rows * width * 2 * (count + STREAMS), transcendentals=0
         ),
         name="forward_streams",
-    )(pick, *slots, mixer_in, mixer_out, bias, gain)
+    )(pick, *slots, mixer_in, mixer_out, bias, gain, *before)
 
 
 def split_dot(left, right, contract):
@@ -182,14 +205,14 @@
     return dot(left, high, contract) + dot(left, low, contract)
 
 
-def backward_kernel(count, pick, *refs):
+def backward_kernel(count, half, pick, order, *refs):
     slots, refs = refs[:count], refs[count:]
     mine, refs = refs[:STREAMS], refs[STREAMS:]
     theirs, refs = refs[:STREAMS], refs[STREAMS:]
     normed, refs = refs[:STREAMS], refs[STREAMS:]
     mix_ref, pre_ref, stat_ref, target_ref, scale_ref, refs = *refs[:5], refs[5:]
     in_ref, out_ref, gain_ref, inverse_gain_ref, refs = *refs[:4], refs[4:]
-    grads, refs = refs[:count], refs[count:]
+    grads_ref, refs = refs[0], refs[1:]
     gain_grad_ref, in_grad_ref, out_grad_ref, bias_grad_ref, last_ref, dmix_ref, gain_sum = refs
     tile = last_ref.shape[0]
 
@@ -207,6 +230,9 @@
             last_ref[...] = slots[j][...]
 
     lane = lax.broadcasted_iota(jnp.int32, (GROUP, LANES), 1)
+
+    def placed(j, start, size):
+        return pl.ds(pl.multiple_of(order[j] * half + pl.program_id(0) * tile + start, GROUP), size)
 
     def group(g, carry):
         rows = pl.ds(pl.multiple_of(g * GROUP, GROUP), GROUP)
@@ -231,14 +257,14 @@
             total = mix[:, j : j + 1] * grad[0]
             for c in range(1, STREAMS):
                 total = total + mix[:, c * count + j : c * count + j + 1] * grad[c]
-            grads[j][rows, :] = total.astype(jnp.bfloat16)
+            grads_ref[placed(j, g * GROUP, GROUP), :] = total.astype(jnp.bfloat16)
             for c in range(STREAMS):
                 value = jnp.sum(grad[c] * part, -1, keepdims=True)
                 dmix = jnp.where(lane == c * count + j, value, dmix)
         dmix_ref[rows, :] = dmix
         return carry
 
-    lax.fori_loop(0, tile // GROUP, group, 0)
+    lax.fori_loop(0, tile // GROUP, group, 0, unroll=UNROLL)
     dmix = dmix_ref[...]
     last = last_ref[...].astype(jnp.float32)
     inverse = lax.rsqrt(jnp.mean(last * last, -1, keepdims=True) + EPS_RMS)
@@ -265,35 +291,37 @@
 
         @pl.when(pick[0] == j)
         def _(j=j):
-            grads[j][...] = (grads[j][...].astype(jnp.float32) + extra).astype(jnp.bfloat16)
+            place = placed(j, 0, tile)
+            grads_ref[place, :] = (grads_ref[place, :].astype(jnp.float32) + extra).astype(jnp.bfloat16)
 
     @pl.when(pl.program_id(0) == pl.num_programs(0) - 1)
     def _():
         gain_grad_ref[...] = jnp.sum(gain_sum[...], 1)
 
 
-def backward_streams(slots, mine, theirs, at, normed, mix, pre, stat, target, scale, pick, mixer_in, mixer_out, gain):
+def backward_streams(slots, start, half, mine, theirs, at, normed, mix, pre, stat, target, scale, pick, order, mixer_in, mixer_out, gain):
     count = len(slots)
-    rows, width = slots[0].shape
+    rows, width = half, slots[0].shape[1]
     tile = min(128, rows)
     steps = rows // tile
     whole = lambda shape: pl.BlockSpec(shape, lambda i: (0,) * len(shape))
     by_row = lambda cols: pl.BlockSpec((tile, cols), lambda i: (i, 0))
-    shifted = pl.BlockSpec((tile, width), lambda i: (at * steps + i, 0))
+    shifted = lambda cols: pl.BlockSpec((tile, cols), lambda i: (at * steps + i, 0))
+    within = pl.BlockSpec((tile, width), lambda i: (start // tile + i, 0))
     hidden = mixer_in.shape[1]
     return pl.pallas_call(
-        lambda *refs: backward_kernel(count, *refs),
+        lambda *refs: backward_kernel(count, half, *refs),
         grid=(steps,),
-        in_specs=[pl.BlockSpec(memory_space=pltpu.SMEM)]
-        + [by_row(width)] * count
-        + [shifted] * (2 * STREAMS)
-        + [by_row(width)] * STREAMS
-        + [by_row(LANES)] * 3
+        in_specs=[pl.BlockSpec(memory_space=pltpu.SMEM)] * 2
+        + [within] * count
+        + [pl.BlockSpec((tile, width), lambda i, c=c: (at * steps + i, c)) for _, c in mine + theirs]
+        + [shifted(width)] * STREAMS
+        + [shifted(LANES)] * 3
         + [by_row(width), by_row(LANES)]
         + [whole(mixer_in.shape), whole(mixer_out.shape), whole(gain.shape), whole(gain.shape)],
-        out_specs=[by_row(width)] * count
+        out_specs=[whole((count * half, width))]
         + [whole((STREAMS, width)), whole((width, hidden)), whole((hidden, LANES)), whole((1, LANES))],
-        out_shape=[jax.ShapeDtypeStruct((rows, width), jnp.bfloat16)] * count
+        out_shape=[jax.ShapeDtypeStruct((count * half, width), jnp.bfloat16)]
         + [
             jax.ShapeDtypeStruct((STREAMS, width), jnp.float32),
             jax.ShapeDtypeStruct((width, hidden), jnp.float32),
@@ -312,7 +340,7 @@
             transcendentals=0,
         ),
         name="backward_streams",
-    )(pick, *slots, *mine, *theirs, *normed, mix, pre, stat, target, scale, mixer_in, mixer_out, gain, 1.0 / gain)
+    )(pick, order, *slots, *(x for x, _ in mine + theirs), *normed, mix, pre, stat, target, scale, mixer_in, mixer_out, gain, 1.0 / gain)
 
 
 def rope_tables(positions):
@@ -335,9 +363,10 @@
 
 
 def attention_kernel(count, half, heads, which, *refs):
-    q_ref, k_ref, v_ref, g_ref, cos_ref, right_ref, left_ref = refs[:7]
-    o_ref, dq_ref, dk_ref, dv_ref = refs[7:11]
-    k_s, dk_s, dv_s, p_s, o_s, dq_s, top_s, sum_s = refs[11:]
+    near, far, (cos_ref, right_ref, left_ref) = refs[:4], refs[4:8], refs[8:11]
+    o_ref, dq_ref, dk_ref, dv_ref, all_ref = refs[11:16]
+    q_s, k_s, v_s, g_s, dk_s, dv_s, p_s, o_s, dq_s, top_s, sum_s = refs[16:]
+    piece = heads * HD
     blocks = 2 * count
     scale = HD ** (-0.5)
     bf16, f32 = jnp.bfloat16, jnp.float32
@@ -346,20 +375,29 @@
     def at(b):
         return pl.ds(pl.multiple_of(((lax.rem(b, 2) ^ m) * count + lax.div(b, 2)) * half, half), half)
 
+    def by_owner(a, side):
+        return pl.ds(pl.multiple_of((2 * a + side) * half, half), half)
+
     def cols(n):
         return slice(n * HD, (n + 1) * HD)
 
-    def prepare(b, carry):
-        rows = pl.ds(pl.multiple_of(b * half, half), half)
-        for n in range(heads):
-            k_s[rows, cols(n)] = turn(
-                k_ref[rows, cols(n)], cos_ref[rows, :], right_ref[rows, :], left_ref[rows, :], 1.0
-            ).astype(bf16)
-        dk_s[rows, :] = jnp.zeros((half, heads * HD), f32)
-        dv_s[rows, :] = jnp.zeros((half, heads * HD), f32)
-        return carry
-
-    lax.fori_loop(0, blocks, prepare, 0)
+    for side, (q_ref, k_ref, v_ref, g_ref) in enumerate((near, far)):
+
+        def prepare(a, carry, side=side, q_ref=q_ref, k_ref=k_ref, v_ref=v_ref, g_ref=g_ref):
+            rows = pl.ds(pl.multiple_of(a * half, half), half)
+            here = pl.ds(pl.multiple_of((side * count + a) * half, half), half)
+            for n in range(heads):
+                for given, kept in ((q_ref, q_s), (k_ref, k_s)):
+                    kept[here, cols(n)] = turn(
+                        given[rows, cols(n)], cos_ref[here, :], right_ref[here, :], left_ref[here, :], 1.0
+                    ).astype(bf16)
+            v_s[here, :] = v_ref[rows, :]
+            g_s[here, :] = g_ref[rows, :]
+            dk_s[here, :] = jnp.zeros((half, heads * HD), f32)
+            dv_s[here, :] = jnp.zeros((half, heads * HD), f32)
+            return carry
+
+        lax.fori_loop(0, count, prepare, 0)
     later = lax.broadcasted_iota(jnp.int32, (half, half), 1) > lax.broadcasted_iota(jnp.int32, (half, half), 0)
 
     def lanes(value, op):
@@ -371,13 +409,8 @@
 
     def query_block(i, carry):
         here = at(i)
-        queries = [
-            turn(
-                q_ref[here, cols(n)], cos_ref[here, :], right_ref[here, :], left_ref[here, :], 1.0
-            ).astype(bf16)
-            for n in range(heads)
-        ]
-        grads = [g_ref[here, cols(n)] for n in range(heads)]
+        queries = [q_s[here, cols(n)] for n in range(heads)]
+        grads = [g_s[here, cols(n)] for n in range(heads)]
 
         def scores(j, last):
             there = at(j)
@@ -404,7 +437,7 @@
                 p = jnp.exp(p_s[n, :, spot] - tops[n])
                 p_s[n, :, spot] = p
                 sum_s[n] += lanes(p, jnp.add)
-                o_s[n] += dot(p.astype(bf16), v_ref[there, cols(n)], (1, 0))
+                o_s[n] += dot(p.astype(bf16), v_s[there, cols(n)], (1, 0))
             return c
 
         lax.fori_loop(0, i + 1, mixing, 0)
@@ -421,7 +454,7 @@
             spot = pl.ds(pl.multiple_of(j * half, half), half)
             for n in range(heads):
                 p = p_s[n, :, spot] * shares[n]
-                dp = dot(grads[n], v_ref[there, cols(n)], (1, 1))
+                dp = dot(grads[n], v_s[there, cols(n)], (1, 1))
                 ds = (p * (dp - deltas[n])).astype(bf16)
                 dq_s[n] += dot(ds, k_s[there, cols(n)], (1, 0))
                 dk_s[there, cols(n)] += dot(ds, queries[n], (0, 0))
@@ -429,39 +462,45 @@
             return c
 
         lax.fori_loop(0, i + 1, back, 0)
+        place = by_owner(lax.div(i, 2), lax.rem(i, 2) ^ m)
         for n in range(heads):
-            dq_ref[here, cols(n)] = turn(
-                dq_s[n] * scale, cos_ref[here, :], right_ref[here, :], left_ref[here, :], -1.0
-            ).astype(bf16)
+            found = turn(dq_s[n] * scale, cos_ref[here, :], right_ref[here, :], left_ref[here, :], -1.0).astype(bf16)
+            dq_ref[here, cols(n)] = found
+            all_ref[place, cols(n)] = found
         return carry
 
     lax.fori_loop(0, blocks, query_block, 0)
 
     def finish(b, carry):
         rows = pl.ds(pl.multiple_of(b * half, half), half)
+        place = by_owner(lax.rem(b, count), lax.div(b, count))
         for n in range(heads):
-            dk_ref[rows, cols(n)] = turn(
+            found = turn(
                 dk_s[rows, cols(n)] * scale, cos_ref[rows, :], right_ref[rows, :], left_ref[rows, :], -1.0
             ).astype(bf16)
-        dv_ref[rows, :] = dv_s[rows, :].astype(bf16)
+            dk_ref[rows, cols(n)] = found
+            all_ref[place, cols(heads + n)] = found
+        found = dv_s[rows, :].astype(bf16)
+        dv_ref[rows, :] = found
+        all_ref[place, 2 * piece : 3 * piece] = found
         return carry
 
     lax.fori_loop(0, blocks, finish, 0)
 
 
-def attention(query, keys, values, grad, positions, which, count):
-    rows, piece = query.shape
+def attention(near, far, positions, which, count):
+    rows, piece = 2 * near[0].shape[0], near[0].shape[1]
     heads, half = piece // HD, rows // (2 * count)
     vmem = pl.BlockSpec(memory_space=pltpu.VMEM)
     out = jax.ShapeDtypeStruct((rows, piece), jnp.bfloat16)
     wide = lambda *shape: pltpu.VMEM(shape, jnp.float32)
     return pl.pallas_call(
         lambda *refs: attention_kernel(count, half, heads, *refs),
-        in_specs=[pl.BlockSpec(memory_space=pltpu.SMEM)] + [vmem] * 7,
-        out_specs=[vmem] * 4,
-        out_shape=[out] * 4,
-        scratch_shapes=[
-            pltpu.VMEM((rows, piece), jnp.bfloat16),
+        in_specs=[pl.BlockSpec(memory_space=pltpu.SMEM)] + [vmem] * 11,
+        out_specs=[vmem] * 5,
+        out_shape=[out] * 4 + [jax.ShapeDtypeStruct((rows, 3 * piece), jnp.bfloat16)],
+        scratch_shapes=[pltpu.VMEM((rows, piece), jnp.bfloat16)] * 4
+        + [
             wide(rows, piece),
             wide(rows, piece),
             wide(heads, half, rows),
@@ -472,30 +511,182 @@
         ],
         compiler_params=pltpu.CompilerParams(vmem_limit_bytes=VMEM),
         cost_estimate=pl.CostEstimate(
-            flops=6 * rows * rows * piece, bytes_accessed=rows * piece * 20, transcendentals=rows * rows * heads // 2
+            flops=40 * rows * rows * piece, bytes_accessed=rows * piece * 20, transcendentals=rows * rows * heads // 2
         ),
         name="attention",
-    )(which, query, keys, values, grad, *rope_tables(positions))
-
-
-def total(value, plane):
+    )(which, *near, *far, *rope_tables(positions))
+
+
+def project(streams, weights, types):
+    rows, width = streams[0].shape
+    count = len(streams)
+    piece = weights.shape[1] // count
+    tile = min(256, rows)
+
+    def kernel(*refs):
+        for c in range(count):
+            found = dot(refs[c][...], refs[count][:, c * piece : (c + 1) * piece], (1, 0))
+            refs[count + 1 + c][...] = found.astype(types[c])
+
+    return pl.pallas_call(
+        kernel,
+        grid=(rows // tile,),
+        in_specs=[pl.BlockSpec((tile, width), lambda i: (i, 0))] * count
+        + [pl.BlockSpec(weights.shape, lambda i: (0, 0))],
+        out_specs=[pl.BlockSpec((tile, piece), lambda i: (i, 0))] * count,
+        out_shape=[jax.ShapeDtypeStruct((rows, piece), t) for t in types],
+        compiler_params=pltpu.CompilerParams(vmem_limit_bytes=VMEM),
+        cost_estimate=pl.CostEstimate(
+            flops=2 * rows * width * piece * count, bytes_accessed=2 * rows * width * count, transcendentals=0
+        ),
+        name="project",
+    )(*streams, weights)
+
+
+def project_back(entries, weights):
+    count = len(entries)
+    rows, piece = entries[0].shape[0], entries[0].shape[1] // 3
+    width = weights[0].shape[0]
+    side = rows // 2
+
+    def kernel(*refs):
+        found = dot(refs[0][...], refs[count][...], (1, 1))
+        for j in range(1, count):
+            found = found + dot(refs[j][...], refs[count + j][...], (1, 1))
+        refs[2 * count][...] = found[:side].astype(jnp.bfloat16)
+        refs[2 * count + 1][...] = found[side:].astype(jnp.bfloat16)
+
+    return pl.pallas_call(
+        kernel,
+        grid=(3, 2),
+        in_specs=[pl.BlockSpec((rows, piece), lambda c, i: (0, c))] * count
+        + [pl.BlockSpec((width // 2, piece), lambda c, i: (i, c))] * count,
+        out_specs=[pl.BlockSpec((side, width // 2), lambda c, i: (0, 2 * c + i))] * 2,
+        out_shape=[jax.ShapeDtypeStruct((side, 3 * width), jnp.bfloat16)] * 2,
+        compiler_params=pltpu.CompilerParams(vmem_limit_bytes=VMEM),
+        name="project_back",
+    )(*entries, *weights)
+
+
+def add_in_slots(near, far, order, count):
+    rows, width = near.shape
+    block = rows // count
+    tile = min(128, block)
+    steps = block // tile
+    side = count // 2
+
+    def kernel(order, a, b, c, d, low, high):
+        low[...] = (a[...].astype(jnp.float32) + b[...].astype(jnp.float32)).astype(jnp.bfloat16)
+        high[...] = (c[...].astype(jnp.float32) + d[...].astype(jnp.float32)).astype(jnp.bfloat16)
+
+    def spec(shift):
+        return pl.BlockSpec((tile, width), lambda j, i, order: (order[shift + j] * steps + i, 0))
+
+    out = pl.BlockSpec((tile, width), lambda j, i, order: (j * steps + i, 0))
+    return pl.pallas_call(
+        kernel,
+        grid_spec=pltpu.PrefetchScalarGridSpec(
+            num_scalar_prefetch=1,
+            grid=(side, steps),
+            in_specs=[spec(0), spec(0), spec(side), spec(side)],
+            out_specs=[out, out],
+        ),
+        out_shape=[jax.ShapeDtypeStruct((rows // 2, width), jnp.bfloat16)] * 2,
+        compiler_params=pltpu.CompilerParams(vmem_limit_bytes=VMEM),
+        name="add_in_slots",
+    )(order, near, far, near, far)
+
+
+def outer(groups):
+    pieces = len(groups[0][0])
+    rows = min(a.shape[0] for a, _ in groups[0][0])
+    width = groups[0][0][0][0].shape[1]
+    tile = min(256, width)
+    sizes = [right[0][0].shape[1] for _, right in groups]
+    specs, arrays = [], []
+    for left, right in groups:
+        for a, k in left:
+            specs.append(pl.BlockSpec((rows, tile), lambda i, k=k: (k, i)))
+            arrays.append(a)
+        for b, k in right:
+            specs.append(pl.BlockSpec((rows, b.shape[1]), lambda i, k=k: (k, 0)))
+            arrays.append(b)
+
+    def kernel(*refs):
+        out, at = refs[-1], 0
+        for g, size in enumerate(sizes):
+            mine = refs[2 * pieces * g : 2 * pieces * (g + 1)]
+            found = dot(mine[0][...], mine[pieces][...], (0, 0))
+            for p in range(1, pieces):
+                found = found + dot(mine[p][...], mine[pieces + p][...], (0, 0))
+            out[:, at : at + size] = found.astype(jnp.bfloat16)
+            at += size
+
+    total_rows = rows * pieces
+    return pl.pallas_call(
+        kernel,
+        grid=(width // tile,),
+        in_specs=specs,
+        out_specs=pl.BlockSpec((tile, sum(sizes)), lambda i: (i, 0)),
+        out_shape=jax.ShapeDtypeStruct((width, sum(sizes)), jnp.bfloat16),
+        compiler_params=pltpu.CompilerParams(vmem_limit_bytes=VMEM),
+        cost_estimate=pl.CostEstimate(
+            flops=2 * total_rows * width * sum(sizes),
+            bytes_accessed=2 * total_rows * (width * len(groups) + sum(sizes)) + 2 * width * sum(sizes),
+            transcendentals=0,
+        ),
+        name="outer",
+    )(*arrays)
+
+
+def total_over_dp(value, plane):
     z, zs = lax.axis_index("dp"), lax.axis_size("dp")
     rows = value.shape[0]
     side = rows // plane.cores
-    block = side // plane.size
-    part = block // zs
     cut = lambda x, at, size: lax.dynamic_slice_in_dim(x, at * size, size, 0)
+    put = lambda out, x, at: lax.dynamic_update_slice_in_dim(out, x, at * x.shape[0], 0)
     value = cut(value, plane.m, side) + plane.swap(cut(value, 1 - plane.m, side))
-    value = plane.scatter([cut(value, plane.h ^ plane.place(j), block) for j in range(plane.size)])
-    ring = lambda x, k: lax.ppermute(x, "dp", [(i, (i + k) % zs) for i in range(zs)])
+    over_dp = lambda x, k: lax.ppermute(x, "dp", [(i, (i + k) % zs) for i in range(zs)])
+    part = side // zs
     mine = cut(value, z, part)
     for k in range(1, zs):
-        mine = mine + ring(cut(value, (z + k) % zs, part), k)
-    out = lax.dynamic_update_slice_in_dim(jnp.zeros((block,) + value.shape[1:], value.dtype), mine, z * part, 0)
+        mine = mine + over_dp(cut(value, (z + k) % zs, part), k)
+    out = put(jnp.zeros_like(value), mine, z)
     for k in range(1, zs):
-        out = lax.dynamic_update_slice_in_dim(out, ring(mine, k), (z + zs - k) % zs * part, 0)
-    out = plane.ordered(plane.gather(out))
-    return plane.both(out, plane.swap(out), 0).reshape((rows,) + value.shape[1:])
+        out = put(out, over_dp(mine, k), (z + zs - k) % zs)
+    return out
+
+
+def total_over_plane(out, plane):
+    side = out.shape[0]
+    cut = lambda x, at, size: lax.dynamic_slice_in_dim(x, at * size, size, 0)
+    block = side // plane.size
+    mine = cut(out, plane.h, block)
+    for j in range(1, plane.size):
+        mine = mine + plane.direct(cut(out, plane.h ^ plane.place(j), block), j)
+    out = plane.ordered([mine] + [plane.direct(mine, j) for j in range(1, plane.size)])
+    return plane.both(out, plane.swap(out), 0).reshape((2 * side,) + out.shape[1:])
+
+
+def interleave(own, sibling, m, half):
+    rows, width = own.shape
+    count = rows // half
+
+    def kernel(which, own_ref, sibling_ref, out):
+        at = lambda side: pl.ds(pl.multiple_of(side * half, half), half)
+        out[at(which[0]), :] = own_ref[...]
+        out[at(1 - which[0]), :] = sibling_ref[...]
+
+    block = pl.BlockSpec((half, width), lambda a: (a, 0))
+    return pl.pallas_call(
+        kernel,
+        grid=(count,),
+        in_specs=[pl.BlockSpec(memory_space=pltpu.SMEM), block, block],
+        out_specs=pl.BlockSpec((2 * half, width), lambda a: (a, 0)),
+        out_shape=jax.ShapeDtypeStruct((2 * rows, width), own.dtype),
+        compiler_params=pltpu.CompilerParams(vmem_limit_bytes=VMEM),
+        name="interleave",
+    )(m, own, sibling)
 
 
 def place_wide(entries, h, out_type, pieces, turned):
@@ -572,29 +763,22 @@
         gain = lax.dynamic_update_slice_in_dim(gain, came[None], (z + zs - k) % zs, 0)
     gain = gain.reshape(zs * count, STREAMS, -1).transpose(1, 0, 2).reshape(STREAMS, width).astype(f32)
 
-    parted = history.reshape(count, cores, half, width)
-    own_rows = [lax.dynamic_index_in_dim(parted[a], m, 0, keepdims=False) for a in range(count)]
-    up_parts = plane.trade(up_weight)
-    up_full = lax.all_gather(plane.stacked(up_parts), "dp", axis=0, tiled=True)
-    slots, waited = [], up_parts[-1]
-    marks = []
-    for a in range(count):
-        found = plane.gather(after(own_rows[a], waited))
-        marks.append(found[1])
-        slots.append(found)
-    down_parts = plane.trade(after(down_weight, marks[0]).T)
-    down_full = lax.all_gather(plane.stacked(down_parts), "dp", axis=0, tiled=True)
-    packed = jnp.stack(
-        [query_weight, key_weight, value_weight, after(out_weight, marks[min(1, count - 1)]).T], 0
-    )
-    packed = packed.reshape(4, depth, count, -1).transpose(1, 2, 0, 3).reshape(depth, -1)
-    narrow_full = lax.all_gather(plane.stacked(plane.trade(packed)), "dp", axis=0, tiled=True)
-    piece = narrow_full.shape[1] // 4
-    query_full, key_full, value_full, out_full = (
-        narrow_full[:, i * piece : (i + 1) * piece] for i in range(4)
-    )
-
+    parts = 2 if count % 2 == 0 else 1
+    per = count // parts
+    parted = history.reshape(parts, per, cores, half, width)
+    own_rows = [
+        lax.dynamic_index_in_dim(parted[g], m, 1, keepdims=False).reshape(per * half, width) for g in range(parts)
+    ]
+    swap_columns = lambda x: lax.all_to_all(x, "hist", 1, 0, tiled=True)
+    slots = [plane.gather(after(own_rows[0], part))]
+    up_mine = swap_columns(after(up_weight, part))
+    up_full = lax.all_gather(up_mine, "dp", axis=0, tiled=True)
+    for g in range(1, parts):
+        slots.append(plane.gather(after(own_rows[g], slots[-1][1])))
+    down_mine = swap_columns(after(down_weight.T, up_mine, gain, slots[-1][1]))
+    down_full = lax.all_gather(down_mine, "dp", axis=0, tiled=True)
     layer_of = [h ^ plane.place(j) for j in range(count)]
+    order = jnp.stack(layer_of).astype(jnp.int32)
     pick = sum(jnp.where(layer_of[j] == count - 1, j, 0) for j in range(count)).astype(jnp.int32).reshape(1)
 
     def to_slots(values):
@@ -614,15 +798,22 @@
     )
     bias_wide = jnp.pad(to_slots(mixer_bias).reshape(1, pairs), ((0, 0), (0, LANES - pairs)))
 
-    normed, mixes, pres, stats, others = [], [], [], [], []
-    for a in range(count):
-        *one, mix, pre, stat = forward_streams(slots[a], pick, in_wide, out_wide, bias_wide, gain)
-        normed.append(one)
-        mixes.append(mix)
-        pres.append(pre)
-        stats.append(stat)
-        others.append([plane.swap(x) for x in one])
-    streams = [jnp.concatenate([x[c] for x in normed + others], 0) for c in range(STREAMS)]
+    found = []
+    for g in range(parts):
+        found = forward_streams(slots[g], g, parts, found, pick, in_wide, out_wide, bias_wide, gain)
+        if g == 0:
+            packed = jnp.stack([query_weight, key_weight, value_weight, out_weight.T], 0)
+            packed = packed.reshape(4, depth, count, -1).transpose(1, 2, 0, 3).reshape(depth, -1)
+            packed, *found = lax.optimization_barrier((packed, *found))
+    narrow_mine = swap_columns(packed)
+    narrow_full = lax.all_gather(narrow_mine, "dp", axis=0, tiled=True)
+    piece = narrow_full.shape[1] // 4
+    out_full = narrow_full[:, 3 * piece :]
+    all_weights = plane.gather(narrow_full[:, : 3 * piece])
+    near_streams, (mixes, pres, stats) = list(found[:STREAMS]), found[STREAMS:]
+    far_streams = [None] * STREAMS
+    for c in reversed(range(STREAMS)):
+        far_streams[c] = plane.swap(near_streams[c])
     block = jnp.arange(count)[:, None] * rows + jnp.arange(half)[None, :]
     positions = jnp.concatenate([(block + m * half).reshape(-1), (block + (1 - m) * half).reshape(-1)])
 
@@ -630,103 +821,129 @@
     own_target = lax.dynamic_slice_in_dim(target, m * half, half, 0)
     own_scale = lax.dynamic_slice_in_dim(loss_count, m * half, half, 0).astype(f32) * domain_one
     branch_own = (own_target.astype(f32) * own_scale[:, None]).astype(bf16)
-    branch_near = plane.ordered(plane.gather(after(branch_own, marks[-1])))
-    branch_grad = jnp.concatenate([branch_near, plane.swap(branch_near)], 0)
-
-    hidden_pre = dot(streams[3], up_full, (1, 0))
-    hidden = gelu_exact(hidden_pre).astype(bf16)
-    act_grad = dot(branch_grad, down_full, (1, 0))
-    pre_grad = (act_grad * gelu_slope(hidden_pre)).astype(bf16)
-    down_part = dot(branch_grad, hidden, (0, 0)).astype(bf16)
-    up_part = dot(streams[3], pre_grad, (0, 0)).astype(bf16)
-
-    streams[0], streams[1], streams[2] = lax.optimization_barrier(
-        (streams[0], streams[1], streams[2], up_part, down_part)
-    )[:3]
-    query = dot(streams[0], query_full, (1, 0))
-    keys = dot(streams[1], key_full, (1, 0))
-    values = dot(streams[2], value_full, (1, 0)).astype(bf16)
-    attended_grad = dot(branch_grad, out_full, (1, 0)).astype(bf16)
-    attended, query_back, key_back, value_back = attention(
-        query, keys, values, attended_grad, positions, which_m, count
-    )
-
-    branch_far = (
-        dot(attended[near:], out_full, (1, 1)) + dot(hidden[near:], down_full, (1, 1))
-    ).astype(bf16)
-    query_back, key_back, value_back, branch_far = lax.optimization_barrier(
-        (query_back, key_back, value_back, branch_far)
-    )
-    branch = dot(attended[:near], out_full, (1, 1)) + dot(hidden[:near], down_full, (1, 1))
-    branch_sum = (branch + plane.swap(branch_far).astype(f32)).astype(bf16)
-    branch_rows = plane.scatter(
-        [lax.dynamic_slice_in_dim(branch_sum, layer_of[j] * half, half, 0) for j in range(count)]
-    ).astype(f32)
-    own_mix = lax.dynamic_index_in_dim(jnp.stack(mixes, 0), h, 0, keepdims=False)[:, :pairs]
-    own_mix = own_mix.reshape(half, STREAMS, count)
-    own_layers = [lax.dynamic_index_in_dim(jnp.stack([s[j] for s in slots], 0), h, 0, keepdims=False) for j in range(count)]
+    near_grad = plane.ordered(plane.gather(after(branch_own, slots[-1][1])))
+    far_grad = plane.swap(near_grad)
+
+    def mlp(stream, grad):
+        before = dot(stream, up_full, (1, 0))
+        back = dot(grad, down_full, (1, 0)) * gelu_slope(before)
+        return gelu_exact(before).astype(bf16), back.astype(bf16)
+
+    near_hidden, near_back = mlp(near_streams[3], near_grad)
+    far_hidden, far_back = mlp(far_streams[3], far_grad)
+    both = lambda near_one, far_one: [(near_one, 0), (far_one, 0)]
+    local = lambda one: [(one, 0), (one, 1)]
+    grads = both(near_grad, far_grad)
+    down_part = outer([(grads, both(near_hidden, far_hidden))])
+    down_sum = lax.psum_scatter(down_part, "dp", scatter_dimension=0, tiled=True)
+    up_part = outer([(both(near_streams[3], far_streams[3]), both(near_back, far_back))])
+    up_sum = lax.psum_scatter(up_part, "dp", scatter_dimension=0, tiled=True)
+
+    near_given, far_given, _, _ = lax.optimization_barrier(
+        (near_streams[:3] + [near_grad], far_streams[:3] + [far_grad], up_part, down_part)
+    )
+
+    types = (f32, f32, bf16, bf16)
+    attended, query_back, key_back, value_back, backs = attention(
+        project(near_given, narrow_full, types), project(far_given, narrow_full, types), positions, which_m, count
+    )
+
+    def owned(near_one, far_one):
+        return plane.scatter_packed(*add_in_slots(near_one, plane.swap(far_one), order, count))
+
+    near_back, far_back, up_part = lax.optimization_barrier((near_back, far_back, up_part))
+    far_mlp = dot(far_back, up_full, (1, 1)).astype(bf16)
+    near_mlp = dot(near_back, up_full, (1, 1)).astype(bf16)
+    owned_mlp = owned(near_mlp, far_mlp)
+    backs, attended, _, down_sum, all_weights = lax.optimization_barrier(
+        (backs, attended, owned_mlp, down_sum, all_weights)
+    )
+    own_backs = [lax.dynamic_slice_in_dim(backs, layer_of[j] * rows, rows, 0) for j in range(count)]
+    own_backs = own_backs[:1] + [plane.direct(own_backs[j], j) for j in range(1, count)]
+    narrow_part = outer(
+        [
+            (both(near_streams[0], far_streams[0]), local(query_back)),
+            (both(near_streams[1], far_streams[1]), local(key_back)),
+            (both(near_streams[2], far_streams[2]), local(value_back)),
+            (grads, local(attended)),
+        ]
+    )
+    narrow_sum = lax.psum_scatter(narrow_part, "dp", scatter_dimension=0, tiled=True)
+    own_backs[0] = after(own_backs[0], narrow_part)
+    near_backs, far_backs = project_back(own_backs, all_weights)
+    far_backs = plane.swap(far_backs)
+
+    attended = after(attended, near_backs)
+    branch_far = (dot(attended[near:], out_full, (1, 1)) + dot(far_hidden, down_full, (1, 1))).astype(bf16)
+    branch = (dot(attended[:near], out_full, (1, 1)) + dot(near_hidden, down_full, (1, 1))).astype(bf16)
+    branch_low, branch_high = owned(branch, branch_far)
+    own_mix = lax.dynamic_slice_in_dim(mixes, h * half, half, 0)[:, :pairs].reshape(half, STREAMS, count)
+
+    def own_block(j):
+        found = lax.dynamic_slice_in_dim(slots[0][j], h % per * half, half, 0)
+        for g in range(1, parts):
+            found = jnp.where(h // per == g, lax.dynamic_slice_in_dim(slots[g][j], h % per * half, half, 0), found)
+        return found
+
+    own_layers = [own_block(j) for j in range(count)]
+    mix_own = from_slots(own_mix)
+    mix_rows = plane.both(mix_own, plane.swap(mix_own), 0).reshape(rows, STREAMS, count)
+
+    def spread(summed, turned):
+        return place_wide(plane.trade_rows(summed), which_h, f32, len(turned), turned)
+
+    wide_sum = jnp.concatenate([up_sum, down_sum], 1)
+
+    scale_wide = jnp.broadcast_to(own_scale[:, None], (half, LANES))
+    own_part = lambda x: lax.dynamic_slice_in_dim(x, h * half, half, 0)
+    found = backward_streams(
+        own_layers,
+        0,
+        half,
+        [(near_backs, 0), (near_backs, 1), (near_backs, 2), (owned_mlp[0], 0)],
+        [(far_backs, 0), (far_backs, 1), (far_backs, 2), (owned_mlp[1], 0)],
+        0,
+        [own_part(x) for x in near_streams],
+        own_part(mixes),
+        own_part(pres),
+        own_part(stats),
+        own_target,
+        scale_wide,
+        pick,
+        order,
+        in_wide,
+        out_wide,
+        gain,
+    )
+    layer_grads, sums = found[0], found[1:]
+    layer_grads, branch_low, wide_sum = lax.optimization_barrier((layer_grads, branch_low, wide_sum))
+    branch_rows = branch_low.astype(f32) + branch_high.astype(f32)
     residual = sum(own_mix[:, STREAMS - 1, j, None] * own_layers[j].astype(f32) for j in range(count))
     output_own = (residual + branch_rows).astype(bf16)
     output = plane.both(output_own, plane.swap(output_own), 0).reshape(rows, width)
-    mix_own = from_slots(own_mix)
-    mix_rows = plane.both(mix_own, plane.swap(mix_own), 0).reshape(rows, STREAMS, count)
-
-    tails = [
-        (query_back, query_full),
-        (key_back, key_full),
-        (value_back, value_full),
-        (pre_grad, up_full),
-    ]
-    theirs = [plane.swap(dot(x[near:], w, (1, 1)).astype(bf16)) for x, w in tails]
-    mine = [dot(x[:near], w, (1, 1)).astype(bf16) for x, w in tails]
-
-    narrow_part = jnp.concatenate(
-        [
-            dot(streams[0], query_back, (0, 0)),
-            dot(streams[1], key_back, (0, 0)),
-            dot(streams[2], value_back, (0, 0)),
-            dot(branch_grad, attended, (0, 0)),
-        ],
-        1,
-    ).astype(bf16)
-
-    def spread(part, turned):
-        summed = lax.psum_scatter(part, "dp", scatter_dimension=0, tiled=True)
-        return place_wide(plane.trade_rows(summed), which_h, f32, len(turned), turned)
-
-    (up_grad,) = spread(up_part, (False,))
-    (down_grad,) = spread(down_part, (True,))
-    query_grad, key_grad, value_grad, out_grad = spread(narrow_part, (False, False, False, True))
-
-    scale_wide = after(jnp.broadcast_to(own_scale[:, None], (half, LANES)), narrow_part, branch_sum)
-    sums = None
-    history_grad = jnp.zeros((group_rows, width), bf16)
-    for a in range(count):
-        scale = jnp.where(h == a, scale_wide, 0.0)
-        found = backward_streams(
-            slots[a], mine, theirs, a, normed[a], mixes[a], pres[a], stats[a], own_target, scale, pick, in_wide, out_wide, gain
-        )
-        held, rest = list(found[:count]), found[count:]
-        sums = rest if sums is None else tuple(x + y for x, y in zip(sums, rest))
-        final = plane.scatter(held)
-        history_grad = lax.dynamic_update_slice_in_dim(history_grad, final, a * rows + m * half, 0)
-        history_grad = lax.dynamic_update_slice_in_dim(history_grad, plane.swap(final), a * rows + (1 - m) * half, 0)
-    history_grad = history_grad.reshape(history.shape)
-
+    came = lax.all_to_all(layer_grads, "hist", 0, 0, tiled=True)
     gain_sum, in_sum, out_sum, bias_sum = sums
     out_sum = from_slots(out_sum[:, :pairs].reshape(LANES, STREAMS, count)).reshape(LANES, pairs)
     bias_sum = from_slots(bias_sum[:, :pairs].reshape(1, STREAMS, count)).reshape(1, pairs)
-    small = jnp.concatenate(
-        [in_sum, gain_sum.T, jnp.pad(jnp.concatenate([out_sum, bias_sum], 0), ((0, width - LANES - 1), (0, 0)))], 1
-    )
-    small = total(small, plane)
+    spare = LANES - hidden_units - STREAMS
+    spare -= spare % 8
+    packed_sum = jnp.concatenate([out_sum, bias_sum], 0).reshape(-1)
+    packed_sum = jnp.pad(packed_sum, (0, width * spare - packed_sum.shape[0])).reshape(width, spare)
+    small = jnp.concatenate([in_sum[:, :hidden_units], gain_sum.T, packed_sum], 1)
+    small = total_over_dp(jnp.pad(small, ((0, 0), (0, LANES - small.shape[1]))), plane)
+    came, small, narrow_sum, wide_sum = lax.optimization_barrier((came, small, narrow_sum, wide_sum))
+    up_grad, down_grad = spread(wide_sum, (False, True))
+    history_grad = interleave(came, plane.swap(came), which_m, half).reshape(history.shape)
+    query_grad, key_grad, value_grad, out_grad = spread(narrow_sum, (False, False, False, True))
+    small = total_over_plane(small, plane)
     mixer_in_grad = small[:, :hidden_units]
-    gain_all = small[:, LANES : LANES + STREAMS].T
-    place = (lax.axis_index("dp") * count + h) * norm_gain.shape[1]
+    gain_all = small[:, hidden_units : hidden_units + STREAMS].T
+    place = (z * count + h) * norm_gain.shape[1]
     norm_gain_grad = lax.dynamic_slice_in_dim(gain_all, place, norm_gain.shape[1], 1)
-    tail = small[:, LANES + STREAMS :]
-    mixer_out_grad = tail[:hidden_units].reshape(hidden_units, STREAMS, count)
-    mixer_bias_grad = tail[LANES].reshape(STREAMS, count)
+    tail = small[:, hidden_units + STREAMS : hidden_units + STREAMS + spare].reshape(-1)[: (LANES + 1) * pairs]
+    tail = tail.reshape(LANES + 1, STREAMS, count)
+    mixer_out_grad = tail[:hidden_units]
+    mixer_bias_grad = tail[LANES]
     return (
         output,
         mix_rows,

time: 877 us -> 759 us (0.87)
  matrix products: 157 us -> 86.3 us
  local copies, waits for them, and re-layouts: 138 us -> 75.2 us
  starting transfers between devices: 115 us -> 67.6 us
  Pallas kernels: 200 us -> 232 us
  blocking collectives: 0 us -> 29.8 us
  waiting for transfers between devices: 191 us -> 203 us
  other arithmetic: 51.3 us -> 42.5 us
    dot_general x24 -> x10, matrix products: 157 us -> 86.3 us  [dot(): lax.dot_general(left, right, (((contract[0],), (contract[1],)), ((), ()))...]
    unnamed x208 -> x86, local copies, waits for them, and re-layouts: 62.8 us -> 17.8 us
    ppermute x39 -> x19, waiting for transfers between devices: 135 us -> 90.7 us  [step(): return lax.ppermute(value, PLANE, pairs)]
    all_to_all x0 -> x2, waiting for transfers between devices: none -> 39.1 us  [the longest x1 31.5 us: shards(): swap_columns = lambda x: lax.all_to_all(x, 'hist', 1, 0, tiled=True)]
    pallas_call x8 -> x12, Pallas kernels: 130 us -> 163 us  [the longest x3 47.9 us: outer(): pl.pallas_call(kernel, grid=(width // tile,), in_specs=specs, out_specs=p...]
    all_to_all x0 -> x2, blocking collectives: none -> 29.8 us  [shards(): swap_columns = lambda x: lax.all_to_all(x, 'hist', 1, 0, tiled=True)]
    ppermute x39 -> x19, starting transfers between devices: 50.8 us -> 22.2 us  [step(): return lax.ppermute(value, PLANE, pairs)]
    ppermute x30 -> x13, starting transfers between devices: 22.9 us -> 2.42 us  [swap(): return lax.ppermute(value, 'mp', [(m, m ^ 1) for m in range(self.cores)])]
  transfers between devices with their start and end apart: 102 -> 64, of which waited for: 29 -> 28; matrix products, arithmetic and copies ran while one was open for 38% -> 26% of each run, Pallas kernels for 23% -> 30%
where the time goes in v3:
time: 759 us; the launch traced here: 752 us
  Pallas kernels  232 us (31%)
  waiting for transfers between devices  203 us (27%)
  matrix products  86.3 us (11%)
  local copies, waits for them, and re-layouts  75.2 us (10%)
  starting transfers between devices  67.6 us (9%)
  other arithmetic  42.5 us (6%)
  blocking collectives  29.8 us (4%)
  between operations  15.9 us (2%)
    ppermute x19, waiting for transfers between devices, step(): return lax.ppermute(value, PLANE, pairs)  90.7 us
    dot_general x10, matrix products, dot(): lax.dot_general(left, right, (((contract[0],), (contract[1],)), ((), ()))...  86.3 us
    pallas_call x1, Pallas kernels, attention(): pl.pallas_call(lambda *refs: attention_kernel(count, half, heads, *refs),...  61.3 us
    pallas_call x3, Pallas kernels, outer(): pl.pallas_call(kernel, grid=(width // tile,), in_specs=specs, out_specs=p...  47.9 us
    pallas_call x2, Pallas kernels, forward_streams(): pl.pallas_call(lambda *refs: forward_kernel(count, *refs[:given], *refs[g...  37.9 us
    all_to_all x1, waiting for transfers between devices, shards(): swap_columns = lambda x: lax.all_to_all(x, 'hist', 1, 0, tiled=True)  31.5 us
    all_to_all x2, blocking collectives, shards(): swap_columns = lambda x: lax.all_to_all(x, 'hist', 1, 0, tiled=True)  29.8 us
    ppermute x9, waiting for transfers between devices, direct(): return lax.ppermute(value, PLANE, pairs)  23.4 us
  transfers between devices with their start and end apart: 64, of which 28 were waited for; matrix products, arithmetic and copies ran while one was open for 26% of the time, Pallas kernels for 30%

profile of v3, /device:TPU:0, one launch (start us, length us, event | category | flops | bytes accessed | tf_op | source)
XLA Modules:
  0.0 752.2 jit_solution(8024239353446977385)
XLA Ops:
  19.2 14.4 %all_to_all.69 = bf16[128,4,1024]{0,2,1:T(8,128)(2,1)S(1)} all-to-all(bf16[128,4,1024]{0,2,1:T(8,128)(2,1)S(1)} %bitcast.131), channel_id=1, replica_groups=mesh['dp'=4,'hist'=4,'mp'=2] {'hist'}, dimensions={1} | all-to-all | bytes 2097152 | tf_op jit(solution)/shard_map/all_to_all | solution.py:772
  41.8 23.5 %collective-permute-done.3.refs_2_ = bf16[512,2048]{1,0:T(8,128)(2,1)S(1)} collective-permute-done((bf16[512,2048]{1,0:T(8,128)(2,1)S(1)}, bf16[512,2048]{1,0:T(8,128)(2,1)S(1)}, u32[]{:S(2)}, u32[]{:S(2)}) %collective-permute-start.3) | collective-permute-done | bytes 2097184 | tf_op jit(solution)/shard_map/ppermute | solution.py:61
  77.5 15.5 %collective-permute-done.4.refs_2_ = bf16[512,2048]{1,0:T(8,128)(2,1)} collective-permute-done((bf16[512,2048]{1,0:T(8,128)(2,1)}, bf16[512,2048]{1,0:T(8,128)(2,1)}, u32[]{:S(2)}, u32[]{:S(2)}) %collective-permute-start.4) | collective-permute-done | bytes 2097184 | tf_op jit(solution)/shard_map/ppermute | solution.py:61
  93.0 15.3 %all_to_all.70 = bf16[128,4,1024]{0,2,1:T(8,128)(2,1)S(1)} all-to-all(bf16[128,4,1024]{0,2,1:T(8,128)(2,1)} %bitcast.135), channel_id=1, replica_groups=mesh['dp'=4,'hist'=4,'mp'=2] {'hist'}, dimensions={1} | all-to-all | bytes 2097152 | tf_op jit(solution)/shard_map/all_to_all | solution.py:772
  132.3 13.2 %collective-permute-done.10.refs_3_ = bf16[512,2048]{1,0:T(8,128)(2,1)} collective-permute-done((bf16[512,2048]{1,0:T(8,128)(2,1)S(1)}, bf16[512,2048]{1,0:T(8,128)(2,1)}, u32[]{:S(2)}, u32[]{:S(2)}) %collective-permute-start.10) | collective-permute-done | bytes 2097184 | tf_op jit(solution)/shard_map/ppermute | solution.py:61
  145.5 22.5 %collective-permute-done.11.refs_4_ = bf16[512,2048]{1,0:T(8,128)(2,1)} collective-permute-done((bf16[512,2048]{1,0:T(8,128)(2,1)}, bf16[512,2048]{1,0:T(8,128)(2,1)}, u32[]{:S(2)}, u32[]{:S(2)}) %collective-permute-start.11) | collective-permute-done | bytes 2097184 | tf_op jit(solution)/shard_map/ppermute | solution.py:61
  168.0 18.9 %forward_streams.2 = (bf16[1024,2048]{1,0:T(8,128)(2,1)}, bf16[1024,2048]{1,0:T(8,128)(2,1)}, bf16[1024,2048]{1,0:T(8,128)(2,1)}, bf16[1024,2048]{1,0:T(8,128)(2...) custom-call(s32[1]{0:T(128)} %bitcast.refs_0_, bf16[512,2048]{1,0:T(8,128)(2,1)} %bitcast.117, ...), custom_call_target="tpu_custom_call" | custom-call | flops 83886080 | bytes 16777216 | tf_op jit(solution)/shard_map/forward_streams/pallas_call | solution.py:182
  192.6 31.5 %all-to-all-done.2 = bf16[128,4,1024]{0,2,1:T(8,128)(2,1)S(1)} async-done(((bf16[128,4,1024]{0,2,1:T(8,128)(2,1)}), bf16[128,4,1024]{0,2,1:T(8,128)(2,1)S(1)}, u32[]{:S(2)}, u32[]{:S(2)}) %all-to-all-start.2) | async-done | bytes 1048608 | tf_op jit(solution)/shard_map/all_to_all | solution.py:772
  225.7 19.0 %forward_streams.3 = (bf16[1024,2048]{1,0:T(8,128)(2,1)}, bf16[1024,2048]{1,0:T(8,128)(2,1)}, bf16[1024,2048]{1,0:T(8,128)(2,1)}, bf16[1024,2048]{1,0:T(8,128)(2...) custom-call(s32[1]{0:T(128)} %bitcast.refs_0_, ...), custom_call_target="tpu_custom_call", output_to_operand_aliasing={{0}: (9, {}), {1}: (10, {}), {2}: (11, {}), {3}: (12, {}), ... | custom-call | flops 83886080 | bytes 16777216 | tf_op jit(solution)/shard_map/forward_streams/pallas_call | solution.py:182
  254.5 11.0 %multiply_convert_fusion.1 = (bf16[1024,1024]{1,0:T(8,128)(2,1)}, f32[1024,1024]{1,0:T(8,128)}) fusion(bf16[1024,2048]{1,0:T(8,128)(2,1)} %get-tuple-element.117.refs_0_, bf16[2048,1024]{1,0:T(8,128)(2,1)} %all-gather.6.cloned.1.call-done), kind=kOutput, calls=%fused_computation.19 | convolution fusion | flops 4300210176 | bytes 14680064 | tf_op jit(solution)/shard_map/dot_general | solution.py:24
  265.5 8.9 %multiply_convert_fusion = (bf16[1024,1024]{1,0:T(8,128)(2,1)}, f32[1024,1024]{1,0:T(8,128)}) fusion(bf16[1024,2048]{1,0:T(8,128)(2,1)} %collective-permute-done.19.refs_1_, bf16[2048,1024]{1,0:T(8,128)(2,1)S(1)} %copy-done.34), kind=kOutput, calls=%fused_computation.18 | convolution fusion | flops 4300210176 | bytes 14680064 | tf_op jit(solution)/shard_map/dot_general | solution.py:24
  274.4 14.2 %outer.4 = bf16[2048,1024]{1,0:T(8,128)(2,1)} custom-call(bf16[1024,2048]{1,0:T(8,128)(2,1)} %constant_dynamic-update-slice_fusion.8.refs_0_.refs_3_.refs_12_, bf16[1024,2048]{1,0:T(8,128)(2,1)} %collective-permute-done.18.refs_1_.refs_3_.refs_13_, bf16[1024,1024]{1,0:T(8,128)(2,1)} %get-tuple-element.309.refs_2_, bf16[1024,1024]{1,0:T(8,128)(2,1)} %get-tuple-element.311.refs_3_), custom_call_target="tpu_custom_call" | custom-call | flops 8589934592 | bytes 16777216 | tf_op jit(solution)/shard_map/outer/pallas_call | solution.py:626
  289.1 10.4 %fusion.11.refs_3_ = bf16[1024,1024]{1,0:T(8,128)(2,1)} fusion(f32[1024,1024]{1,0:T(8,128)} %get-tuple-element.312, bf16[1024,2048]{1,0:T(8,128)(2,1)} %collective-permute-done.18.refs_1_.refs_3_.refs_13_, bf16[2048,1024]{1,0:T(8,128)(2,1)} %all-gather.4.cloned.1.call-done), kind=kOutput, calls=%fused_computation.15 | convolution fusion | flops 4305453056 | bytes 14680064 | tf_op jit(solution)/shard_map/dot_general | solution.py:24
  299.6 8.9 %fusion.5.refs_2_ = bf16[1024,1024]{1,0:T(8,128)(2,1)} fusion(f32[1024,1024]{1,0:T(8,128)S(1)} %copy-done.36, bf16[1024,2048]{1,0:T(8,128)(2,1)} %constant_dynamic-update-slice_fusion.8.refs_0_.refs_3_.refs_12_, bf16[2048,1024]{1,0:T(8,128)(2,1)S(1)} %copy-done.33), kind=kOutput, calls=%fused_computation.9 | convolution fusion | flops 4305453056 | bytes 14680064 | tf_op jit(solution)/shard_map/dot_general | solution.py:24
  308.5 14.4 %outer.3 = bf16[2048,1024]{1,0:T(8,128)(2,1)} custom-call(bf16[1024,2048]{1,0:T(8,128)(2,1)} %get-tuple-element.117.refs_0_, bf16[1024,2048]{1,0:T(8,128)(2,1)} %collective-permute-done.19.refs_1_, bf16[1024,1024]{1,0:T(8,128)(2,1)} %fusion.5.refs_2_, bf16[1024,1024]{1,0:T(8,128)(2,1)} %fusion.11.refs_3_), custom_call_target="tpu_custom_call" | custom-call | flops 8589934592 | bytes 16777216 | tf_op jit(solution)/shard_map/outer/pallas_call | solution.py:626
  323.0 8.3 %convolution_convert_fusion = bf16[1024,2048]{1,0:T(8,128)(2,1)} fusion(bf16[1024,1024]{1,0:T(8,128)(2,1)S(1)} %copy-done.37, bf16[2048,1024]{1,0:T(8,128)(2,1)} %all-gather.6.cloned.1.call-done), kind=kOutput, calls=%fused_computation.22 | convolution fusion | flops 4297064448 | bytes 10485760 | tf_op jit(solution)/shard_map/dot_general | solution.py:24
  336.1 9.4 %convolution_convert_fusion.1.a.c = bf16[1024,2048]{1,0:T(8,128)(2,1)} fusion(bf16[1024,1024]{1,0:T(8,128)(2,1)} %fusion.5.refs_2_, bf16[2048,1024]{1,0:T(8,128)(2,1)} %all-gather.6.cloned.1.call-done), kind=kOutput, calls=%fused_computation.23 | convolution fusion | flops 4297064448 | bytes 10485760 | tf_op jit(solution)/shard_map/dot_general | solution.py:24
  345.5 6.7 add_in_slots.2
  362.0 11.3 %project.2 = (f32[1024,256]{1,0:T(8,128)}, f32[1024,256]{1,0:T(8,128)}, bf16[1024,256]{1,0:T(8,128)(2,1)}, bf16[1024,256]{1,0:T(8,128)(2,1)}) custom-call(bf16[1024,2048]{1,0:T(8,128)(2,1)} %get-tuple-element.120.refs_0_, bf16[1024,2048]{1,0:T(8,128)(2,1)} %get-tuple-element.121.refs_1_.refs_4_, bf16[1024,2048]{1,0:T(8,128)(2,1)} %get-tuple-element.122.refs_2_.refs_8_, ...), custom_call_target="tpu_custom_call" | custom-call | flops 4294967296 | bytes 16777216 | tf_op jit(solution)/shard_map/project/pallas_call | solution.py:531
  373.3 11.2 %project.3 = (f32[1024,256]{1,0:T(8,128)}, f32[1024,256]{1,0:T(8,128)}, bf16[1024,256]{1,0:T(8,128)(2,1)}, bf16[1024,256]{1,0:T(8,128)(2,1)}) custom-call(bf16[1024,2048]{1,0:T(8,128)(2,1)} %collective-permute-done.15.refs_0_.refs_1_, bf16[1024,2048]{1,0:T(8,128)(2,1)} %collective-permute-done.16.refs_1_.refs_5_, ...), custom_call_target="tpu_custom_call" | custom-call | flops 4294967296 | bytes 16777216 | tf_op jit(solution)/shard_map/project/pallas_call | solution.py:531
  398.7 61.3 %attention.1 = (bf16[2048,256]{1,0:T(8,128)(2,1)}, bf16[2048,256]{1,0:T(8,128)(2,1)}, bf16[2048,256]{1,0:T(8,128)(2,1)}, bf16[2048,256]{1,0:T(8,128)(2,1)}, bf16[2048,768]{1,0:T(8,128)(2,1)}) custom-call(s32[1]{0:T(128)} %bitcast.31.refs_0_.which, f32[1024,256]{1,0:T(8,128)} %get-tuple-element.125.refs_1_, f32[1024,256]{1,0:T(8,128)} %get-tuple-element.126.refs_2_, ...), custom_call_target="tpu_custom_call" | custom-call | flops 42949672960 | bytes 10485760 | tf_op jit(solution)/shard_map/attention/pallas_call | solution.py:497
  460.0 10.8 %fusion.59 = f32[1024,2048]{1,0:T(8,128)} fusion(bf16[1024,1024]{1,0:T(8,128)(2,1)} %get-tuple-element.311.refs_3_, bf16[2048,1024]{1,0:T(8,128)(2,1)} %all-gather.4.cloned.1.call-done), kind=kOutput, calls=%fused_computation.223 | convolution fusion | flops 4294967296 | bytes 14680064 | tf_op jit(solution)/shard_map/dot_general | solution.py:24
  479.0 19.3 %outer.5 = bf16[2048,1024]{1,0:T(8,128)(2,1)} custom-call(bf16[1024,2048]{1,0:T(8,128)(2,1)} %get-tuple-element.120.refs_0_, bf16[1024,2048]{1,0:T(8,128)(2,1)} %collective-permute-done.15.refs_0_.refs_1_, bf16[2048,256]{1,0:T(8,128)(2,1)} %get-tuple-element.144.refs_2_.refs_3_, bf16[2048,256]{1,0:T(8,128)(2,1)} %get-tuple-element.144.refs_2_.refs_3_, ...), custom_call_target="tpu_custom_call" | custom-call | flops 8589934592 | bytes 41943040 | tf_op jit(solution)/shard_map/outer/pallas_call | solution.py:626
  498.3 15.0 %collective-permute-done.27.refs_2_ = bf16[512,768]{1,0:T(8,128)(2,1)} collective-permute-done((bf16[512,768]{1,0:T(8,128)(2,1)S(1)}, bf16[512,768]{1,0:T(8,128)(2,1)}, u32[]{:S(2)}, u32[]{:S(2)}) %collective-permute-start.27) | collective-permute-done | bytes 786464 | tf_op jit(solution)/shard_map/ppermute | solution.py:93
  513.3 12.7 %project_back.1 = (bf16[256,6144]{1,0:T(8,128)(2,1)}, bf16[256,6144]{1,0:T(8,128)(2,1)}) custom-call(bf16[512,768]{1,0:T(8,128)(2,1)} %get-tuple-element.148.refs_0_, bf16[512,768]{1,0:T(8,128)(2,1)} %collective-permute-done.26.refs_1_, bf16[512,768]{1,0:T(8,128)(2,1)} %collective-permute-done.27.refs_2_, bf16[512,768]{1,0:T(8,128)(2,1)} %copy-done.17, ...), custom_call_target="tpu_custom_call" | custom-call | tf_op jit(solution)/shard_map/project_back/pallas_call | solution.py:559
  526.1 7.0 add_convert_fusion
  537.4 7.1 fusion.58
  549.0 6.6 add_in_slots.3
  579.5 22.1 %backward_streams.1 = (bf16[1024,2048]{1,0:T(8,128)(2,1)}, f32[4,2048]{1,0:T(4,128)}, f32[2048,128]{1,0:T(8,128)}, f32[128,128]{1,0:T(8,128)}, f32[1,128]{1,0:T(1,128)}) custom-call(s32[1]{0:T(128)} %bitcast.refs_0_, s32[4]{0:T(128)} %pad_add_fusion.order.refs_1_, bf16[256,2048]{1,0:T(8,128)(2,1)} %dynamic-slice_select_fusion.3.refs_2_, ...), custom_call_target="tpu_custom_call" | custom-call | flops 83886080 | bytes 20971520 | tf_op jit(solution)/shard_map/backward_streams/pallas_call | solution.py:312
  653.3 7.6 %all-to-all-done.3 = bf16[4,256,2048]{2,1,0:T(8,128)(2,1)} async-done(((bf16[4,256,2048]{2,1,0:T(8,128)(2,1)}), bf16[4,256,2048]{2,1,0:T(8,128)(2,1)}, u32[]{:S(2)}, u32[]{:S(2)}) %all-to-all-start.3) | async-done | bytes 4194336 | tf_op jit(solution)/shard_map/all_to_all | solution.py:924
  706.7 10.8 %collective-permute-done.51.refs_2_ = bf16[128,1024]{1,0:T(8,128)(2,1)S(1)} collective-permute-done((bf16[128,1024]{1,0:T(8,128)(2,1)S(1)}, bf16[128,1024]{1,0:T(8,128)(2,1)S(1)}, u32[]{:S(2)}, u32[]{:S(2)}) %collective-permute-start.51) | collective-permute-done | bytes 262176 | tf_op jit(solution)/shard_map/ppermute | solution.py:113
  737.9 7.0 interleave.1
  (333 shorter events, 260.3 us)
Async XLA Ops:
  7.2 247.4 %all-gather.6.cloned.1.call-start = ((), (), s32[]{:S(2)}) async-start(), calls=%async_computation.8 | async-start | bytes 5242880 | tf_op jit(solution)/shard_map/all_gather | solution.py:775
  35.0 254.1 %all-gather.4.cloned.1.call-start = ((), (), s32[]{:S(2)}) async-start(), calls=%async_computation.7 | async-start | bytes 5242880 | tf_op jit(solution)/shard_map/all_gather | solution.py:779
  39.2 26.1 %collective-permute-start.3 = (bf16[512,2048]{1,0:T(8,128)(2,1)S(1)}, bf16[512,2048]{1,0:T(8,128)(2,1)S(1)}, u32[]{:S(2)}, u32[]{:S(2)}) collective-permute-start(bf16[512,2048]{1,0:T(8,128)(2,1)S(1)} %bitcast.115), channel_id=1, source_target_pairs={{0,2},{1,5},{2,0},{3,7},{4,6},{5,1},{6,4},{7,3},{8,10},{9,13},{10,... | collective-permute-start | bytes 6291464 | tf_op jit(solution)/shard_map/ppermute | solution.py:61
  66.6 26.4 %collective-permute-start.4 = (bf16[512,2048]{1,0:T(8,128)(2,1)}, bf16[512,2048]{1,0:T(8,128)(2,1)}, u32[]{:S(2)}, u32[]{:S(2)}) collective-permute-start(bf16[512,2048]{1,0:T(8,128)(2,1)} %bitcast.2.refs_1_), channel_id=1, source_target_pairs={{0,2},{1,5},{2,0},{3,7},{4,6},{5,1},{6,4},{7,3},{8,10},{9,13},{10,... | collective-permute-start | bytes 6291464 | tf_op jit(solution)/shard_map/ppermute | solution.py:61
  109.7 35.8 %collective-permute-start.10 = (bf16[512,2048]{1,0:T(8,128)(2,1)S(1)}, bf16[512,2048]{1,0:T(8,128)(2,1)}, u32[]{:S(2)}, u32[]{:S(2)}) collective-permute-start(bf16[512,2048]{1,0:T(8,128)(2,1)S(1)} %bitcast.116), channel_id=1, source_target_pairs={{0,4},{1,3},{2,6},{3,1},{4,0},{5,7},{6,2},{7,5},{8,12},{9,11},{10,... | collective-permute-start | bytes 6291464 | tf_op jit(solution)/shard_map/ppermute | solution.py:61
  111.0 57.0 %collective-permute-start.11 = (bf16[512,2048]{1,0:T(8,128)(2,1)}, bf16[512,2048]{1,0:T(8,128)(2,1)}, u32[]{:S(2)}, u32[]{:S(2)}) collective-permute-start(bf16[512,2048]{1,0:T(8,128)(2,1)} %copy-done.10), channel_id=1, source_target_pairs={{0,4},{1,3},{2,6},{3,1},{4,0},{5,7},{6,2},{7,5},{8,12},{9,11},{10,... | collective-permute-start | bytes 6291464 | tf_op jit(solution)/shard_map/ppermute | solution.py:61
  113.2 112.4 %collective-permute-start.5 = (bf16[512,2048]{1,0:T(8,128)(2,1)}, bf16[512,2048]{1,0:T(8,128)(2,1)}, u32[]{:S(2)}, u32[]{:S(2)}) collective-permute-start(bf16[512,2048]{1,0:T(8,128)(2,1)} %bitcast.2.refs_1_), channel_id=1, source_target_pairs={{0,4},{1,3},{2,6},{3,1},{4,0},{5,7},{6,2},{7,5},{8,12},{9,11},{10,... | collective-permute-start | bytes 6291464 | tf_op jit(solution)/shard_map/ppermute | solution.py:61
  114.6 111.1 %collective-permute-start.6 = (bf16[512,2048]{1,0:T(8,128)(2,1)}, bf16[512,2048]{1,0:T(8,128)(2,1)}, u32[]{:S(2)}, u32[]{:S(2)}) collective-permute-start(bf16[512,2048]{1,0:T(8,128)(2,1)} %collective-permute-done.4.refs_2_), channel_id=1, source_target_pairs={{0,4},{1,3},{2,6},{3,1},{4,0},{5,7},{6,2},{7,5},{8,12},{9,11},{10,... | collective-permute-start | bytes 6291464 | tf_op jit(solution)/shard_map/ppermute | solution.py:61
  118.5 73.9 %collective-permute-start.12 = (bf16[256,2048]{1,0:T(8,128)(2,1)S(1)}, bf16[256,2048]{1,0:T(8,128)(2,1)}, u32[]{:S(2)}, u32[]{:S(2)}) collective-permute-start(bf16[256,2048]{1,0:T(8,128)(2,1)S(1)} %get-tuple-element.116), channel_id=1, source_target_pairs={{0,2},{1,5},{2,0},{3,7},{4,6},{5,1},{6,4},{7,3},{8,10},{9,13},{10,... | collective-permute-start | bytes 3145736 | tf_op jit(solution)/shard_map/ppermute | solution.py:61
  186.9 37.2 %all-to-all-start.2 = ((bf16[128,4,1024]{0,2,1:T(8,128)(2,1)}), bf16[128,4,1024]{0,2,1:T(8,128)(2,1)S(1)}, u32[]{:S(2)}, u32[]{:S(2)}) async-start(bf16[128,4,1024]{0,2,1:T(8,128)(2,1)} %bitcast.40), calls=%async_computation.2 | async-start | bytes 2097152 | tf_op jit(solution)/shard_map/all_to_all | solution.py:772
  190.4 141.9 %all-gather.8.cloned.1.call-start = ((), (), s32[]{:S(2)}) async-start(), calls=%async_computation.9 | async-start | bytes 5242880 | tf_op jit(solution)/shard_map/all_gather | solution.py:809
  190.5 60.2 %collective-permute-start.13 = (bf16[256,2048]{1,0:T(8,128)(2,1)S(1)}, bf16[256,2048]{1,0:T(8,128)(2,1)S(1)}, u32[]{:S(2)}, u32[]{:S(2)}) collective-permute-start(bf16[256,2048]{1,0:T(8,128)(2,1)S(1)} %get-tuple-element.116), channel_id=1, source_target_pairs={{0,4},{1,3},{2,6},{3,1},{4,0},{5,7},{6,2},{7,5},{8,12},{9,11},{10,... | collective-permute-start | bytes 3145736 | tf_op jit(solution)/shard_map/ppermute | solution.py:61
  192.4 59.3 %collective-permute-start.14 = (bf16[256,2048]{1,0:T(8,128)(2,1)}, bf16[256,2048]{1,0:T(8,128)(2,1)}, u32[]{:S(2)}, u32[]{:S(2)}) collective-permute-start(bf16[256,2048]{1,0:T(8,128)(2,1)} %collective-permute-done.12), channel_id=1, source_target_pairs={{0,4},{1,3},{2,6},{3,1},{4,0},{5,7},{6,2},{7,5},{8,12},{9,11},{10,... | collective-permute-start | bytes 3145736 | tf_op jit(solution)/shard_map/ppermute | solution.py:61
  225.4 247.2 %reduce-scatter.4.cloned.1.call-start = ((), (), s32[]{:S(2)}) async-start(), calls=%async_computation.10 | async-start | bytes 5242880 | tf_op jit(solution)/shard_map/reduce_scatter | solution.py:838
  288.6 286.2 %reduce-scatter.6.cloned.1.call-start = ((), (), s32[]{:S(2)}) async-start(), calls=%async_computation.11 | async-start | bytes 5242880 | tf_op jit(solution)/shard_map/reduce_scatter | solution.py:840
  331.4 29.3 %collective-permute-start.15 = (bf16[1024,2048]{1,0:T(8,128)(2,1)}, bf16[1024,2048]{1,0:T(8,128)(2,1)}, u32[]{:S(2)}, u32[]{:S(2)}) collective-permute-start(bf16[1024,2048]{1,0:T(8,128)(2,1)} %get-tuple-element.120.refs_0_), channel_id=1, source_target_pairs={{0,1},{1,0},{2,3},{3,2},{4,5},{5,4},{6,7},{7,6},{8,9},{9,8},{10,11... | collective-permute-start | bytes 12582920 | tf_op jit(solution)/shard_map/ppermute | solution.py:124
  331.8 30.2 %collective-permute-start.16 = (bf16[1024,2048]{1,0:T(8,128)(2,1)}, bf16[1024,2048]{1,0:T(8,128)(2,1)}, u32[]{:S(2)}, u32[]{:S(2)}) collective-permute-start(bf16[1024,2048]{1,0:T(8,128)(2,1)} %get-tuple-element.121.refs_1_.refs_4_), channel_id=1, source_target_pairs={{0,1},{1,0},{2,3},{3,2},{4,5},{5,4},{6,7},{7,6},{8,9},{9,8},{10,11... | collective-permute-start | bytes 12582920 | tf_op jit(solution)/shard_map/ppermute | solution.py:124
  331.9 30.1 %collective-permute-start.17 = (bf16[1024,2048]{1,0:T(8,128)(2,1)}, bf16[1024,2048]{1,0:T(8,128)(2,1)}, u32[]{:S(2)}, u32[]{:S(2)}) collective-permute-start(bf16[1024,2048]{1,0:T(8,128)(2,1)} %get-tuple-element.122.refs_2_.refs_8_), channel_id=1, source_target_pairs={{0,1},{1,0},{2,3},{3,2},{4,5},{5,4},{6,7},{7,6},{8,9},{9,8},{10,11... | collective-permute-start | bytes 12582920 | tf_op jit(solution)/shard_map/ppermute | solution.py:124
  334.5 54.1 %collective-permute-start.23 = (bf16[2048,768]{1,0:T(8,128)(2,1)S(1)}, bf16[2048,768]{1,0:T(8,128)(2,1)}, u32[]{:S(2)}, u32[]{:S(2)}) collective-permute-start(bf16[2048,768]{1,0:T(8,128)(2,1)S(1)} %slice.243.refs_4_), channel_id=1, source_target_pairs={{0,2},{1,5},{2,0},{3,7},{4,6},{5,1},{6,4},{7,3},{8,10},{9,13},{10,... | collective-permute-start | bytes 9437192 | tf_op jit(solution)/shard_map/ppermute | solution.py:61
  352.2 41.3 %collective-permute-start.21 = (bf16[512,2048]{1,0:T(8,128)(2,1)}, bf16[512,2048]{1,0:T(8,128)(2,1)}, u32[]{:S(2)}, u32[]{:S(2)}) collective-permute-start(bf16[512,2048]{1,0:T(8,128)(2,1)} %get-tuple-element.142), channel_id=1, source_target_pairs={{0,4},{1,3},{2,6},{3,1},{4,0},{5,7},{6,2},{7,5},{8,12},{9,11},{10,... | collective-permute-start | bytes 6291464 | tf_op jit(solution)/shard_map/ppermute | solution.py:61
  360.7 292.6 %reduce-scatter.8.cloned.1.call-start = ((), (), s32[]{:S(2)}) async-start(), calls=%async_computation.12 | async-start | bytes 5242880 | tf_op jit(solution)/shard_map/reduce_scatter | solution.py:871
  360.8 110.0 %collective-permute-start.24 = (bf16[2048,768]{1,0:T(8,128)(2,1)S(1)}, bf16[2048,768]{1,0:T(8,128)(2,1)S(1)}, u32[]{:S(2)}, u32[]{:S(2)}) collective-permute-start(bf16[2048,768]{1,0:T(8,128)(2,1)S(1)} %slice.243.refs_4_), channel_id=1, source_target_pairs={{0,4},{1,3},{2,6},{3,1},{4,0},{5,7},{6,2},{7,5},{8,12},{9,11},{10,... | collective-permute-start | bytes 9437192 | tf_op jit(solution)/shard_map/ppermute | solution.py:61
  388.7 83.9 %collective-permute-start.25 = (bf16[2048,768]{1,0:T(8,128)(2,1)}, bf16[2048,768]{1,0:T(8,128)(2,1)}, u32[]{:S(2)}, u32[]{:S(2)}) collective-permute-start(bf16[2048,768]{1,0:T(8,128)(2,1)} %collective-permute-done.23.refs_5_), channel_id=1, source_target_pairs={{0,4},{1,3},{2,6},{3,1},{4,0},{5,7},{6,2},{7,5},{8,12},{9,11},{10,... | collective-permute-start | bytes 9437192 | tf_op jit(solution)/shard_map/ppermute | solution.py:61
  397.6 75.0 %collective-permute-start.22 = (bf16[256,2048]{1,0:T(8,128)(2,1)S(1)}, bf16[256,2048]{1,0:T(8,128)(2,1)}, u32[]{:S(2)}, u32[]{:S(2)}) collective-permute-start(bf16[256,2048]{1,0:T(8,128)(2,1)S(1)} %get-tuple-element.264), channel_id=1, source_target_pairs={{0,2},{1,5},{2,0},{3,7},{4,6},{5,1},{6,4},{7,3},{8,10},{9,13},{10,... | collective-permute-start | bytes 3145736 | tf_op jit(solution)/shard_map/ppermute | solution.py:61
  476.9 36.4 %collective-permute-start.27 = (bf16[512,768]{1,0:T(8,128)(2,1)S(1)}, bf16[512,768]{1,0:T(8,128)(2,1)}, u32[]{:S(2)}, u32[]{:S(2)}) collective-permute-start(bf16[512,768]{1,0:T(8,128)(2,1)S(1)} %get-tuple-element.253), channel_id=1, source_target_pairs={{0,4},{1,3},{2,6},{3,1},{4,0},{5,7},{6,2},{7,5},{8,12},{9,11},{10,... | collective-permute-start | bytes 2359304 | tf_op jit(solution)/shard_map/ppermute | solution.py:93
  477.9 35.4 %collective-permute-start.26 = (bf16[512,768]{1,0:T(8,128)(2,1)S(1)}, bf16[512,768]{1,0:T(8,128)(2,1)}, u32[]{:S(2)}, u32[]{:S(2)}) collective-permute-start(bf16[512,768]{1,0:T(8,128)(2,1)S(1)} %get-tuple-element.254), channel_id=1, source_target_pairs={{0,2},{1,5},{2,0},{3,7},{4,6},{5,1},{6,4},{7,3},{8,10},{9,13},{10,... | collective-permute-start | bytes 2359304 | tf_op jit(solution)/shard_map/ppermute | solution.py:93
  537.3 40.6 %collective-permute-start.29 = (bf16[256,6144]{1,0:T(8,128)(2,1)}, bf16[256,6144]{1,0:T(8,128)(2,1)S(1)}, u32[]{:S(2)}, u32[]{:S(2)}) collective-permute-start(bf16[256,6144]{1,0:T(8,128)(2,1)} %get-tuple-element.154), channel_id=1, source_target_pairs={{0,1},{1,0},{2,3},{3,2},{4,5},{5,4},{6,7},{7,6},{8,9},{9,8},{10,11... | collective-permute-start | bytes 9437192 | tf_op jit(solution)/shard_map/ppermute | solution.py:124
  555.6 46.9 %collective-permute-start.31 = (bf16[512,2048]{1,0:T(8,128)(2,1)}, bf16[512,2048]{1,0:T(8,128)(2,1)}, u32[]{:S(2)}, u32[]{:S(2)}) collective-permute-start(bf16[512,2048]{1,0:T(8,128)(2,1)} %get-tuple-element.160), channel_id=1, source_target_pairs={{0,4},{1,3},{2,6},{3,1},{4,0},{5,7},{6,2},{7,5},{8,12},{9,11},{10,... | collective-permute-start | bytes 6291464 | tf_op jit(solution)/shard_map/ppermute | solution.py:61
  607.0 53.9 %all-to-all-start.3 = ((bf16[4,256,2048]{2,1,0:T(8,128)(2,1)}), bf16[4,256,2048]{2,1,0:T(8,128)(2,1)}, u32[]{:S(2)}, u32[]{:S(2)}) async-start(bf16[4,256,2048]{2,1,0:T(8,128)(2,1)} %bitcast.125), calls=%async_computation.5 | async-start | bytes 8388608 | tf_op jit(solution)/shard_map/all_to_all | solution.py:924
  660.9 77.0 %collective-permute-start.42 = (bf16[1024,2048]{1,0:T(8,128)(2,1)}, bf16[1024,2048]{1,0:T(8,128)(2,1)}, u32[]{:S(2)}, u32[]{:S(2)}) collective-permute-start(bf16[1024,2048]{1,0:T(8,128)(2,1)} %bitcast.49.own_ref), channel_id=1, source_target_pairs={{0,1},{1,0},{2,3},{3,2},{4,5},{5,4},{6,7},{7,6},{8,9},{9,8},{10,11... | collective-permute-start | bytes 12582920 | tf_op jit(solution)/shard_map/ppermute | solution.py:124
  674.2 25.9 %collective-permute-start.33 = (bf16[256,2048]{1,0:T(8,128)(2,1)S(1)}, bf16[256,2048]{1,0:T(8,128)(2,1)S(1)}, u32[]{:S(2)}, u32[]{:S(2)}) collective-permute-start(bf16[256,2048]{1,0:T(8,128)(2,1)S(1)} %add_convert_fusion.4), channel_id=1, source_target_pairs={{0,1},{1,0},{2,3},{3,2},{4,5},{5,4},{6,7},{7,6},{8,9},{9,8},{10,11... | collective-permute-start | bytes 3145736 | tf_op jit(solution)/shard_map/ppermute | solution.py:124
  700.1 23.3 %collective-permute-start.55 = (bf16[128,2048]{1,0:T(8,128)(2,1)S(1)}, bf16[128,2048]{1,0:T(8,128)(2,1)S(1)}, u32[]{:S(2)}, u32[]{:S(2)}) collective-permute-start(bf16[128,2048]{1,0:T(8,128)(2,1)S(1)} %get-tuple-element.256), channel_id=1, source_target_pairs={{0,6},{2,4},{4,2},{6,0},{1,7},{3,5},{5,3},{7,1},{8,14},{10,12},{12... | collective-permute-start | bytes 1572872 | tf_op jit(solution)/shard_map/ppermute | solution.py:113
  (70 other events, 1145.7 us)
Sparse Core Ops, SparseCore 0:
  35.1 80.7 all-gather.5
  117.5 79.2 all-gather.3
  225.5 80.5 all-gather.7
  308.3 75.2 reduce-scatter.3
  385.8 77.2 reduce-scatter.5
  533.3 77.3 reduce-scatter.7

commit v4 on v3

--- a/solution.py
+++ b/solution.py
@@ -365,127 +365,129 @@
 def attention_kernel(count, half, heads, which, *refs):
     near, far, (cos_ref, right_ref, left_ref) = refs[:4], refs[4:8], refs[8:11]
     o_ref, dq_ref, dk_ref, dv_ref, all_ref = refs[11:16]
-    q_s, k_s, v_s, g_s, dk_s, dv_s, p_s, o_s, dq_s, top_s, sum_s = refs[16:]
+    q_s, k_s, v_s, g_s, k_t, v_t, g_t, dk_s, dv_s, p_s, o_s, dq_s = refs[16:]
     piece = heads * HD
-    blocks = 2 * count
+    block = 2 * half
     scale = HD ** (-0.5)
     bf16, f32 = jnp.bfloat16, jnp.float32
     m = which[0]
 
-    def at(b):
-        return pl.ds(pl.multiple_of(((lax.rem(b, 2) ^ m) * count + lax.div(b, 2)) * half, half), half)
-
-    def by_owner(a, side):
-        return pl.ds(pl.multiple_of((2 * a + side) * half, half), half)
-
     def cols(n):
         return slice(n * HD, (n + 1) * HD)
 
+    def part(b):
+        return pl.ds(pl.multiple_of(b * half, half), half)
+
+    def span(j):
+        return pl.ds(pl.multiple_of(j * block, block), block)
+
+    def turned(value, here, sign):
+        return turn(value, cos_ref[here, :], right_ref[here, :], left_ref[here, :], sign)
+
     for side, (q_ref, k_ref, v_ref, g_ref) in enumerate((near, far)):
 
         def prepare(a, carry, side=side, q_ref=q_ref, k_ref=k_ref, v_ref=v_ref, g_ref=g_ref):
-            rows = pl.ds(pl.multiple_of(a * half, half), half)
-            here = pl.ds(pl.multiple_of((side * count + a) * half, half), half)
+            rows, here, there = part(a), part(side * count + a), part(2 * a + (side ^ m))
             for n in range(heads):
-                for given, kept in ((q_ref, q_s), (k_ref, k_s)):
-                    kept[here, cols(n)] = turn(
-                        given[rows, cols(n)], cos_ref[here, :], right_ref[here, :], left_ref[here, :], 1.0
-                    ).astype(bf16)
-            v_s[here, :] = v_ref[rows, :]
-            g_s[here, :] = g_ref[rows, :]
-            dk_s[here, :] = jnp.zeros((half, heads * HD), f32)
-            dv_s[here, :] = jnp.zeros((half, heads * HD), f32)
+                q_s[there, cols(n)] = turned(q_ref[rows, cols(n)], here, 1.0).astype(bf16)
+                keys = turned(k_ref[rows, cols(n)], here, 1.0)
+                k_s[there, cols(n)] = keys.astype(bf16)
+                k_t[cols(n), there] = keys.T.astype(bf16)
+                v_t[cols(n), there] = v_ref[rows, cols(n)].astype(f32).T.astype(bf16)
+                g_t[cols(n), there] = g_ref[rows, cols(n)].astype(f32).T.astype(bf16)
+            v_s[there, :] = v_ref[rows, :]
+            g_s[there, :] = g_ref[rows, :]
+            dk_s[there, :] = jnp.zeros((half, piece), f32)
+            dv_s[there, :] = jnp.zeros((half, piece), f32)
             return carry
 
         lax.fori_loop(0, count, prepare, 0)
-    later = lax.broadcasted_iota(jnp.int32, (half, half), 1) > lax.broadcasted_iota(jnp.int32, (half, half), 0)
-
-    def lanes(value, op):
-        parts = [value[:, i : i + LANES] for i in range(0, value.shape[1], LANES)]
-        out = parts[0]
-        for part in parts[1:]:
-            out = op(out, part)
+    later = lax.broadcasted_iota(jnp.int32, (block, block), 0) > lax.broadcasted_iota(jnp.int32, (block, block), 1)
+
+    def rows_of_eight(value, op):
+        out = value[:8]
+        for at in range(8, value.shape[0], 8):
+            out = op(out, value[at : at + 8])
         return out
 
     def query_block(i, carry):
-        here = at(i)
+        here = span(i)
         queries = [q_s[here, cols(n)] for n in range(heads)]
         grads = [g_s[here, cols(n)] for n in range(heads)]
 
-        def scores(j, last):
-            there = at(j)
+        def scores(j, tops, last=False):
+            there = span(j)
+            out = []
             for n in range(heads):
-                s = dot(queries[n], k_s[there, cols(n)], (1, 1)) * scale
+                s = dot(k_s[there, cols(n)], queries[n], (1, 1)) * (scale * 1.4426950408889634)
                 if last:
                     s = jnp.where(later, -1e30, s)
-                p_s[n, :, pl.ds(pl.multiple_of(j * half, half), half)] = s
-                top = lanes(s, jnp.maximum)
-                top_s[n] = jnp.maximum(top_s[n], top)
-
-        top_s[...] = jnp.full(top_s.shape, -1e30, f32)
-        lax.fori_loop(0, i, lambda j, c: (scores(j, False), c)[1], 0)
-        scores(i, True)
-        tops = [jnp.max(top_s[n], -1, keepdims=True) for n in range(heads)]
+                p_s[n, there, :] = s
+                out.append(jnp.maximum(tops[n], rows_of_eight(s, jnp.maximum)))
+            return tuple(out)
+
+        tops = lax.fori_loop(0, i, scores, tuple(jnp.full((8, block), -1e30, f32) for _ in range(heads)))
+        tops = [jnp.max(x, 0, keepdims=True) for x in scores(i, tops, True)]
         o_s[...] = jnp.zeros(o_s.shape, f32)
         dq_s[...] = jnp.zeros(dq_s.shape, f32)
-        sum_s[...] = jnp.zeros(sum_s.shape, f32)
-
-        def mixing(j, c):
-            there = at(j)
-            spot = pl.ds(pl.multiple_of(j * half, half), half)
+
+        def mixing(j, sums):
+            there = span(j)
+            out = []
             for n in range(heads):
-                p = jnp.exp(p_s[n, :, spot] - tops[n])
-                p_s[n, :, spot] = p
-                sum_s[n] += lanes(p, jnp.add)
-                o_s[n] += dot(p.astype(bf16), v_s[there, cols(n)], (1, 0))
-            return c
-
-        lax.fori_loop(0, i + 1, mixing, 0)
+                p = jnp.exp2(p_s[n, there, :] - tops[n])
+                p_s[n, there, :] = p
+                out.append(sums[n] + rows_of_eight(p, jnp.add))
+                o_s[n] += dot(v_t[cols(n), there], p.astype(bf16), (1, 0))
+            return tuple(out)
+
+        sums = lax.fori_loop(0, i + 1, mixing, tuple(jnp.zeros((8, block), f32) for _ in range(heads)))
         shares, deltas = [], []
         for n in range(heads):
-            share = 1.0 / jnp.sum(sum_s[n], -1, keepdims=True)
+            share = 1.0 / jnp.sum(sums[n], 0, keepdims=True)
             found = o_s[n] * share
-            o_ref[here, cols(n)] = found.astype(bf16)
+            deltas.append(jnp.sum(found * g_t[cols(n), here].astype(f32), 0, keepdims=True))
+            found = found.T.astype(bf16)
+            for b in range(2):
+                o_ref[part((b ^ m) * count + i), cols(n)] = found[b * half : (b + 1) * half]
             shares.append(share)
-            deltas.append(jnp.sum(found * grads[n].astype(f32), -1, keepdims=True))
 
         def back(j, c):
-            there = at(j)
-            spot = pl.ds(pl.multiple_of(j * half, half), half)
+            there = span(j)
             for n in range(heads):
-                p = p_s[n, :, spot] * shares[n]
-                dp = dot(grads[n], v_s[there, cols(n)], (1, 1))
+                p = p_s[n, there, :] * shares[n]
+                dp = dot(v_s[there, cols(n)], grads[n], (1, 1))
                 ds = (p * (dp - deltas[n])).astype(bf16)
-                dq_s[n] += dot(ds, k_s[there, cols(n)], (1, 0))
-                dk_s[there, cols(n)] += dot(ds, queries[n], (0, 0))
-                dv_s[there, cols(n)] += dot(p.astype(bf16), grads[n], (0, 0))
+                dq_s[n] += dot(k_t[cols(n), there], ds, (1, 0))
+                dk_s[there, cols(n)] += dot(ds, queries[n], (1, 0))
+                dv_s[there, cols(n)] += dot(p.astype(bf16), grads[n], (1, 0))
             return c
 
         lax.fori_loop(0, i + 1, back, 0)
-        place = by_owner(lax.div(i, 2), lax.rem(i, 2) ^ m)
         for n in range(heads):
-            found = turn(dq_s[n] * scale, cos_ref[here, :], right_ref[here, :], left_ref[here, :], -1.0).astype(bf16)
-            dq_ref[here, cols(n)] = found
-            all_ref[place, cols(n)] = found
+            found = dq_s[n].T * scale
+            for b in range(2):
+                rows = part((b ^ m) * count + i)
+                value = turned(found[b * half : (b + 1) * half], rows, -1.0).astype(bf16)
+                dq_ref[rows, cols(n)] = value
+                all_ref[part(2 * i + (b ^ m)), cols(n)] = value
         return carry
 
-    lax.fori_loop(0, blocks, query_block, 0)
-
-    def finish(b, carry):
-        rows = pl.ds(pl.multiple_of(b * half, half), half)
-        place = by_owner(lax.rem(b, count), lax.div(b, count))
-        for n in range(heads):
-            found = turn(
-                dk_s[rows, cols(n)] * scale, cos_ref[rows, :], right_ref[rows, :], left_ref[rows, :], -1.0
-            ).astype(bf16)
-            dk_ref[rows, cols(n)] = found
-            all_ref[place, cols(heads + n)] = found
-        found = dv_s[rows, :].astype(bf16)
-        dv_ref[rows, :] = found
-        all_ref[place, 2 * piece : 3 * piece] = found
-        return carry
-
-    lax.fori_loop(0, blocks, finish, 0)
+    lax.fori_loop(0, count, query_block, 0)
+    for side in range(2):
+
+        def finish(a, carry, side=side):
+            here, there, place = part(side * count + a), part(2 * a + (side ^ m)), part(2 * a + side)
+            for n in range(heads):
+                found = turned(dk_s[there, cols(n)] * scale, here, -1.0).astype(bf16)
+                dk_ref[here, cols(n)] = found
+                all_ref[place, cols(heads + n)] = found
+            found = dv_s[there, :].astype(bf16)
+            dv_ref[here, :] = found
+            all_ref[place, 2 * piece : 3 * piece] = found
+            return carry
+
+        lax.fori_loop(0, count, finish, 0)
 
 
 def attention(near, far, positions, which, count):
@@ -500,18 +502,17 @@
         out_specs=[vmem] * 5,
         out_shape=[out] * 4 + [jax.ShapeDtypeStruct((rows, 3 * piece), jnp.bfloat16)],
         scratch_shapes=[pltpu.VMEM((rows, piece), jnp.bfloat16)] * 4
+        + [pltpu.VMEM((piece, rows), jnp.bfloat16)] * 3
         + [
             wide(rows, piece),
             wide(rows, piece),
-            wide(heads, half, rows),
-            wide(heads, half, HD),
-            wide(heads, half, HD),
-            wide(heads, half, LANES),
-            wide(heads, half, LANES),
+            wide(heads, rows, 2 * half),
+            wide(heads, HD, 2 * half),
+            wide(heads, HD, 2 * half),
         ],
         compiler_params=pltpu.CompilerParams(vmem_limit_bytes=VMEM),
         cost_estimate=pl.CostEstimate(
-            flops=40 * rows * rows * piece, bytes_accessed=rows * piece * 20, transcendentals=rows * rows * heads // 2
+            flops=18 * rows * rows * piece, bytes_accessed=rows * piece * 20, transcendentals=rows * rows * heads // 2
         ),
         name="attention",
     )(which, *near, *far, *rope_tables(positions))
@@ -521,7 +522,7 @@
     rows, width = streams[0].shape
     count = len(streams)
     piece = weights.shape[1] // count
-    tile = min(256, rows)
+    tile = min(512, rows)
 
     def kernel(*refs):
         for c in range(count):
@@ -571,7 +572,7 @@
 def add_in_slots(near, far, order, count):
     rows, width = near.shape
     block = rows // count
-    tile = min(128, block)
+    tile = min(256, block)
     steps = block // tile
     side = count // 2
 
@@ -601,7 +602,7 @@
     pieces = len(groups[0][0])
     rows = min(a.shape[0] for a, _ in groups[0][0])
     width = groups[0][0][0][0].shape[1]
-    tile = min(256, width)
+    tile = min(512, width)
     sizes = [right[0][0].shape[1] for _, right in groups]
     specs, arrays = [], []
     for left, right in groups:
@@ -689,35 +690,29 @@
     )(m, own, sibling)
 
 
-def place_wide(entries, h, out_type, pieces, turned):
-    count = len(entries)
-    depth, cols = entries[0].shape
+def place_wide(blocks, count, pieces, turned):
+    depth, cols = blocks.shape[0] // count, blocks.shape[1]
     size = cols // pieces
 
-    def kernel(which, *refs):
-        a = pl.program_id(0)
-        for r in range(count):
-
-            @pl.when((which[0] ^ a) == r)
-            def _(r=r):
-                for i in range(pieces):
-                    block = refs[r][:, i * size : (i + 1) * size].astype(jnp.float32)
-                    refs[count + i][...] = block.T if turned[i] else block
+    def kernel(*refs):
+        for i in range(pieces):
+            block = refs[0][:, i * size : (i + 1) * size].astype(jnp.float32)
+            refs[1 + i][...] = block.T if turned[i] else block
 
     return pl.pallas_call(
         kernel,
         grid=(count,),
-        in_specs=[pl.BlockSpec(memory_space=pltpu.SMEM)] + [pl.BlockSpec((depth, cols), lambda a: (0, 0))] * count,
+        in_specs=[pl.BlockSpec((depth, cols), lambda a: (a, 0))],
         out_specs=[
             pl.BlockSpec((size, depth), lambda a: (a, 0)) if t else pl.BlockSpec((depth, size), lambda a: (0, a))
             for t in turned
         ],
         out_shape=[
-            jax.ShapeDtypeStruct((count * size, depth) if t else (depth, count * size), out_type) for t in turned
+            jax.ShapeDtypeStruct((count * size, depth) if t else (depth, count * size), jnp.float32) for t in turned
         ],
         compiler_params=pltpu.CompilerParams(vmem_limit_bytes=VMEM),
         name="place_wide",
-    )(h, *entries)
+    )(blocks)
 
 
 def after(value, *others):
@@ -775,8 +770,13 @@
     up_full = lax.all_gather(up_mine, "dp", axis=0, tiled=True)
     for g in range(1, parts):
         slots.append(plane.gather(after(own_rows[g], slots[-1][1])))
-    down_mine = swap_columns(after(down_weight.T, up_mine, gain, slots[-1][1]))
-    down_full = lax.all_gather(down_mine, "dp", axis=0, tiled=True)
+    packed = jnp.stack([query_weight, key_weight, value_weight, out_weight.T], 0)
+    packed = packed.reshape(4, depth, count, -1).transpose(1, 2, 0, 3).reshape(depth, -1)
+    narrow_mine = swap_columns(after(packed, up_mine, gain, slots[-1][1]))
+    narrow_full = lax.all_gather(narrow_mine, "dp", axis=0, tiled=True)
+    piece = narrow_full.shape[1] // 4
+    out_full = narrow_full[:, 3 * piece :]
+
     layer_of = [h ^ plane.place(j) for j in range(count)]
     order = jnp.stack(layer_of).astype(jnp.int32)
     pick = sum(jnp.where(layer_of[j] == count - 1, j, 0) for j in range(count)).astype(jnp.int32).reshape(1)
@@ -802,13 +802,9 @@
     for g in range(parts):
         found = forward_streams(slots[g], g, parts, found, pick, in_wide, out_wide, bias_wide, gain)
         if g == 0:
-            packed = jnp.stack([query_weight, key_weight, value_weight, out_weight.T], 0)
-            packed = packed.reshape(4, depth, count, -1).transpose(1, 2, 0, 3).reshape(depth, -1)
-            packed, *found = lax.optimization_barrier((packed, *found))
-    narrow_mine = swap_columns(packed)
-    narrow_full = lax.all_gather(narrow_mine, "dp", axis=0, tiled=True)
-    piece = narrow_full.shape[1] // 4
-    out_full = narrow_full[:, 3 * piece :]
+            down_turned, *found = lax.optimization_barrier((down_weight.T, *found))
+    down_mine = swap_columns(down_turned)
+    down_full = lax.all_gather(down_mine, "dp", axis=0, tiled=True)
     all_weights = plane.gather(narrow_full[:, : 3 * piece])
     near_streams, (mixes, pres, stats) = list(found[:STREAMS]), found[STREAMS:]
     far_streams = [None] * STREAMS
@@ -836,11 +832,25 @@
     grads = both(near_grad, far_grad)
     down_part = outer([(grads, both(near_hidden, far_hidden))])
     down_sum = lax.psum_scatter(down_part, "dp", scatter_dimension=0, tiled=True)
+    near_back, far_back, all_weights[1], *far_streams = lax.optimization_barrier(
+        (near_back, far_back, all_weights[1], *far_streams)
+    )
     up_part = outer([(both(near_streams[3], far_streams[3]), both(near_back, far_back))])
     up_sum = lax.psum_scatter(up_part, "dp", scatter_dimension=0, tiled=True)
 
-    near_given, far_given, _, _ = lax.optimization_barrier(
-        (near_streams[:3] + [near_grad], far_streams[:3] + [far_grad], up_part, down_part)
+    own_mix = lax.dynamic_slice_in_dim(mixes, h * half, half, 0)[:, :pairs].reshape(half, STREAMS, count)
+
+    def own_block(j):
+        found = lax.dynamic_slice_in_dim(slots[0][j], h % per * half, half, 0)
+        for g in range(1, parts):
+            found = jnp.where(h // per == g, lax.dynamic_slice_in_dim(slots[g][j], h % per * half, half, 0), found)
+        return found
+
+    own_layers = [own_block(j) for j in range(count)]
+    own_part = lambda x: lax.dynamic_slice_in_dim(x, h * half, half, 0)
+    own_given = [own_part(x) for x in near_streams], own_part(mixes), own_part(pres), own_part(stats)
+    near_given, far_given, _, _, own_given, own_layers, all_weights[2] = lax.optimization_barrier(
+        (near_streams[:3] + [near_grad], far_streams[:3] + [far_grad], up_part, down_part, own_given, own_layers, all_weights[2])
     )
 
     types = (f32, f32, bf16, bf16)
@@ -869,7 +879,7 @@
         ]
     )
     narrow_sum = lax.psum_scatter(narrow_part, "dp", scatter_dimension=0, tiled=True)
-    own_backs[0] = after(own_backs[0], narrow_part)
+    own_backs, wide_sum, _ = lax.optimization_barrier((own_backs, jnp.concatenate([up_sum, down_sum], 1), narrow_part))
     near_backs, far_backs = project_back(own_backs, all_weights)
     far_backs = plane.swap(far_backs)
 
@@ -877,25 +887,15 @@
     branch_far = (dot(attended[near:], out_full, (1, 1)) + dot(far_hidden, down_full, (1, 1))).astype(bf16)
     branch = (dot(attended[:near], out_full, (1, 1)) + dot(near_hidden, down_full, (1, 1))).astype(bf16)
     branch_low, branch_high = owned(branch, branch_far)
-    own_mix = lax.dynamic_slice_in_dim(mixes, h * half, half, 0)[:, :pairs].reshape(half, STREAMS, count)
-
-    def own_block(j):
-        found = lax.dynamic_slice_in_dim(slots[0][j], h % per * half, half, 0)
-        for g in range(1, parts):
-            found = jnp.where(h // per == g, lax.dynamic_slice_in_dim(slots[g][j], h % per * half, half, 0), found)
-        return found
-
-    own_layers = [own_block(j) for j in range(count)]
     mix_own = from_slots(own_mix)
     mix_rows = plane.both(mix_own, plane.swap(mix_own), 0).reshape(rows, STREAMS, count)
 
-    def spread(summed, turned):
-        return place_wide(plane.trade_rows(summed), which_h, f32, len(turned), turned)
-
-    wide_sum = jnp.concatenate([up_sum, down_sum], 1)
+    def spread(summed):
+        return lax.all_to_all(summed, "hist", 0, 0, tiled=True)
+
+    wide_sum = spread(wide_sum)
 
     scale_wide = jnp.broadcast_to(own_scale[:, None], (half, LANES))
-    own_part = lambda x: lax.dynamic_slice_in_dim(x, h * half, half, 0)
     found = backward_streams(
         own_layers,
         0,
@@ -903,10 +903,7 @@
         [(near_backs, 0), (near_backs, 1), (near_backs, 2), (owned_mlp[0], 0)],
         [(far_backs, 0), (far_backs, 1), (far_backs, 2), (owned_mlp[1], 0)],
         0,
-        [own_part(x) for x in near_streams],
-        own_part(mixes),
-        own_part(pres),
-        own_part(stats),
+        *own_given,
         own_target,
         scale_wide,
         pick,
@@ -932,9 +929,9 @@
     small = jnp.concatenate([in_sum[:, :hidden_units], gain_sum.T, packed_sum], 1)
     small = total_over_dp(jnp.pad(small, ((0, 0), (0, LANES - small.shape[1]))), plane)
     came, small, narrow_sum, wide_sum = lax.optimization_barrier((came, small, narrow_sum, wide_sum))
-    up_grad, down_grad = spread(wide_sum, (False, True))
+    up_grad, down_grad = place_wide(wide_sum, count, 2, (False, True))
     history_grad = interleave(came, plane.swap(came), which_m, half).reshape(history.shape)
-    query_grad, key_grad, value_grad, out_grad = spread(narrow_sum, (False, False, False, True))
+    query_grad, key_grad, value_grad, out_grad = place_wide(spread(narrow_sum), count, 4, (False, False, False, True))
     small = total_over_plane(small, plane)
     mixer_in_grad = small[:, :hidden_units]
     gain_all = small[:, hidden_units : hidden_units + STREAMS].T

time: 759 us -> 731 us (0.963)
  Pallas kernels: 232 us -> 206 us
    pallas_call x1, Pallas kernels: 61.3 us -> 39.3 us  [attention(): pl.pallas_call(lambda *refs: attention_kernel(count, half, heads, *refs),...]
    ppermute x6 -> x0, waiting for transfers between devices: 20.4 us -> none  [trade_rows(): lax.ppermute(block(r), 'hist', [(h, h ^ r) for h in range(self.size)])]
    ppermute x19, waiting for transfers between devices: 90.7 us -> 108 us  [step(): return lax.ppermute(value, PLANE, pairs)]
    all_gather x1, waiting for transfers between devices: 0.02 us -> 14.8 us  [shards(): down_full = lax.all_gather(down_mine, 'dp', axis=0, tiled=True)]
    ppermute x6 -> x0, starting transfers between devices: 9.67 us -> none  [trade_rows(): lax.ppermute(block(r), 'hist', [(h, h ^ r) for h in range(self.size)])]
    all_to_all x0 -> x2, starting transfers between devices: none -> 8 us  [spread(): return lax.all_to_all(summed, 'hist', 0, 0, tiled=True)]
    unnamed x86 -> x88, local copies, waits for them, and re-layouts: 17.8 us -> 10.8 us
  transfers between devices with their start and end apart: 64 -> 60, of which waited for: 28 -> 25; matrix products, arithmetic and copies ran while one was open for 26% -> 25% of each run, Pallas kernels for 30% -> 26%
where the time goes in v4:
time: 731 us; the launch traced here: 725 us
  Pallas kernels  206 us (28%)
  waiting for transfers between devices  203 us (28%)
  matrix products  82 us (11%)
  local copies, waits for them, and re-layouts  73 us (10%)
  starting transfers between devices  70 us (10%)
  other arithmetic  43.9 us (6%)
  blocking collectives  30.3 us (4%)
  between operations  16 us (2%)
    ppermute x19, waiting for transfers between devices, step(): return lax.ppermute(value, PLANE, pairs)  108 us
    dot_general x10, matrix products, dot(): lax.dot_general(left, right, (((contract[0],), (contract[1],)), ((), ()))...  82 us
    pallas_call x3, Pallas kernels, outer(): pl.pallas_call(kernel, grid=(width // tile,), in_specs=specs, out_specs=p...  45.5 us
    pallas_call x1, Pallas kernels, attention(): pl.pallas_call(lambda *refs: attention_kernel(count, half, heads, *refs),...  39.3 us
    pallas_call x2, Pallas kernels, forward_streams(): pl.pallas_call(lambda *refs: forward_kernel(count, *refs[:given], *refs[g...  37.9 us
    all_to_all x1, waiting for transfers between devices, shards(): swap_columns = lambda x: lax.all_to_all(x, 'hist', 1, 0, tiled=True)  31.5 us
    all_to_all x2, blocking collectives, shards(): swap_columns = lambda x: lax.all_to_all(x, 'hist', 1, 0, tiled=True)  30.3 us
    ppermute x19, starting transfers between devices, step(): return lax.ppermute(value, PLANE, pairs)  23.3 us
  transfers between devices with their start and end apart: 60, of which 25 were waited for; matrix products, arithmetic and copies ran while one was open for 25% of the time, Pallas kernels for 26%

profile of v4, /device:TPU:0, one launch (start us, length us, event | category | flops | bytes accessed | tf_op | source)
XLA Modules:
  0.0 724.8 jit_solution(67582171261464769)
XLA Ops:
  17.7 15.4 %all_to_all.92 = bf16[128,4,1024]{0,2,1:T(8,128)(2,1)S(1)} all-to-all(bf16[128,4,1024]{0,2,1:T(8,128)(2,1)S(1)} %bitcast.139), channel_id=1, replica_groups=mesh['dp'=4,'hist'=4,'mp'=2] {'hist'}, dimensions={1} | all-to-all | bytes 2097152 | tf_op jit(solution)/shard_map/all_to_all | solution.py:767
  41.2 23.5 %collective-permute-done.3.refs_2_ = bf16[512,2048]{1,0:T(8,128)(2,1)S(1)} collective-permute-done((bf16[512,2048]{1,0:T(8,128)(2,1)S(1)}, bf16[512,2048]{1,0:T(8,128)(2,1)S(1)}, u32[]{:S(2)}, u32[]{:S(2)}) %collective-permute-start.3) | collective-permute-done | bytes 2097184 | tf_op jit(solution)/shard_map/ppermute | solution.py:61
  76.4 16.3 %collective-permute-done.4.refs_2_ = bf16[512,2048]{1,0:T(8,128)(2,1)} collective-permute-done((bf16[512,2048]{1,0:T(8,128)(2,1)}, bf16[512,2048]{1,0:T(8,128)(2,1)}, u32[]{:S(2)}, u32[]{:S(2)}) %collective-permute-start.4) | collective-permute-done | bytes 2097184 | tf_op jit(solution)/shard_map/ppermute | solution.py:61
  92.7 14.9 %all_to_all.93 = bf16[128,4,1024]{0,2,1:T(8,128)(2,1)S(1)} all-to-all(bf16[128,4,1024]{0,2,1:T(8,128)(2,1)S(1)} %bitcast.135), channel_id=1, replica_groups=mesh['dp'=4,'hist'=4,'mp'=2] {'hist'}, dimensions={1} | all-to-all | bytes 2097152 | tf_op jit(solution)/shard_map/all_to_all | solution.py:767
  123.9 20.7 %collective-permute-done.10.refs_3_ = bf16[512,2048]{1,0:T(8,128)(2,1)} collective-permute-done((bf16[512,2048]{1,0:T(8,128)(2,1)S(1)}, bf16[512,2048]{1,0:T(8,128)(2,1)}, u32[]{:S(2)}, u32[]{:S(2)}) %collective-permute-start.10) | collective-permute-done | bytes 2097184 | tf_op jit(solution)/shard_map/ppermute | solution.py:61
  144.5 22.5 %collective-permute-done.11.refs_4_ = bf16[512,2048]{1,0:T(8,128)(2,1)} collective-permute-done((bf16[512,2048]{1,0:T(8,128)(2,1)}, bf16[512,2048]{1,0:T(8,128)(2,1)}, u32[]{:S(2)}, u32[]{:S(2)}) %collective-permute-start.11) | collective-permute-done | bytes 2097184 | tf_op jit(solution)/shard_map/ppermute | solution.py:61
  167.0 18.9 %forward_streams.2 = (bf16[1024,2048]{1,0:T(8,128)(2,1)}, bf16[1024,2048]{1,0:T(8,128)(2,1)}, bf16[1024,2048]{1,0:T(8,128)(2,1)}, bf16[1024,2048]{1,0:T(8,128)(2...) custom-call(s32[1]{0:T(128)} %bitcast.refs_0_, bf16[512,2048]{1,0:T(8,128)(2,1)} %bitcast.121, ...), custom_call_target="tpu_custom_call" | custom-call | flops 83886080 | bytes 16777216 | tf_op jit(solution)/shard_map/forward_streams/pallas_call | solution.py:182
  191.6 31.5 %all-to-all-done = bf16[128,4,1024]{0,2,1:T(8,128)(2,1)S(1)} async-done(((bf16[128,4,1024]{0,2,1:T(8,128)(2,1)}), bf16[128,4,1024]{0,2,1:T(8,128)(2,1)S(1)}, u32[]{:S(2)}, u32[]{:S(2)}) %all-to-all-start) | async-done | bytes 1048608 | tf_op jit(solution)/shard_map/all_to_all | solution.py:767
  224.7 19.0 %forward_streams.3 = (bf16[1024,2048]{1,0:T(8,128)(2,1)}, bf16[1024,2048]{1,0:T(8,128)(2,1)}, bf16[1024,2048]{1,0:T(8,128)(2,1)}, bf16[1024,2048]{1,0:T(8,128)(2...) custom-call(s32[1]{0:T(128)} %bitcast.refs_0_, ...), custom_call_target="tpu_custom_call", output_to_operand_aliasing={{0}: (9, {}), {1}: (10, {}), {2}: (11, {}), {3}: (12, {}), ... | custom-call | flops 83886080 | bytes 16777216 | tf_op jit(solution)/shard_map/forward_streams/pallas_call | solution.py:182
  253.6 10.9 %multiply_convert_fusion.1 = (bf16[1024,1024]{1,0:T(8,128)(2,1)}, f32[1024,1024]{1,0:T(8,128)}) fusion(bf16[1024,2048]{1,0:T(8,128)(2,1)} %get-tuple-element.141.refs_0_, bf16[2048,1024]{1,0:T(8,128)(2,1)} %all-gather.6.cloned.1.call-done), kind=kOutput, calls=%fused_computation.19 | convolution fusion | flops 4300210176 | bytes 14680064 | tf_op jit(solution)/shard_map/dot_general | solution.py:24
  264.5 8.9 %multiply_convert_fusion = (bf16[1024,1024]{1,0:T(8,128)(2,1)}, f32[1024,1024]{1,0:T(8,128)}) fusion(bf16[1024,2048]{1,0:T(8,128)(2,1)} %collective-permute-done.16.refs_1_, bf16[2048,1024]{1,0:T(8,128)(2,1)S(1)} %copy-done.32), kind=kOutput, calls=%fused_computation.18 | convolution fusion | flops 4300210176 | bytes 14680064 | tf_op jit(solution)/shard_map/dot_general | solution.py:24
  273.4 13.4 %outer.4 = bf16[2048,1024]{1,0:T(8,128)(2,1)} custom-call(bf16[1024,2048]{1,0:T(8,128)(2,1)} %constant_dynamic-update-slice_fusion.8.refs_0_.refs_3_.refs_12_, bf16[1024,2048]{1,0:T(8,128)(2,1)} %collective-permute-done.15.refs_1_.refs_3_.refs_13_, bf16[1024,1024]{1,0:T(8,128)(2,1)} %get-tuple-element.347.refs_2_, bf16[1024,1024]{1,0:T(8,128)(2,1)} %get-tuple-element.349.refs_3_), custom_call_target="tpu_custom_call" | custom-call | flops 8589934592 | bytes 16777216 | tf_op jit(solution)/shard_map/outer/pallas_call | solution.py:627
  290.9 14.8 %all-gather.4.cloned.1.call-done = bf16[2048,1024]{1,0:T(8,128)(2,1)} async-done(((bf16[512,1024]{1,0:T(8,128)(2,1)}), bf16[2048,1024]{1,0:T(8,128)(2,1)}) %all-gather.4.cloned.1.call-update) | async-done | bytes 4194320 | tf_op jit(solution)/shard_map/all_gather | solution.py:807
  305.7 10.4 %fusion.11.refs_3_ = bf16[1024,1024]{1,0:T(8,128)(2,1)} fusion(f32[1024,1024]{1,0:T(8,128)} %get-tuple-element.350, bf16[1024,2048]{1,0:T(8,128)(2,1)} %collective-permute-done.15.refs_1_.refs_3_.refs_13_, bf16[2048,1024]{1,0:T(8,128)(2,1)} %all-gather.4.cloned.1.call-done), kind=kOutput, calls=%fused_computation.15 | convolution fusion | flops 4305453056 | bytes 14680064 | tf_op jit(solution)/shard_map/dot_general | solution.py:24
  316.1 8.9 %fusion.5.refs_2_ = bf16[1024,1024]{1,0:T(8,128)(2,1)} fusion(f32[1024,1024]{1,0:T(8,128)S(1)} %copy-done.37, bf16[1024,2048]{1,0:T(8,128)(2,1)} %constant_dynamic-update-slice_fusion.8.refs_0_.refs_3_.refs_12_, bf16[2048,1024]{1,0:T(8,128)(2,1)S(1)} %copy-done.34), kind=kOutput, calls=%fused_computation.9 | convolution fusion | flops 4305453056 | bytes 14680064 | tf_op jit(solution)/shard_map/dot_general | solution.py:24
  327.3 13.8 %outer.3 = bf16[2048,1024]{1,0:T(8,128)(2,1)} custom-call(bf16[1024,2048]{1,0:T(8,128)(2,1)} %get-tuple-element.141.refs_0_, bf16[1024,2048]{1,0:T(8,128)(2,1)} %collective-permute-done.16.refs_1_, bf16[1024,1024]{1,0:T(8,128)(2,1)} %fusion.5.refs_2_, bf16[1024,1024]{1,0:T(8,128)(2,1)} %fusion.11.refs_3_), custom_call_target="tpu_custom_call" | custom-call | flops 8589934592 | bytes 16777216 | tf_op jit(solution)/shard_map/outer/pallas_call | solution.py:627
  341.2 9.4 %convolution_convert_fusion = bf16[1024,2048]{1,0:T(8,128)(2,1)} fusion(bf16[1024,1024]{1,0:T(8,128)(2,1)} %fusion.11.refs_3_, bf16[2048,1024]{1,0:T(8,128)(2,1)} %all-gather.6.cloned.1.call-done), kind=kOutput, calls=%fused_computation.22 | convolution fusion | flops 4297064448 | bytes 10485760 | tf_op jit(solution)/shard_map/dot_general | solution.py:24
  376.5 6.3 convolution_convert_fusion.1.a.c
  395.0 8.4 %fusion.59 = f32[1024,2048]{1,0:T(8,128)} fusion(bf16[1024,1024]{1,0:T(8,128)(2,1)} %get-tuple-element.349.refs_3_, bf16[2048,1024]{1,0:T(8,128)(2,1)S(1)} %copy-done.35), kind=kOutput, calls=%fused_computation.215 | convolution fusion | flops 4294967296 | bytes 14680064 | tf_op jit(solution)/shard_map/dot_general | solution.py:24
  404.0 11.4 %project.3 = (f32[1024,256]{1,0:T(8,128)}, f32[1024,256]{1,0:T(8,128)}, bf16[1024,256]{1,0:T(8,128)(2,1)}, bf16[1024,256]{1,0:T(8,128)(2,1)}) custom-call(bf16[1024,2048]{1,0:T(8,128)(2,1)} %collective-permute-done.18.refs_0_.refs_1_, bf16[1024,2048]{1,0:T(8,128)(2,1)} %collective-permute-done.19.refs_1_.refs_5_, ...), custom_call_target="tpu_custom_call" | custom-call | flops 4294967296 | bytes 16777216 | tf_op jit(solution)/shard_map/project/pallas_call | solution.py:532
  415.4 11.0 %project.2 = (f32[1024,256]{1,0:T(8,128)}, f32[1024,256]{1,0:T(8,128)}, bf16[1024,256]{1,0:T(8,128)(2,1)}, bf16[1024,256]{1,0:T(8,128)(2,1)}) custom-call(bf16[1024,2048]{1,0:T(8,128)(2,1)} %get-tuple-element.156.refs_0_, bf16[1024,2048]{1,0:T(8,128)(2,1)} %get-tuple-element.157.refs_1_.refs_4_, bf16[1024,2048]{1,0:T(8,128)(2,1)} %get-tuple-element.158.refs_2_.refs_8_, ...), custom_call_target="tpu_custom_call" | custom-call | flops 4294967296 | bytes 16777216 | tf_op jit(solution)/shard_map/project/pallas_call | solution.py:532
  431.0 39.3 %attention.1 = (bf16[2048,256]{1,0:T(8,128)(2,1)}, bf16[2048,256]{1,0:T(8,128)(2,1)}, bf16[2048,256]{1,0:T(8,128)(2,1)}, bf16[2048,256]{1,0:T(8,128)(2,1)}, bf16[2048,768]{1,0:T(8,128)(2,1)}) custom-call(s32[1]{0:T(128)} %bitcast.42.refs_0_.which, f32[1024,256]{1,0:T(8,128)} %get-tuple-element.160.refs_1_, f32[1024,256]{1,0:T(8,128)} %get-tuple-element.161.refs_2_, ...), custom_call_target="tpu_custom_call" | custom-call | flops 19327352832 | bytes 10485760 | tf_op jit(solution)/shard_map/attention/pallas_call | solution.py:499
  477.6 18.3 %outer.5 = bf16[2048,1024]{1,0:T(8,128)(2,1)} custom-call(bf16[1024,2048]{1,0:T(8,128)(2,1)} %get-tuple-element.156.refs_0_, bf16[1024,2048]{1,0:T(8,128)(2,1)} %collective-permute-done.18.refs_0_.refs_1_, bf16[2048,256]{1,0:T(8,128)(2,1)} %get-tuple-element.182.refs_2_.refs_3_, bf16[2048,256]{1,0:T(8,128)(2,1)} %get-tuple-element.182.refs_2_.refs_3_, ...), custom_call_target="tpu_custom_call" | custom-call | flops 8589934592 | bytes 41943040 | tf_op jit(solution)/shard_map/outer/pallas_call | solution.py:627
  498.6 12.2 %collective-permute-done.28.refs_3_ = bf16[512,768]{1,0:T(8,128)(2,1)} collective-permute-done((bf16[512,768]{1,0:T(8,128)(2,1)S(1)}, bf16[512,768]{1,0:T(8,128)(2,1)}, u32[]{:S(2)}, u32[]{:S(2)}) %collective-permute-start.28) | collective-permute-done | bytes 786464 | tf_op jit(solution)/shard_map/ppermute | solution.py:93
  510.9 12.6 %project_back.1 = (bf16[256,6144]{1,0:T(8,128)(2,1)}, bf16[256,6144]{1,0:T(8,128)(2,1)}) custom-call(bf16[512,768]{1,0:T(8,128)(2,1)} %get-tuple-element.186.refs_0_, bf16[512,768]{1,0:T(8,128)(2,1)} %collective-permute-done.26.refs_1_, bf16[512,768]{1,0:T(8,128)(2,1)} %collective-permute-done.27.refs_2_, bf16[512,768]{1,0:T(8,128)(2,1)} %collective-permute-done.28.refs_3_, ...), custom_call_target="tpu_custom_call" | custom-call | tf_op jit(solution)/shard_map/project_back/pallas_call | solution.py:560
  523.5 7.1 add_convert_fusion
  531.2 7.2 %fusion.58 = f32[1024,2048]{1,0:T(8,128)S(1)} fusion(bf16[1024,1024]{1,0:T(8,128)(2,1)} %get-tuple-element.347.refs_2_, bf16[2048,1024]{1,0:T(8,128)(2,1)} %all-gather.4.cloned.1.call-done), kind=kOutput, calls=%fused_computation.214 | convolution fusion | flops 4294967296 | bytes 14680064 | tf_op jit(solution)/shard_map/dot_general | solution.py:24
  543.0 5.8 add_in_slots.3
  557.6 22.1 %backward_streams.1 = (bf16[1024,2048]{1,0:T(8,128)(2,1)}, f32[4,2048]{1,0:T(4,128)}, f32[2048,128]{1,0:T(8,128)}, f32[128,128]{1,0:T(8,128)}, f32[1,128]{1,0:T(1,128)}) custom-call(s32[1]{0:T(128)} %bitcast.refs_0_, s32[4]{0:T(128)} %pad_add_fusion.order.refs_1_, bf16[256,2048]{1,0:T(8,128)(2,1)} %dynamic-slice_select_fusion.3.refs_2_, ...), custom_call_target="tpu_custom_call" | custom-call | flops 83886080 | bytes 20971520 | tf_op jit(solution)/shard_map/backward_streams/pallas_call | solution.py:312
  580.4 11.0 %collective-permute-done.31 = bf16[512,2048]{1,0:T(8,128)(2,1)} collective-permute-done((bf16[512,2048]{1,0:T(8,128)(2,1)}, bf16[512,2048]{1,0:T(8,128)(2,1)}, u32[]{:S(2)}, u32[]{:S(2)}) %collective-permute-start.31) | collective-permute-done | bytes 2097184 | tf_op jit(solution)/shard_map/ppermute | solution.py:61
  652.1 9.3 %collective-permute-done.32 = bf16[256,2048]{1,0:T(8,128)(2,1)} collective-permute-done((bf16[256,2048]{1,0:T(8,128)(2,1)}, bf16[256,2048]{1,0:T(8,128)(2,1)}, u32[]{:S(2)}, u32[]{:S(2)}) %collective-permute-start.32) | collective-permute-done | bytes 1048608 | tf_op jit(solution)/shard_map/ppermute | solution.py:61
  710.5 7.0 interleave.1
  (325 shorter events, 246.7 us)
Async XLA Ops:
  7.2 246.4 %all-gather.6.cloned.1.call-start = ((), (), s32[]{:S(2)}) async-start(), calls=%async_computation.10 | async-start | bytes 5242880 | tf_op jit(solution)/shard_map/all_gather | solution.py:770
  34.4 253.4 %all-gather.8.cloned.1.call-start = ((), (), s32[]{:S(2)}) async-start(), calls=%async_computation.11 | async-start | bytes 5242880 | tf_op jit(solution)/shard_map/all_gather | solution.py:776
  38.7 26.1 %collective-permute-start.3 = (bf16[512,2048]{1,0:T(8,128)(2,1)S(1)}, bf16[512,2048]{1,0:T(8,128)(2,1)S(1)}, u32[]{:S(2)}, u32[]{:S(2)}) collective-permute-start(bf16[512,2048]{1,0:T(8,128)(2,1)S(1)} %bitcast.119), channel_id=1, source_target_pairs={{0,2},{1,5},{2,0},{3,7},{4,6},{5,1},{6,4},{7,3},{8,10},{9,13},{10,... | collective-permute-start | bytes 6291464 | tf_op jit(solution)/shard_map/ppermute | solution.py:61
  66.1 26.6 %collective-permute-start.4 = (bf16[512,2048]{1,0:T(8,128)(2,1)}, bf16[512,2048]{1,0:T(8,128)(2,1)}, u32[]{:S(2)}, u32[]{:S(2)}) collective-permute-start(bf16[512,2048]{1,0:T(8,128)(2,1)} %bitcast.2.refs_1_), channel_id=1, source_target_pairs={{0,2},{1,5},{2,0},{3,7},{4,6},{5,1},{6,4},{7,3},{8,10},{9,13},{10,... | collective-permute-start | bytes 6291464 | tf_op jit(solution)/shard_map/ppermute | solution.py:61
  108.9 35.6 %collective-permute-start.10 = (bf16[512,2048]{1,0:T(8,128)(2,1)S(1)}, bf16[512,2048]{1,0:T(8,128)(2,1)}, u32[]{:S(2)}, u32[]{:S(2)}) collective-permute-start(bf16[512,2048]{1,0:T(8,128)(2,1)S(1)} %bitcast.120), channel_id=1, source_target_pairs={{0,4},{1,3},{2,6},{3,1},{4,0},{5,7},{6,2},{7,5},{8,12},{9,11},{10,... | collective-permute-start | bytes 6291464 | tf_op jit(solution)/shard_map/ppermute | solution.py:61
  110.3 56.7 %collective-permute-start.11 = (bf16[512,2048]{1,0:T(8,128)(2,1)}, bf16[512,2048]{1,0:T(8,128)(2,1)}, u32[]{:S(2)}, u32[]{:S(2)}) collective-permute-start(bf16[512,2048]{1,0:T(8,128)(2,1)} %copy-done.10), channel_id=1, source_target_pairs={{0,4},{1,3},{2,6},{3,1},{4,0},{5,7},{6,2},{7,5},{8,12},{9,11},{10,... | collective-permute-start | bytes 6291464 | tf_op jit(solution)/shard_map/ppermute | solution.py:61
  113.1 111.5 %collective-permute-start.5 = (bf16[512,2048]{1,0:T(8,128)(2,1)}, bf16[512,2048]{1,0:T(8,128)(2,1)}, u32[]{:S(2)}, u32[]{:S(2)}) collective-permute-start(bf16[512,2048]{1,0:T(8,128)(2,1)} %bitcast.2.refs_1_), channel_id=1, source_target_pairs={{0,4},{1,3},{2,6},{3,1},{4,0},{5,7},{6,2},{7,5},{8,12},{9,11},{10,... | collective-permute-start | bytes 6291464 | tf_op jit(solution)/shard_map/ppermute | solution.py:61
  114.4 110.3 %collective-permute-start.6 = (bf16[512,2048]{1,0:T(8,128)(2,1)}, bf16[512,2048]{1,0:T(8,128)(2,1)}, u32[]{:S(2)}, u32[]{:S(2)}) collective-permute-start(bf16[512,2048]{1,0:T(8,128)(2,1)} %collective-permute-done.4.refs_2_), channel_id=1, source_target_pairs={{0,4},{1,3},{2,6},{3,1},{4,0},{5,7},{6,2},{7,5},{8,12},{9,11},{10,... | collective-permute-start | bytes 6291464 | tf_op jit(solution)/shard_map/ppermute | solution.py:61
  118.4 73.0 %collective-permute-start.12 = (bf16[256,2048]{1,0:T(8,128)(2,1)S(1)}, bf16[256,2048]{1,0:T(8,128)(2,1)}, u32[]{:S(2)}, u32[]{:S(2)}) collective-permute-start(bf16[256,2048]{1,0:T(8,128)(2,1)S(1)} %get-tuple-element.139), channel_id=1, source_target_pairs={{0,2},{1,5},{2,0},{3,7},{4,6},{5,1},{6,4},{7,3},{8,10},{9,13},{10,... | collective-permute-start | bytes 3145736 | tf_op jit(solution)/shard_map/ppermute | solution.py:61
  185.9 37.2 %all-to-all-start = ((bf16[128,4,1024]{0,2,1:T(8,128)(2,1)}), bf16[128,4,1024]{0,2,1:T(8,128)(2,1)S(1)}, u32[]{:S(2)}, u32[]{:S(2)}) async-start(bf16[128,4,1024]{0,2,1:T(8,128)(2,1)} %bitcast.19), calls=%async_computation | async-start | bytes 2097152 | tf_op jit(solution)/shard_map/all_to_all | solution.py:767
  189.4 116.3 %all-gather.4.cloned.1.call-start = ((), (), s32[]{:S(2)}) async-start(), calls=%async_computation.9 | async-start | bytes 5242880 | tf_op jit(solution)/shard_map/all_gather | solution.py:807
  189.5 60.2 %collective-permute-start.13 = (bf16[256,2048]{1,0:T(8,128)(2,1)S(1)}, bf16[256,2048]{1,0:T(8,128)(2,1)S(1)}, u32[]{:S(2)}, u32[]{:S(2)}) collective-permute-start(bf16[256,2048]{1,0:T(8,128)(2,1)S(1)} %get-tuple-element.139), channel_id=1, source_target_pairs={{0,4},{1,3},{2,6},{3,1},{4,0},{5,7},{6,2},{7,5},{8,12},{9,11},{10,... | collective-permute-start | bytes 3145736 | tf_op jit(solution)/shard_map/ppermute | solution.py:61
  191.4 59.3 %collective-permute-start.14 = (bf16[256,2048]{1,0:T(8,128)(2,1)}, bf16[256,2048]{1,0:T(8,128)(2,1)}, u32[]{:S(2)}, u32[]{:S(2)}) collective-permute-start(bf16[256,2048]{1,0:T(8,128)(2,1)} %collective-permute-done.12), channel_id=1, source_target_pairs={{0,4},{1,3},{2,6},{3,1},{4,0},{5,7},{6,2},{7,5},{8,12},{9,11},{10,... | collective-permute-start | bytes 3145736 | tf_op jit(solution)/shard_map/ppermute | solution.py:61
  224.4 245.9 %reduce-scatter.4.cloned.1.call-start = ((), (), s32[]{:S(2)}) async-start(), calls=%async_computation.12 | async-start | bytes 5242880 | tf_op jit(solution)/shard_map/reduce_scatter | solution.py:834
  286.8 209.0 %reduce-scatter.6.cloned.1.call-start = ((), (), s32[]{:S(2)}) async-start(), calls=%async_computation.13 | async-start | bytes 5242880 | tf_op jit(solution)/shard_map/reduce_scatter | solution.py:839
  287.1 37.9 %collective-permute-start.18 = (bf16[1024,2048]{1,0:T(8,128)(2,1)}, bf16[1024,2048]{1,0:T(8,128)(2,1)}, u32[]{:S(2)}, u32[]{:S(2)}) collective-permute-start(bf16[1024,2048]{1,0:T(8,128)(2,1)} %get-tuple-element.156.refs_0_), channel_id=1, source_target_pairs={{0,1},{1,0},{2,3},{3,2},{4,5},{5,4},{6,7},{7,6},{8,9},{9,8},{10,11... | collective-permute-start | bytes 12582920 | tf_op jit(solution)/shard_map/ppermute | solution.py:124
  287.2 37.8 %collective-permute-start.19 = (bf16[1024,2048]{1,0:T(8,128)(2,1)}, bf16[1024,2048]{1,0:T(8,128)(2,1)}, u32[]{:S(2)}, u32[]{:S(2)}) collective-permute-start(bf16[1024,2048]{1,0:T(8,128)(2,1)} %get-tuple-element.157.refs_1_.refs_4_), channel_id=1, source_target_pairs={{0,1},{1,0},{2,3},{3,2},{4,5},{5,4},{6,7},{7,6},{8,9},{9,8},{10,11... | collective-permute-start | bytes 12582920 | tf_op jit(solution)/shard_map/ppermute | solution.py:124
  287.7 37.3 %collective-permute-start.20 = (bf16[1024,2048]{1,0:T(8,128)(2,1)}, bf16[1024,2048]{1,0:T(8,128)(2,1)}, u32[]{:S(2)}, u32[]{:S(2)}) collective-permute-start(bf16[1024,2048]{1,0:T(8,128)(2,1)} %get-tuple-element.158.refs_2_.refs_8_), channel_id=1, source_target_pairs={{0,1},{1,0},{2,3},{3,2},{4,5},{5,4},{6,7},{7,6},{8,9},{9,8},{10,11... | collective-permute-start | bytes 12582920 | tf_op jit(solution)/shard_map/ppermute | solution.py:124
  289.9 37.4 %collective-permute-start.17 = (bf16[2048,768]{1,0:T(8,128)(2,1)S(1)}, bf16[2048,768]{1,0:T(8,128)(2,1)}, u32[]{:S(2)}, u32[]{:S(2)}) collective-permute-start(bf16[2048,768]{1,0:T(8,128)(2,1)S(1)} %slice.238.refs_4_), channel_id=1, source_target_pairs={{0,2},{1,5},{2,0},{3,7},{4,6},{5,1},{6,4},{7,3},{8,10},{9,13},{10,... | collective-permute-start | bytes 9437192 | tf_op jit(solution)/shard_map/ppermute | solution.py:61
  350.6 32.2 %collective-permute-start.22 = (bf16[1024,2048]{1,0:T(8,128)(2,1)}, bf16[1024,2048]{1,0:T(8,128)(2,1)}, u32[]{:S(2)}, u32[]{:S(2)}) collective-permute-start(bf16[1024,2048]{1,0:T(8,128)(2,1)} %convolution_convert_fusion), channel_id=1, source_target_pairs={{0,1},{1,0},{2,3},{3,2},{4,5},{5,4},{6,7},{7,6},{8,9},{9,8},{10,11... | collective-permute-start | bytes 12582920 | tf_op jit(solution)/shard_map/ppermute | solution.py:124
  358.8 288.4 %reduce-scatter.8.cloned.1.call-start = ((), (), s32[]{:S(2)}) async-start(), calls=%async_computation.14 | async-start | bytes 5242880 | tf_op jit(solution)/shard_map/reduce_scatter | solution.py:881
  364.6 38.8 %collective-permute-start.21 = (bf16[2048,768]{1,0:T(8,128)(2,1)S(1)}, bf16[2048,768]{1,0:T(8,128)(2,1)S(1)}, u32[]{:S(2)}, u32[]{:S(2)}) collective-permute-start(bf16[2048,768]{1,0:T(8,128)(2,1)S(1)} %copy-done.4), channel_id=1, source_target_pairs={{0,4},{1,3},{2,6},{3,1},{4,0},{5,7},{6,2},{7,5},{8,12},{9,11},{10,... | collective-permute-start | bytes 9437192 | tf_op jit(solution)/shard_map/ppermute | solution.py:61
  388.6 37.8 %collective-permute-start.23 = (bf16[512,2048]{1,0:T(8,128)(2,1)}, bf16[512,2048]{1,0:T(8,128)(2,1)}, u32[]{:S(2)}, u32[]{:S(2)}) collective-permute-start(bf16[512,2048]{1,0:T(8,128)(2,1)} %get-tuple-element.177), channel_id=1, source_target_pairs={{0,4},{1,3},{2,6},{3,1},{4,0},{5,7},{6,2},{7,5},{8,12},{9,11},{10,... | collective-permute-start | bytes 6291464 | tf_op jit(solution)/shard_map/ppermute | solution.py:61
  403.4 66.9 %collective-permute-start.25 = (bf16[2048,768]{1,0:T(8,128)(2,1)}, bf16[2048,768]{1,0:T(8,128)(2,1)}, u32[]{:S(2)}, u32[]{:S(2)}) collective-permute-start(bf16[2048,768]{1,0:T(8,128)(2,1)} %collective-permute-done.17.refs_5_), channel_id=1, source_target_pairs={{0,4},{1,3},{2,6},{3,1},{4,0},{5,7},{6,2},{7,5},{8,12},{9,11},{10,... | collective-permute-start | bytes 9437192 | tf_op jit(solution)/shard_map/ppermute | solution.py:61
  430.0 40.4 %collective-permute-start.24 = (bf16[256,2048]{1,0:T(8,128)(2,1)S(1)}, bf16[256,2048]{1,0:T(8,128)(2,1)S(1)}, u32[]{:S(2)}, u32[]{:S(2)}) collective-permute-start(bf16[256,2048]{1,0:T(8,128)(2,1)S(1)} %get-tuple-element.306), channel_id=1, source_target_pairs={{0,2},{1,5},{2,0},{3,7},{4,6},{5,1},{6,4},{7,3},{8,10},{9,13},{10,... | collective-permute-start | bytes 3145736 | tf_op jit(solution)/shard_map/ppermute | solution.py:61
  476.0 34.9 %collective-permute-start.28 = (bf16[512,768]{1,0:T(8,128)(2,1)S(1)}, bf16[512,768]{1,0:T(8,128)(2,1)}, u32[]{:S(2)}, u32[]{:S(2)}) collective-permute-start(bf16[512,768]{1,0:T(8,128)(2,1)S(1)} %get-tuple-element.298), channel_id=1, source_target_pairs={{0,6},{1,7},{2,4},{3,5},{4,2},{5,3},{6,0},{7,1},{8,14},{9,15},{10,... | collective-permute-start | bytes 2359304 | tf_op jit(solution)/shard_map/ppermute | solution.py:93
  530.6 25.2 %collective-permute-start.29 = (bf16[256,6144]{1,0:T(8,128)(2,1)}, bf16[256,6144]{1,0:T(8,128)(2,1)S(1)}, u32[]{:S(2)}, u32[]{:S(2)}) collective-permute-start(bf16[256,6144]{1,0:T(8,128)(2,1)} %get-tuple-element.195), channel_id=1, source_target_pairs={{0,1},{1,0},{2,3},{3,2},{4,5},{5,4},{6,7},{7,6},{8,9},{9,8},{10,11... | collective-permute-start | bytes 9437192 | tf_op jit(solution)/shard_map/ppermute | solution.py:124
  548.9 42.6 %collective-permute-start.31 = (bf16[512,2048]{1,0:T(8,128)(2,1)}, bf16[512,2048]{1,0:T(8,128)(2,1)}, u32[]{:S(2)}, u32[]{:S(2)}) collective-permute-start(bf16[512,2048]{1,0:T(8,128)(2,1)} %get-tuple-element.206), channel_id=1, source_target_pairs={{0,4},{1,3},{2,6},{3,1},{4,0},{5,7},{6,2},{7,5},{8,12},{9,11},{10,... | collective-permute-start | bytes 6291464 | tf_op jit(solution)/shard_map/ppermute | solution.py:61
  550.7 47.1 %all-to-all-start.3 = ((bf16[4,128,2048]{2,1,0:T(8,128)(2,1)}), bf16[4,128,2048]{2,1,0:T(8,128)(2,1)}, u32[]{:S(2)}, u32[]{:S(2)}) async-start(bf16[4,128,2048]{2,1,0:T(8,128)(2,1)} %bitcast.129), calls=%async_computation.5 | async-start | bytes 4194304 | tf_op jit(solution)/shard_map/all_to_all | solution.py:894
  597.8 53.2 %all-to-all-start.4 = ((bf16[4,256,2048]{2,1,0:T(8,128)(2,1)}), bf16[4,256,2048]{2,1,0:T(8,128)(2,1)}, u32[]{:S(2)}, u32[]{:S(2)}) async-start(bf16[4,256,2048]{2,1,0:T(8,128)(2,1)} %bitcast.130), calls=%async_computation.6 | async-start | bytes 8388608 | tf_op jit(solution)/shard_map/all_to_all | solution.py:921
  635.5 25.8 %collective-permute-start.32 = (bf16[256,2048]{1,0:T(8,128)(2,1)}, bf16[256,2048]{1,0:T(8,128)(2,1)}, u32[]{:S(2)}, u32[]{:S(2)}) collective-permute-start(bf16[256,2048]{1,0:T(8,128)(2,1)} %get-tuple-element.305), channel_id=1, source_target_pairs={{0,2},{1,5},{2,0},{3,7},{4,6},{5,1},{6,4},{7,3},{8,10},{9,13},{10,... | collective-permute-start | bytes 3145736 | tf_op jit(solution)/shard_map/ppermute | solution.py:61
  651.0 59.5 %collective-permute-start.42 = (bf16[1024,2048]{1,0:T(8,128)(2,1)}, bf16[1024,2048]{1,0:T(8,128)(2,1)}, u32[]{:S(2)}, u32[]{:S(2)}) collective-permute-start(bf16[1024,2048]{1,0:T(8,128)(2,1)} %bitcast.51.own_ref), channel_id=1, source_target_pairs={{0,1},{1,0},{2,3},{3,2},{4,5},{5,4},{6,7},{7,6},{8,9},{9,8},{10,11... | collective-permute-start | bytes 12582920 | tf_op jit(solution)/shard_map/ppermute | solution.py:124
  (67 other events, 1132.8 us)
Sparse Core Ops, SparseCore 0:
  34.5 80.8 all-gather.5
  117.0 79.1 all-gather.7
  224.5 81.1 all-gather.3
  307.8 75.2 reduce-scatter.3
  385.4 77.2 reduce-scatter.5
  530.7 77.8 reduce-scatter.7

commit v5 on v4

--- a/solution.py
+++ b/solution.py
@@ -658,15 +658,18 @@
     return out
 
 
-def total_over_plane(out, plane):
-    side = out.shape[0]
-    cut = lambda x, at, size: lax.dynamic_slice_in_dim(x, at * size, size, 0)
-    block = side // plane.size
-    mine = cut(out, plane.h, block)
+def total_over_hist(out, plane):
+    block = out.shape[0] // plane.size
+    cut = lambda x, at: lax.dynamic_slice_in_dim(x, at * block, block, 0)
+    mine = cut(out, plane.h)
     for j in range(1, plane.size):
-        mine = mine + plane.direct(cut(out, plane.h ^ plane.place(j), block), j)
+        mine = mine + plane.direct(cut(out, plane.h ^ plane.place(j)), j)
+    return mine
+
+
+def over_plane(mine, plane):
     out = plane.ordered([mine] + [plane.direct(mine, j) for j in range(1, plane.size)])
-    return plane.both(out, plane.swap(out), 0).reshape((2 * side,) + out.shape[1:])
+    return plane.both(out, plane.swap(out), 0).reshape((2 * out.shape[0],) + out.shape[1:])
 
 
 def interleave(own, sibling, m, half):
@@ -717,6 +720,9 @@
 
 def after(value, *others):
     return lax.optimization_barrier((value,) + others)[0]
+
+
+tie = lax.optimization_barrier
 
 
 def shards(
@@ -886,7 +892,8 @@
     attended = after(attended, near_backs)
     branch_far = (dot(attended[near:], out_full, (1, 1)) + dot(far_hidden, down_full, (1, 1))).astype(bf16)
     branch = (dot(attended[:near], out_full, (1, 1)) + dot(near_hidden, down_full, (1, 1))).astype(bf16)
-    branch_low, branch_high = owned(branch, branch_far)
+    branch_slots = add_in_slots(branch, plane.swap(branch_far), order, count)
+    branch_low, branch_high = plane.scatter_packed(*branch_slots)
     mix_own = from_slots(own_mix)
     mix_rows = plane.both(mix_own, plane.swap(mix_own), 0).reshape(rows, STREAMS, count)
 
@@ -895,7 +902,7 @@
 
     wide_sum = spread(wide_sum)
 
-    scale_wide = jnp.broadcast_to(own_scale[:, None], (half, LANES))
+    scale_wide, _ = tie((jnp.broadcast_to(own_scale[:, None], (half, LANES)), branch_slots))
     found = backward_streams(
         own_layers,
         0,
@@ -913,11 +920,6 @@
         gain,
     )
     layer_grads, sums = found[0], found[1:]
-    layer_grads, branch_low, wide_sum = lax.optimization_barrier((layer_grads, branch_low, wide_sum))
-    branch_rows = branch_low.astype(f32) + branch_high.astype(f32)
-    residual = sum(own_mix[:, STREAMS - 1, j, None] * own_layers[j].astype(f32) for j in range(count))
-    output_own = (residual + branch_rows).astype(bf16)
-    output = plane.both(output_own, plane.swap(output_own), 0).reshape(rows, width)
     came = lax.all_to_all(layer_grads, "hist", 0, 0, tiled=True)
     gain_sum, in_sum, out_sum, bias_sum = sums
     out_sum = from_slots(out_sum[:, :pairs].reshape(LANES, STREAMS, count)).reshape(LANES, pairs)
@@ -928,11 +930,21 @@
     packed_sum = jnp.pad(packed_sum, (0, width * spare - packed_sum.shape[0])).reshape(width, spare)
     small = jnp.concatenate([in_sum[:, :hidden_units], gain_sum.T, packed_sum], 1)
     small = total_over_dp(jnp.pad(small, ((0, 0), (0, LANES - small.shape[1]))), plane)
-    came, small, narrow_sum, wide_sum = lax.optimization_barrier((came, small, narrow_sum, wide_sum))
+    came, small, narrow_sum, wide_sum, branch_low = tie((came, small, narrow_sum, wide_sum, branch_low))
+    swapped = plane.swap(came)
+    narrow_sum = spread(narrow_sum)
+    small = total_over_hist(small, plane)
+    history_grad = interleave(came, swapped, which_m, half).reshape(history.shape)
     up_grad, down_grad = place_wide(wide_sum, count, 2, (False, True))
-    history_grad = interleave(came, plane.swap(came), which_m, half).reshape(history.shape)
-    query_grad, key_grad, value_grad, out_grad = place_wide(spread(narrow_sum), count, 4, (False, False, False, True))
-    small = total_over_plane(small, plane)
+    history_grad, up_grad, down_grad, narrow_sum, small, branch_low, branch_high = tie(
+        (history_grad, up_grad, down_grad, narrow_sum, small, branch_low, branch_high)
+    )
+    branch_rows = branch_low.astype(f32) + branch_high.astype(f32)
+    residual = sum(own_mix[:, STREAMS - 1, j, None] * own_layers[j].astype(f32) for j in range(count))
+    output_own = (residual + branch_rows).astype(bf16)
+    output = plane.both(output_own, plane.swap(output_own), 0).reshape(rows, width)
+    query_grad, key_grad, value_grad, out_grad = place_wide(narrow_sum, count, 4, (False, False, False, True))
+    small = over_plane(small, plane)
     mixer_in_grad = small[:, :hidden_units]
     gain_all = small[:, hidden_units : hidden_units + STREAMS].T
     place = (z * count + h) * norm_gain.shape[1]

time: 731 us -> 723 us (0.989)
  local copies, waits for them, and re-layouts: 73 us -> 64.2 us
    ppermute x19, waiting for transfers between devices: 108 us -> 87.3 us  [step(): return lax.ppermute(value, PLANE, pairs)]
    ppermute x9, waiting for transfers between devices: 22.2 us -> 35.8 us  [direct(): return lax.ppermute(value, PLANE, pairs)]
  transfers between devices with their start and end apart: 60 -> 60, of which waited for: 25 -> 21; matrix products, arithmetic and copies ran while one was open for 25% -> 25% of each run, Pallas kernels for 26% -> 27%
where the time goes in v5:
time: 723 us; the launch traced here: 716 us
  Pallas kernels  207 us (29%)
  waiting for transfers between devices  198 us (27%)
  matrix products  88.3 us (12%)
  starting transfers between devices  71.3 us (10%)
  local copies, waits for them, and re-layouts  64.2 us (9%)
  other arithmetic  41 us (6%)
  blocking collectives  30.3 us (4%)
  between operations  16.2 us (2%)
    dot_general x10, matrix products, dot(): lax.dot_general(left, right, (((contract[0],), (contract[1],)), ((), ()))...  88.3 us
    ppermute x19, waiting for transfers between devices, step(): return lax.ppermute(value, PLANE, pairs)  87.3 us
    pallas_call x3, Pallas kernels, outer(): pl.pallas_call(kernel, grid=(width // tile,), in_specs=specs, out_specs=p...  45.6 us
    pallas_call x1, Pallas kernels, attention(): pl.pallas_call(lambda *refs: attention_kernel(count, half, heads, *refs),...  39.2 us
    pallas_call x2, Pallas kernels, forward_streams(): pl.pallas_call(lambda *refs: forward_kernel(count, *refs[:given], *refs[g...  37.9 us
    ppermute x9, waiting for transfers between devices, direct(): return lax.ppermute(value, PLANE, pairs)  35.8 us
    all_to_all x1, waiting for transfers between devices, shards(): swap_columns = lambda x: lax.all_to_all(x, 'hist', 1, 0, tiled=True)  31.5 us
    all_to_all x2, blocking collectives, shards(): swap_columns = lambda x: lax.all_to_all(x, 'hist', 1, 0, tiled=True)  30.3 us
  transfers between devices with their start and end apart: 60, of which 21 were waited for; matrix products, arithmetic and copies ran while one was open for 25% of the time, Pallas kernels for 27%

profile of v5, /device:TPU:0, one launch (start us, length us, event | category | flops | bytes accessed | tf_op | source)
XLA Modules:
  0.0 716.2 jit_solution(12795319513973918062)
XLA Ops:
  17.7 15.4 %all_to_all.93 = bf16[128,4,1024]{0,2,1:T(8,128)(2,1)S(1)} all-to-all(bf16[128,4,1024]{0,2,1:T(8,128)(2,1)S(1)} %bitcast.138), channel_id=1, replica_groups=mesh['dp'=4,'hist'=4,'mp'=2] {'hist'}, dimensions={1} | all-to-all | bytes 2097152 | tf_op jit(solution)/shard_map/all_to_all | solution.py:773
  41.2 23.5 %collective-permute-done.3.refs_2_ = bf16[512,2048]{1,0:T(8,128)(2,1)S(1)} collective-permute-done((bf16[512,2048]{1,0:T(8,128)(2,1)S(1)}, bf16[512,2048]{1,0:T(8,128)(2,1)S(1)}, u32[]{:S(2)}, u32[]{:S(2)}) %collective-permute-start.3) | collective-permute-done | bytes 2097184 | tf_op jit(solution)/shard_map/ppermute | solution.py:61
  76.4 16.3 %collective-permute-done.4.refs_2_ = bf16[512,2048]{1,0:T(8,128)(2,1)} collective-permute-done((bf16[512,2048]{1,0:T(8,128)(2,1)}, bf16[512,2048]{1,0:T(8,128)(2,1)}, u32[]{:S(2)}, u32[]{:S(2)}) %collective-permute-start.4) | collective-permute-done | bytes 2097184 | tf_op jit(solution)/shard_map/ppermute | solution.py:61
  92.7 14.9 %all_to_all.94 = bf16[128,4,1024]{0,2,1:T(8,128)(2,1)S(1)} all-to-all(bf16[128,4,1024]{0,2,1:T(8,128)(2,1)S(1)} %bitcast.134), channel_id=1, replica_groups=mesh['dp'=4,'hist'=4,'mp'=2] {'hist'}, dimensions={1} | all-to-all | bytes 2097152 | tf_op jit(solution)/shard_map/all_to_all | solution.py:773
  123.9 20.7 %collective-permute-done.10.refs_3_ = bf16[512,2048]{1,0:T(8,128)(2,1)} collective-permute-done((bf16[512,2048]{1,0:T(8,128)(2,1)S(1)}, bf16[512,2048]{1,0:T(8,128)(2,1)}, u32[]{:S(2)}, u32[]{:S(2)}) %collective-permute-start.10) | collective-permute-done | bytes 2097184 | tf_op jit(solution)/shard_map/ppermute | solution.py:61
  144.6 22.5 %collective-permute-done.11.refs_4_ = bf16[512,2048]{1,0:T(8,128)(2,1)} collective-permute-done((bf16[512,2048]{1,0:T(8,128)(2,1)}, bf16[512,2048]{1,0:T(8,128)(2,1)}, u32[]{:S(2)}, u32[]{:S(2)}) %collective-permute-start.11) | collective-permute-done | bytes 2097184 | tf_op jit(solution)/shard_map/ppermute | solution.py:61
  167.0 18.9 %forward_streams.2 = (bf16[1024,2048]{1,0:T(8,128)(2,1)}, bf16[1024,2048]{1,0:T(8,128)(2,1)}, bf16[1024,2048]{1,0:T(8,128)(2,1)}, bf16[1024,2048]{1,0:T(8,128)(2...) custom-call(s32[1]{0:T(128)} %bitcast.refs_0_, bf16[512,2048]{1,0:T(8,128)(2,1)} %bitcast.121, ...), custom_call_target="tpu_custom_call" | custom-call | flops 83886080 | bytes 16777216 | tf_op jit(solution)/shard_map/forward_streams/pallas_call | solution.py:182
  191.6 31.5 %all-to-all-done = bf16[128,4,1024]{0,2,1:T(8,128)(2,1)S(1)} async-done(((bf16[128,4,1024]{0,2,1:T(8,128)(2,1)}), bf16[128,4,1024]{0,2,1:T(8,128)(2,1)S(1)}, u32[]{:S(2)}, u32[]{:S(2)}) %all-to-all-start) | async-done | bytes 1048608 | tf_op jit(solution)/shard_map/all_to_all | solution.py:773
  224.7 19.0 %forward_streams.3 = (bf16[1024,2048]{1,0:T(8,128)(2,1)}, bf16[1024,2048]{1,0:T(8,128)(2,1)}, bf16[1024,2048]{1,0:T(8,128)(2,1)}, bf16[1024,2048]{1,0:T(8,128)(2...) custom-call(s32[1]{0:T(128)} %bitcast.refs_0_, ...), custom_call_target="tpu_custom_call", output_to_operand_aliasing={{0}: (9, {}), {1}: (10, {}), {2}: (11, {}), {3}: (12, {}), ... | custom-call | flops 83886080 | bytes 16777216 | tf_op jit(solution)/shard_map/forward_streams/pallas_call | solution.py:182
  253.6 10.9 %multiply_convert_fusion.1 = (bf16[1024,1024]{1,0:T(8,128)(2,1)}, f32[1024,1024]{1,0:T(8,128)}) fusion(bf16[1024,2048]{1,0:T(8,128)(2,1)} %get-tuple-element.147.refs_0_, bf16[2048,1024]{1,0:T(8,128)(2,1)} %all-gather.6.cloned.1.call-done), kind=kOutput, calls=%fused_computation.19 | convolution fusion | flops 4300210176 | bytes 14680064 | tf_op jit(solution)/shard_map/dot_general | solution.py:24
  264.5 8.9 %multiply_convert_fusion = (bf16[1024,1024]{1,0:T(8,128)(2,1)}, f32[1024,1024]{1,0:T(8,128)}) fusion(bf16[1024,2048]{1,0:T(8,128)(2,1)} %collective-permute-done.16.refs_1_, bf16[2048,1024]{1,0:T(8,128)(2,1)S(1)} %copy-done.28), kind=kOutput, calls=%fused_computation.18 | convolution fusion | flops 4300210176 | bytes 14680064 | tf_op jit(solution)/shard_map/dot_general | solution.py:24
  273.5 13.4 %outer.4 = bf16[2048,1024]{1,0:T(8,128)(2,1)} custom-call(bf16[1024,2048]{1,0:T(8,128)(2,1)} %constant_dynamic-update-slice_fusion.8.refs_0_.refs_3_.refs_12_, bf16[1024,2048]{1,0:T(8,128)(2,1)} %collective-permute-done.15.refs_1_.refs_3_.refs_13_, bf16[1024,1024]{1,0:T(8,128)(2,1)} %get-tuple-element.357.refs_2_, bf16[1024,1024]{1,0:T(8,128)(2,1)} %get-tuple-element.359.refs_3_), custom_call_target="tpu_custom_call" | custom-call | flops 8589934592 | bytes 16777216 | tf_op jit(solution)/shard_map/outer/pallas_call | solution.py:627
  291.0 14.8 %all-gather.4.cloned.1.call-done = bf16[2048,1024]{1,0:T(8,128)(2,1)} async-done(((bf16[512,1024]{1,0:T(8,128)(2,1)}), bf16[2048,1024]{1,0:T(8,128)(2,1)}) %all-gather.4.cloned.1.call-update) | async-done | bytes 4194320 | tf_op jit(solution)/shard_map/all_gather | solution.py:813
  305.7 10.4 %fusion.11.refs_3_ = bf16[1024,1024]{1,0:T(8,128)(2,1)} fusion(f32[1024,1024]{1,0:T(8,128)} %get-tuple-element.360, bf16[1024,2048]{1,0:T(8,128)(2,1)} %collective-permute-done.15.refs_1_.refs_3_.refs_13_, bf16[2048,1024]{1,0:T(8,128)(2,1)} %all-gather.4.cloned.1.call-done), kind=kOutput, calls=%fused_computation.15 | convolution fusion | flops 4305453056 | bytes 14680064 | tf_op jit(solution)/shard_map/dot_general | solution.py:24
  316.2 8.9 %fusion.5.refs_2_ = bf16[1024,1024]{1,0:T(8,128)(2,1)} fusion(f32[1024,1024]{1,0:T(8,128)S(1)} %copy-done.33, bf16[1024,2048]{1,0:T(8,128)(2,1)} %constant_dynamic-update-slice_fusion.8.refs_0_.refs_3_.refs_12_, bf16[2048,1024]{1,0:T(8,128)(2,1)S(1)} %copy-done.30), kind=kOutput, calls=%fused_computation.9 | convolution fusion | flops 4305453056 | bytes 14680064 | tf_op jit(solution)/shard_map/dot_general | solution.py:24
  327.4 13.9 %outer.3 = bf16[2048,1024]{1,0:T(8,128)(2,1)} custom-call(bf16[1024,2048]{1,0:T(8,128)(2,1)} %get-tuple-element.147.refs_0_, bf16[1024,2048]{1,0:T(8,128)(2,1)} %collective-permute-done.16.refs_1_, bf16[1024,1024]{1,0:T(8,128)(2,1)} %fusion.5.refs_2_, bf16[1024,1024]{1,0:T(8,128)(2,1)} %fusion.11.refs_3_), custom_call_target="tpu_custom_call" | custom-call | flops 8589934592 | bytes 16777216 | tf_op jit(solution)/shard_map/outer/pallas_call | solution.py:627
  341.3 9.4 %convolution_convert_fusion = bf16[1024,2048]{1,0:T(8,128)(2,1)} fusion(bf16[1024,1024]{1,0:T(8,128)(2,1)} %fusion.11.refs_3_, bf16[2048,1024]{1,0:T(8,128)(2,1)} %all-gather.6.cloned.1.call-done), kind=kOutput, calls=%fused_computation.22 | convolution fusion | flops 4297064448 | bytes 10485760 | tf_op jit(solution)/shard_map/dot_general | solution.py:24
  376.7 6.3 convolution_convert_fusion.1.a.c
  395.1 8.4 %fusion.59 = f32[1024,2048]{1,0:T(8,128)} fusion(bf16[1024,1024]{1,0:T(8,128)(2,1)} %get-tuple-element.359.refs_3_, bf16[2048,1024]{1,0:T(8,128)(2,1)S(1)} %copy-done.31), kind=kOutput, calls=%fused_computation.215 | convolution fusion | flops 4294967296 | bytes 14680064 | tf_op jit(solution)/shard_map/dot_general | solution.py:24
  404.4 11.1 %project.3 = (f32[1024,256]{1,0:T(8,128)}, f32[1024,256]{1,0:T(8,128)}, bf16[1024,256]{1,0:T(8,128)(2,1)}, bf16[1024,256]{1,0:T(8,128)(2,1)}) custom-call(bf16[1024,2048]{1,0:T(8,128)(2,1)} %collective-permute-done.18.refs_0_.refs_1_, bf16[1024,2048]{1,0:T(8,128)(2,1)} %collective-permute-done.19.refs_1_.refs_5_, ...), custom_call_target="tpu_custom_call" | custom-call | flops 4294967296 | bytes 16777216 | tf_op jit(solution)/shard_map/project/pallas_call | solution.py:532
  415.5 11.0 %project.2 = (f32[1024,256]{1,0:T(8,128)}, f32[1024,256]{1,0:T(8,128)}, bf16[1024,256]{1,0:T(8,128)(2,1)}, bf16[1024,256]{1,0:T(8,128)(2,1)}) custom-call(bf16[1024,2048]{1,0:T(8,128)(2,1)} %get-tuple-element.162.refs_0_, bf16[1024,2048]{1,0:T(8,128)(2,1)} %get-tuple-element.163.refs_1_.refs_4_, bf16[1024,2048]{1,0:T(8,128)(2,1)} %get-tuple-element.164.refs_2_.refs_8_, ...), custom_call_target="tpu_custom_call" | custom-call | flops 4294967296 | bytes 16777216 | tf_op jit(solution)/shard_map/project/pallas_call | solution.py:532
  431.3 39.2 %attention.1 = (bf16[2048,256]{1,0:T(8,128)(2,1)}, bf16[2048,256]{1,0:T(8,128)(2,1)}, bf16[2048,256]{1,0:T(8,128)(2,1)}, bf16[2048,256]{1,0:T(8,128)(2,1)}, bf16[2048,768]{1,0:T(8,128)(2,1)}) custom-call(s32[1]{0:T(128)} %bitcast.38.refs_0_.which, f32[1024,256]{1,0:T(8,128)} %get-tuple-element.166.refs_1_, f32[1024,256]{1,0:T(8,128)} %get-tuple-element.167.refs_2_, ...), custom_call_target="tpu_custom_call" | custom-call | flops 19327352832 | bytes 10485760 | tf_op jit(solution)/shard_map/attention/pallas_call | solution.py:499
  477.8 18.3 %outer.5 = bf16[2048,1024]{1,0:T(8,128)(2,1)} custom-call(bf16[1024,2048]{1,0:T(8,128)(2,1)} %get-tuple-element.162.refs_0_, bf16[1024,2048]{1,0:T(8,128)(2,1)} %collective-permute-done.18.refs_0_.refs_1_, bf16[2048,256]{1,0:T(8,128)(2,1)} %get-tuple-element.188.refs_2_.refs_3_, bf16[2048,256]{1,0:T(8,128)(2,1)} %get-tuple-element.188.refs_2_.refs_3_, ...), custom_call_target="tpu_custom_call" | custom-call | flops 8589934592 | bytes 41943040 | tf_op jit(solution)/shard_map/outer/pallas_call | solution.py:627
  498.9 12.2 %collective-permute-done.28.refs_3_ = bf16[512,768]{1,0:T(8,128)(2,1)} collective-permute-done((bf16[512,768]{1,0:T(8,128)(2,1)S(1)}, bf16[512,768]{1,0:T(8,128)(2,1)}, u32[]{:S(2)}, u32[]{:S(2)}) %collective-permute-start.28) | collective-permute-done | bytes 786464 | tf_op jit(solution)/shard_map/ppermute | solution.py:93
  511.2 12.9 %project_back.1 = (bf16[256,6144]{1,0:T(8,128)(2,1)}, bf16[256,6144]{1,0:T(8,128)(2,1)}) custom-call(bf16[512,768]{1,0:T(8,128)(2,1)} %get-tuple-element.192.refs_0_, bf16[512,768]{1,0:T(8,128)(2,1)} %collective-permute-done.26.refs_1_, bf16[512,768]{1,0:T(8,128)(2,1)} %collective-permute-done.27.refs_2_, bf16[512,768]{1,0:T(8,128)(2,1)} %collective-permute-done.28.refs_3_, ...), custom_call_target="tpu_custom_call" | custom-call | tf_op jit(solution)/shard_map/project_back/pallas_call | solution.py:560
  524.1 7.1 add_convert_fusion
  532.5 10.8 %fusion.58 = f32[1024,2048]{1,0:T(8,128)} fusion(bf16[1024,1024]{1,0:T(8,128)(2,1)} %get-tuple-element.357.refs_2_, bf16[2048,1024]{1,0:T(8,128)(2,1)} %all-gather.4.cloned.1.call-done), kind=kOutput, calls=%fused_computation.214 | convolution fusion | flops 4294967296 | bytes 14680064 | tf_op jit(solution)/shard_map/dot_general | solution.py:24
  547.8 7.2 %add_convert_fusion.1.a.c = bf16[1024,2048]{1,0:T(8,128)(2,1)} fusion(f32[1024,2048]{1,0:T(8,128)} %fusion.58, bf16[2048,1024]{1,0:T(8,128)(2,1)} %all-gather.8.cloned.1.call-done.refs_4_, bf16[2048,256]{1,0:T(8,128)(2,1)} %get-tuple-element.209.refs_14_.refs_15_), kind=kOutput, calls=%fused_computation.1 | convolution fusion | flops 1077936128 | bytes 14155776 | tf_op jit(solution)/shard_map/dot_general | solution.py:24
  565.4 22.1 %backward_streams.1 = (bf16[1024,2048]{1,0:T(8,128)(2,1)}, f32[4,2048]{1,0:T(4,128)}, f32[2048,128]{1,0:T(8,128)}, f32[128,128]{1,0:T(8,128)}, f32[1,128]{1,0:T(1,128)}) custom-call(s32[1]{0:T(128)} %bitcast.refs_0_, s32[4]{0:T(128)} %pad_add_fusion.order.refs_1_, bf16[256,2048]{1,0:T(8,128)(2,1)} %dynamic-slice_select_fusion.3.refs_2_, ...), custom_call_target="tpu_custom_call" | custom-call | flops 83886080 | bytes 20971520 | tf_op jit(solution)/shard_map/backward_streams/pallas_call | solution.py:312
  636.0 7.6 %all-to-all-done.3 = bf16[4,256,2048]{2,1,0:T(8,128)(2,1)} async-done(((bf16[4,256,2048]{2,1,0:T(8,128)(2,1)}), bf16[4,256,2048]{2,1,0:T(8,128)(2,1)}, u32[]{:S(2)}, u32[]{:S(2)}) %all-to-all-start.3) | async-done | bytes 4194336 | tf_op jit(solution)/shard_map/all_to_all | solution.py:923
  658.3 15.8 %collective-permute-done.40 = f32[256,128]{1,0:T(8,128)S(1)} collective-permute-done((f32[256,128]{1,0:T(8,128)S(1)}, f32[256,128]{1,0:T(8,128)S(1)}, u32[]{:S(2)}, u32[]{:S(2)}) %collective-permute-start.40) | collective-permute-done | bytes 131104 | tf_op jit(solution)/shard_map/ppermute | solution.py:93
  676.5 7.5 %interleave.1 = bf16[2048,2048]{1,0:T(8,128)(2,1)} custom-call(s32[1]{0:T(128)} %bitcast.38.refs_0_.which, bf16[1024,2048]{1,0:T(8,128)(2,1)} %bitcast.44.own_ref, bf16[1024,2048]{1,0:T(8,128)(2,1)} %collective-permute-done.39.sibling_ref), custom_call_target="tpu_custom_call" | custom-call | tf_op jit(solution)/shard_map/interleave/pallas_call | solution.py:685
  (318 shorter events, 229.4 us)
Async XLA Ops:
  7.2 246.4 %all-gather.6.cloned.1.call-start = ((), (), s32[]{:S(2)}) async-start(), calls=%async_computation.10 | async-start | bytes 5242880 | tf_op jit(solution)/shard_map/all_gather | solution.py:776
  34.4 253.5 %all-gather.8.cloned.1.call-start = ((), (), s32[]{:S(2)}) async-start(), calls=%async_computation.11 | async-start | bytes 5242880 | tf_op jit(solution)/shard_map/all_gather | solution.py:782
  66.1 26.6 %collective-permute-start.4 = (bf16[512,2048]{1,0:T(8,128)(2,1)}, bf16[512,2048]{1,0:T(8,128)(2,1)}, u32[]{:S(2)}, u32[]{:S(2)}) collective-permute-start(bf16[512,2048]{1,0:T(8,128)(2,1)} %bitcast.2.refs_1_), channel_id=1, source_target_pairs={{0,2},{1,5},{2,0},{3,7},{4,6},{5,1},{6,4},{7,3},{8,10},{9,13},{10,... | collective-permute-start | bytes 6291464 | tf_op jit(solution)/shard_map/ppermute | solution.py:61
  108.9 35.6 %collective-permute-start.10 = (bf16[512,2048]{1,0:T(8,128)(2,1)S(1)}, bf16[512,2048]{1,0:T(8,128)(2,1)}, u32[]{:S(2)}, u32[]{:S(2)}) collective-permute-start(bf16[512,2048]{1,0:T(8,128)(2,1)S(1)} %bitcast.120), channel_id=1, source_target_pairs={{0,4},{1,3},{2,6},{3,1},{4,0},{5,7},{6,2},{7,5},{8,12},{9,11},{10,... | collective-permute-start | bytes 6291464 | tf_op jit(solution)/shard_map/ppermute | solution.py:61
  110.3 56.8 %collective-permute-start.11 = (bf16[512,2048]{1,0:T(8,128)(2,1)}, bf16[512,2048]{1,0:T(8,128)(2,1)}, u32[]{:S(2)}, u32[]{:S(2)}) collective-permute-start(bf16[512,2048]{1,0:T(8,128)(2,1)} %copy-done.9), channel_id=1, source_target_pairs={{0,4},{1,3},{2,6},{3,1},{4,0},{5,7},{6,2},{7,5},{8,12},{9,11},{10,... | collective-permute-start | bytes 6291464 | tf_op jit(solution)/shard_map/ppermute | solution.py:61
  113.1 111.6 %collective-permute-start.5 = (bf16[512,2048]{1,0:T(8,128)(2,1)}, bf16[512,2048]{1,0:T(8,128)(2,1)}, u32[]{:S(2)}, u32[]{:S(2)}) collective-permute-start(bf16[512,2048]{1,0:T(8,128)(2,1)} %bitcast.2.refs_1_), channel_id=1, source_target_pairs={{0,4},{1,3},{2,6},{3,1},{4,0},{5,7},{6,2},{7,5},{8,12},{9,11},{10,... | collective-permute-start | bytes 6291464 | tf_op jit(solution)/shard_map/ppermute | solution.py:61
  114.4 110.3 %collective-permute-start.6 = (bf16[512,2048]{1,0:T(8,128)(2,1)}, bf16[512,2048]{1,0:T(8,128)(2,1)}, u32[]{:S(2)}, u32[]{:S(2)}) collective-permute-start(bf16[512,2048]{1,0:T(8,128)(2,1)} %collective-permute-done.4.refs_2_), channel_id=1, source_target_pairs={{0,4},{1,3},{2,6},{3,1},{4,0},{5,7},{6,2},{7,5},{8,12},{9,11},{10,... | collective-permute-start | bytes 6291464 | tf_op jit(solution)/shard_map/ppermute | solution.py:61
  118.4 73.0 %collective-permute-start.12 = (bf16[256,2048]{1,0:T(8,128)(2,1)S(1)}, bf16[256,2048]{1,0:T(8,128)(2,1)}, u32[]{:S(2)}, u32[]{:S(2)}) collective-permute-start(bf16[256,2048]{1,0:T(8,128)(2,1)S(1)} %get-tuple-element.145), channel_id=1, source_target_pairs={{0,2},{1,5},{2,0},{3,7},{4,6},{5,1},{6,4},{7,3},{8,10},{9,13},{10,... | collective-permute-start | bytes 3145736 | tf_op jit(solution)/shard_map/ppermute | solution.py:61
  185.9 37.2 %all-to-all-start = ((bf16[128,4,1024]{0,2,1:T(8,128)(2,1)}), bf16[128,4,1024]{0,2,1:T(8,128)(2,1)S(1)}, u32[]{:S(2)}, u32[]{:S(2)}) async-start(bf16[128,4,1024]{0,2,1:T(8,128)(2,1)} %bitcast.19), calls=%async_computation | async-start | bytes 2097152 | tf_op jit(solution)/shard_map/all_to_all | solution.py:773
  189.5 116.3 %all-gather.4.cloned.1.call-start = ((), (), s32[]{:S(2)}) async-start(), calls=%async_computation.9 | async-start | bytes 5242880 | tf_op jit(solution)/shard_map/all_gather | solution.py:813
  189.5 60.2 %collective-permute-start.13 = (bf16[256,2048]{1,0:T(8,128)(2,1)S(1)}, bf16[256,2048]{1,0:T(8,128)(2,1)S(1)}, u32[]{:S(2)}, u32[]{:S(2)}) collective-permute-start(bf16[256,2048]{1,0:T(8,128)(2,1)S(1)} %get-tuple-element.145), channel_id=1, source_target_pairs={{0,4},{1,3},{2,6},{3,1},{4,0},{5,7},{6,2},{7,5},{8,12},{9,11},{10,... | collective-permute-start | bytes 3145736 | tf_op jit(solution)/shard_map/ppermute | solution.py:61
  191.5 59.3 %collective-permute-start.14 = (bf16[256,2048]{1,0:T(8,128)(2,1)}, bf16[256,2048]{1,0:T(8,128)(2,1)}, u32[]{:S(2)}, u32[]{:S(2)}) collective-permute-start(bf16[256,2048]{1,0:T(8,128)(2,1)} %collective-permute-done.12), channel_id=1, source_target_pairs={{0,4},{1,3},{2,6},{3,1},{4,0},{5,7},{6,2},{7,5},{8,12},{9,11},{10,... | collective-permute-start | bytes 3145736 | tf_op jit(solution)/shard_map/ppermute | solution.py:61
  224.4 246.2 %reduce-scatter.4.cloned.1.call-start = ((), (), s32[]{:S(2)}) async-start(), calls=%async_computation.12 | async-start | bytes 5242880 | tf_op jit(solution)/shard_map/reduce_scatter | solution.py:840
  286.9 209.3 %reduce-scatter.6.cloned.1.call-start = ((), (), s32[]{:S(2)}) async-start(), calls=%async_computation.13 | async-start | bytes 5242880 | tf_op jit(solution)/shard_map/reduce_scatter | solution.py:845
  287.2 37.9 %collective-permute-start.18 = (bf16[1024,2048]{1,0:T(8,128)(2,1)}, bf16[1024,2048]{1,0:T(8,128)(2,1)}, u32[]{:S(2)}, u32[]{:S(2)}) collective-permute-start(bf16[1024,2048]{1,0:T(8,128)(2,1)} %get-tuple-element.162.refs_0_), channel_id=1, source_target_pairs={{0,1},{1,0},{2,3},{3,2},{4,5},{5,4},{6,7},{7,6},{8,9},{9,8},{10,11... | collective-permute-start | bytes 12582920 | tf_op jit(solution)/shard_map/ppermute | solution.py:124
  287.3 37.8 %collective-permute-start.19 = (bf16[1024,2048]{1,0:T(8,128)(2,1)}, bf16[1024,2048]{1,0:T(8,128)(2,1)}, u32[]{:S(2)}, u32[]{:S(2)}) collective-permute-start(bf16[1024,2048]{1,0:T(8,128)(2,1)} %get-tuple-element.163.refs_1_.refs_4_), channel_id=1, source_target_pairs={{0,1},{1,0},{2,3},{3,2},{4,5},{5,4},{6,7},{7,6},{8,9},{9,8},{10,11... | collective-permute-start | bytes 12582920 | tf_op jit(solution)/shard_map/ppermute | solution.py:124
  287.8 37.3 %collective-permute-start.20 = (bf16[1024,2048]{1,0:T(8,128)(2,1)}, bf16[1024,2048]{1,0:T(8,128)(2,1)}, u32[]{:S(2)}, u32[]{:S(2)}) collective-permute-start(bf16[1024,2048]{1,0:T(8,128)(2,1)} %get-tuple-element.164.refs_2_.refs_8_), channel_id=1, source_target_pairs={{0,1},{1,0},{2,3},{3,2},{4,5},{5,4},{6,7},{7,6},{8,9},{9,8},{10,11... | collective-permute-start | bytes 12582920 | tf_op jit(solution)/shard_map/ppermute | solution.py:124
  290.0 37.4 %collective-permute-start.17 = (bf16[2048,768]{1,0:T(8,128)(2,1)S(1)}, bf16[2048,768]{1,0:T(8,128)(2,1)}, u32[]{:S(2)}, u32[]{:S(2)}) collective-permute-start(bf16[2048,768]{1,0:T(8,128)(2,1)S(1)} %slice.238.refs_4_), channel_id=1, source_target_pairs={{0,2},{1,5},{2,0},{3,7},{4,6},{5,1},{6,4},{7,3},{8,10},{9,13},{10,... | collective-permute-start | bytes 9437192 | tf_op jit(solution)/shard_map/ppermute | solution.py:61
  350.7 32.2 %collective-permute-start.22 = (bf16[1024,2048]{1,0:T(8,128)(2,1)}, bf16[1024,2048]{1,0:T(8,128)(2,1)}, u32[]{:S(2)}, u32[]{:S(2)}) collective-permute-start(bf16[1024,2048]{1,0:T(8,128)(2,1)} %convolution_convert_fusion), channel_id=1, source_target_pairs={{0,1},{1,0},{2,3},{3,2},{4,5},{5,4},{6,7},{7,6},{8,9},{9,8},{10,11... | collective-permute-start | bytes 12582920 | tf_op jit(solution)/shard_map/ppermute | solution.py:124
  358.9 284.7 %reduce-scatter.8.cloned.1.call-start = ((), (), s32[]{:S(2)}) async-start(), calls=%async_computation.14 | async-start | bytes 5242880 | tf_op jit(solution)/shard_map/reduce_scatter | solution.py:887
  364.7 38.8 %collective-permute-start.21 = (bf16[2048,768]{1,0:T(8,128)(2,1)S(1)}, bf16[2048,768]{1,0:T(8,128)(2,1)S(1)}, u32[]{:S(2)}, u32[]{:S(2)}) collective-permute-start(bf16[2048,768]{1,0:T(8,128)(2,1)S(1)} %copy-done.4), channel_id=1, source_target_pairs={{0,4},{1,3},{2,6},{3,1},{4,0},{5,7},{6,2},{7,5},{8,12},{9,11},{10,... | collective-permute-start | bytes 9437192 | tf_op jit(solution)/shard_map/ppermute | solution.py:61
  388.8 37.7 %collective-permute-start.23 = (bf16[512,2048]{1,0:T(8,128)(2,1)}, bf16[512,2048]{1,0:T(8,128)(2,1)}, u32[]{:S(2)}, u32[]{:S(2)}) collective-permute-start(bf16[512,2048]{1,0:T(8,128)(2,1)} %get-tuple-element.183), channel_id=1, source_target_pairs={{0,4},{1,3},{2,6},{3,1},{4,0},{5,7},{6,2},{7,5},{8,12},{9,11},{10,... | collective-permute-start | bytes 6291464 | tf_op jit(solution)/shard_map/ppermute | solution.py:61
  403.5 67.1 %collective-permute-start.25 = (bf16[2048,768]{1,0:T(8,128)(2,1)}, bf16[2048,768]{1,0:T(8,128)(2,1)}, u32[]{:S(2)}, u32[]{:S(2)}) collective-permute-start(bf16[2048,768]{1,0:T(8,128)(2,1)} %collective-permute-done.17.refs_5_), channel_id=1, source_target_pairs={{0,4},{1,3},{2,6},{3,1},{4,0},{5,7},{6,2},{7,5},{8,12},{9,11},{10,... | collective-permute-start | bytes 9437192 | tf_op jit(solution)/shard_map/ppermute | solution.py:61
  430.1 40.5 %collective-permute-start.24 = (bf16[256,2048]{1,0:T(8,128)(2,1)S(1)}, bf16[256,2048]{1,0:T(8,128)(2,1)S(1)}, u32[]{:S(2)}, u32[]{:S(2)}) collective-permute-start(bf16[256,2048]{1,0:T(8,128)(2,1)S(1)} %get-tuple-element.316), channel_id=1, source_target_pairs={{0,2},{1,5},{2,0},{3,7},{4,6},{5,1},{6,4},{7,3},{8,10},{9,13},{10,... | collective-permute-start | bytes 3145736 | tf_op jit(solution)/shard_map/ppermute | solution.py:61
  476.1 35.1 %collective-permute-start.28 = (bf16[512,768]{1,0:T(8,128)(2,1)S(1)}, bf16[512,768]{1,0:T(8,128)(2,1)}, u32[]{:S(2)}, u32[]{:S(2)}) collective-permute-start(bf16[512,768]{1,0:T(8,128)(2,1)S(1)} %get-tuple-element.308), channel_id=1, source_target_pairs={{0,6},{1,7},{2,4},{3,5},{4,2},{5,3},{6,0},{7,1},{8,14},{9,15},{10,... | collective-permute-start | bytes 2359304 | tf_op jit(solution)/shard_map/ppermute | solution.py:93
  531.2 32.6 %collective-permute-start.29 = (bf16[256,6144]{1,0:T(8,128)(2,1)}, bf16[256,6144]{1,0:T(8,128)(2,1)S(1)}, u32[]{:S(2)}, u32[]{:S(2)}) collective-permute-start(bf16[256,6144]{1,0:T(8,128)(2,1)} %get-tuple-element.201), channel_id=1, source_target_pairs={{0,1},{1,0},{2,3},{3,2},{4,5},{5,4},{6,7},{7,6},{8,9},{9,8},{10,11... | collective-permute-start | bytes 9437192 | tf_op jit(solution)/shard_map/ppermute | solution.py:124
  543.3 48.3 %all-to-all-start.4 = ((bf16[4,128,2048]{2,1,0:T(8,128)(2,1)}), bf16[4,128,2048]{2,1,0:T(8,128)(2,1)}, u32[]{:S(2)}, u32[]{:S(2)}) async-start(bf16[4,128,2048]{2,1,0:T(8,128)(2,1)} %bitcast.129), calls=%async_computation.7 | async-start | bytes 4194304 | tf_op jit(solution)/shard_map/all_to_all | solution.py:901
  561.0 71.2 %collective-permute-start.38 = (bf16[512,2048]{1,0:T(8,128)(2,1)}, bf16[512,2048]{1,0:T(8,128)(2,1)}, u32[]{:S(2)}, u32[]{:S(2)}) collective-permute-start(bf16[512,2048]{1,0:T(8,128)(2,1)} %get-tuple-element.211), channel_id=1, source_target_pairs={{0,4},{1,3},{2,6},{3,1},{4,0},{5,7},{6,2},{7,5},{8,12},{9,11},{10,... | collective-permute-start | bytes 6291464 | tf_op jit(solution)/shard_map/ppermute | solution.py:61
  591.6 52.0 %all-to-all-start.3 = ((bf16[4,256,2048]{2,1,0:T(8,128)(2,1)}), bf16[4,256,2048]{2,1,0:T(8,128)(2,1)}, u32[]{:S(2)}, u32[]{:S(2)}) async-start(bf16[4,256,2048]{2,1,0:T(8,128)(2,1)} %bitcast.130), calls=%async_computation.5 | async-start | bytes 8388608 | tf_op jit(solution)/shard_map/all_to_all | solution.py:923
  643.6 32.9 %collective-permute-start.39 = (bf16[1024,2048]{1,0:T(8,128)(2,1)}, bf16[1024,2048]{1,0:T(8,128)(2,1)}, u32[]{:S(2)}, u32[]{:S(2)}) collective-permute-start(bf16[1024,2048]{1,0:T(8,128)(2,1)} %bitcast.44.own_ref), channel_id=1, source_target_pairs={{0,1},{1,0},{2,3},{3,2},{4,5},{5,4},{6,7},{7,6},{8,9},{9,8},{10,11... | collective-permute-start | bytes 12582920 | tf_op jit(solution)/shard_map/ppermute | solution.py:124
  643.6 40.4 %collective-permute-start.43 = (bf16[256,2048]{1,0:T(8,128)(2,1)}, bf16[256,2048]{1,0:T(8,128)(2,1)}, u32[]{:S(2)}, u32[]{:S(2)}) collective-permute-start(bf16[256,2048]{1,0:T(8,128)(2,1)} %get-tuple-element.314), channel_id=1, source_target_pairs={{0,2},{1,5},{2,0},{3,7},{4,6},{5,1},{6,4},{7,3},{8,10},{9,13},{10,... | collective-permute-start | bytes 3145736 | tf_op jit(solution)/shard_map/ppermute | solution.py:61
  646.1 37.9 %all-to-all-start.5 = ((bf16[4,128,1024]{2,1,0:T(8,128)(2,1)}), bf16[4,128,1024]{2,1,0:T(8,128)(2,1)}, u32[]{:S(2)}, u32[]{:S(2)}) async-start(bf16[4,128,1024]{2,1,0:T(8,128)(2,1)} %bitcast.141), calls=%async_computation.8 | async-start | bytes 2097152 | tf_op jit(solution)/shard_map/all_to_all | solution.py:901
  (63 other events, 1092.0 us)
Sparse Core Ops, SparseCore 0:
  34.5 80.8 all-gather.5
  117.0 79.1 all-gather.7
  224.6 81.1 all-gather.3
  307.9 75.2 reduce-scatter.3
  385.4 77.2 reduce-scatter.5
  531.3 77.7 reduce-scatter.7

commit v6 on v5

--- a/solution.py
+++ b/solution.py
@@ -490,7 +490,7 @@
         lax.fori_loop(0, count, finish, 0)
 
 
-def attention(near, far, positions, which, count):
+def attention(near, far, tables, which, count):
     rows, piece = 2 * near[0].shape[0], near[0].shape[1]
     heads, half = piece // HD, rows // (2 * count)
     vmem = pl.BlockSpec(memory_space=pltpu.VMEM)
@@ -515,7 +515,7 @@
             flops=18 * rows * rows * piece, bytes_accessed=rows * piece * 20, transcendentals=rows * rows * heads // 2
         ),
         name="attention",
-    )(which, *near, *far, *rope_tables(positions))
+    )(which, *near, *far, *tables)
 
 
 def project(streams, weights, types):
@@ -804,11 +804,14 @@
     )
     bias_wide = jnp.pad(to_slots(mixer_bias).reshape(1, pairs), ((0, 0), (0, LANES - pairs)))
 
+    block = jnp.arange(count)[:, None] * rows + jnp.arange(half)[None, :]
+    positions = jnp.concatenate([(block + m * half).reshape(-1), (block + (1 - m) * half).reshape(-1)])
+    tables = rope_tables(positions)
     found = []
     for g in range(parts):
         found = forward_streams(slots[g], g, parts, found, pick, in_wide, out_wide, bias_wide, gain)
         if g == 0:
-            down_turned, *found = lax.optimization_barrier((down_weight.T, *found))
+            tables, down_turned, *found = tie((tables, down_weight.T, *found))
     down_mine = swap_columns(down_turned)
     down_full = lax.all_gather(down_mine, "dp", axis=0, tiled=True)
     all_weights = plane.gather(narrow_full[:, : 3 * piece])
@@ -816,8 +819,6 @@
     far_streams = [None] * STREAMS
     for c in reversed(range(STREAMS)):
         far_streams[c] = plane.swap(near_streams[c])
-    block = jnp.arange(count)[:, None] * rows + jnp.arange(half)[None, :]
-    positions = jnp.concatenate([(block + m * half).reshape(-1), (block + (1 - m) * half).reshape(-1)])
 
     domain_one = jnp.sum(jnp.where(jnp.arange(domain_scale.shape[0]) == domain[0], domain_scale, 0.0))
     own_target = lax.dynamic_slice_in_dim(target, m * half, half, 0)
@@ -861,7 +862,7 @@
 
     types = (f32, f32, bf16, bf16)
     attended, query_back, key_back, value_back, backs = attention(
-        project(near_given, narrow_full, types), project(far_given, narrow_full, types), positions, which_m, count
+        project(near_given, narrow_full, types), project(far_given, narrow_full, types), tables, which_m, count
     )
 
     def owned(near_one, far_one):

time: 723 us -> 720 us (level)
    ppermute x19, waiting for transfers between devices: 87.3 us -> 79.7 us  [step(): return lax.ppermute(value, PLANE, pairs)]
  transfers between devices with their start and end apart: 60 -> 60, of which waited for: 21 -> 24; matrix products, arithmetic and copies ran while one was open for 25% -> 26% of each run, Pallas kernels for 27% -> 27%
where the time goes in v6:
time: 720 us; the launch traced here: 712 us
  Pallas kernels  207 us (29%)
  waiting for transfers between devices  197 us (27%)
  matrix products  88 us (12%)
  local copies, waits for them, and re-layouts  68.6 us (10%)
  starting transfers between devices  65.5 us (9%)
  other arithmetic  42.9 us (6%)
  blocking collectives  27.8 us (4%)
  between operations  15.9 us (2%)
    dot_general x10, matrix products, dot(): lax.dot_general(left, right, (((contract[0],), (contract[1],)), ((), ()))...  88 us
    ppermute x19, waiting for transfers between devices, step(): return lax.ppermute(value, PLANE, pairs)  79.7 us
    pallas_call x3, Pallas kernels, outer(): pl.pallas_call(kernel, grid=(width // tile,), in_specs=specs, out_specs=p...  45.1 us
    pallas_call x1, Pallas kernels, attention(): pl.pallas_call(lambda *refs: attention_kernel(count, half, heads, *refs),...  39.3 us
    pallas_call x2, Pallas kernels, forward_streams(): pl.pallas_call(lambda *refs: forward_kernel(count, *refs[:given], *refs[g...  37.9 us
    ppermute x9, waiting for transfers between devices, direct(): return lax.ppermute(value, PLANE, pairs)  36 us
    all_to_all x1, waiting for transfers between devices, shards(): swap_columns = lambda x: lax.all_to_all(x, 'hist', 1, 0, tiled=True)  31.5 us
    all_to_all x2, blocking collectives, shards(): swap_columns = lambda x: lax.all_to_all(x, 'hist', 1, 0, tiled=True)  27.8 us
  transfers between devices with their start and end apart: 60, of which 24 were waited for; matrix products, arithmetic and copies ran while one was open for 26% of the time, Pallas kernels for 27%

profile of v6, /device:TPU:0, one launch (start us, length us, event | category | flops | bytes accessed | tf_op | source)
XLA Modules:
  0.0 712.3 jit_solution(12971852929321830038)
XLA Ops:
  19.2 14.4 %all_to_all.93 = bf16[128,4,1024]{0,2,1:T(8,128)(2,1)S(1)} all-to-all(bf16[128,4,1024]{0,2,1:T(8,128)(2,1)S(1)} %bitcast.138), channel_id=1, replica_groups=mesh['dp'=4,'hist'=4,'mp'=2] {'hist'}, dimensions={1} | all-to-all | bytes 2097152 | tf_op jit(solution)/shard_map/all_to_all | solution.py:773
  41.8 23.5 %collective-permute-done.3.refs_2_ = bf16[512,2048]{1,0:T(8,128)(2,1)S(1)} collective-permute-done((bf16[512,2048]{1,0:T(8,128)(2,1)S(1)}, bf16[512,2048]{1,0:T(8,128)(2,1)S(1)}, u32[]{:S(2)}, u32[]{:S(2)}) %collective-permute-start.3) | collective-permute-done | bytes 2097184 | tf_op jit(solution)/shard_map/ppermute | solution.py:61
  79.8 13.5 %collective-permute-done.4.refs_2_ = bf16[512,2048]{1,0:T(8,128)(2,1)} collective-permute-done((bf16[512,2048]{1,0:T(8,128)(2,1)}, bf16[512,2048]{1,0:T(8,128)(2,1)}, u32[]{:S(2)}, u32[]{:S(2)}) %collective-permute-start.4) | collective-permute-done | bytes 2097184 | tf_op jit(solution)/shard_map/ppermute | solution.py:61
  93.3 13.4 %all_to_all.94 = bf16[128,4,1024]{0,2,1:T(8,128)(2,1)S(1)} all-to-all(bf16[128,4,1024]{0,2,1:T(8,128)(2,1)S(1)} %bitcast.134), channel_id=1, replica_groups=mesh['dp'=4,'hist'=4,'mp'=2] {'hist'}, dimensions={1} | all-to-all | bytes 2097152 | tf_op jit(solution)/shard_map/all_to_all | solution.py:773
  135.0 11.9 %collective-permute-done.10.refs_3_ = bf16[512,2048]{1,0:T(8,128)(2,1)} collective-permute-done((bf16[512,2048]{1,0:T(8,128)(2,1)S(1)}, bf16[512,2048]{1,0:T(8,128)(2,1)}, u32[]{:S(2)}, u32[]{:S(2)}) %collective-permute-start.10) | collective-permute-done | bytes 2097184 | tf_op jit(solution)/shard_map/ppermute | solution.py:61
  146.9 22.5 %collective-permute-done.11.refs_4_ = bf16[512,2048]{1,0:T(8,128)(2,1)} collective-permute-done((bf16[512,2048]{1,0:T(8,128)(2,1)}, bf16[512,2048]{1,0:T(8,128)(2,1)}, u32[]{:S(2)}, u32[]{:S(2)}) %collective-permute-start.11) | collective-permute-done | bytes 2097184 | tf_op jit(solution)/shard_map/ppermute | solution.py:61
  169.4 18.9 %forward_streams.2 = (bf16[1024,2048]{1,0:T(8,128)(2,1)}, bf16[1024,2048]{1,0:T(8,128)(2,1)}, bf16[1024,2048]{1,0:T(8,128)(2,1)}, bf16[1024,2048]{1,0:T(8,128)(2...) custom-call(s32[1]{0:T(128)} %bitcast.refs_0_, bf16[512,2048]{1,0:T(8,128)(2,1)} %bitcast.121, ...), custom_call_target="tpu_custom_call" | custom-call | flops 83886080 | bytes 16777216 | tf_op jit(solution)/shard_map/forward_streams/pallas_call | solution.py:182
  194.0 31.5 %all-to-all-done = bf16[128,4,1024]{0,2,1:T(8,128)(2,1)S(1)} async-done(((bf16[128,4,1024]{0,2,1:T(8,128)(2,1)}), bf16[128,4,1024]{0,2,1:T(8,128)(2,1)S(1)}, u32[]{:S(2)}, u32[]{:S(2)}) %all-to-all-start) | async-done | bytes 1048608 | tf_op jit(solution)/shard_map/all_to_all | solution.py:773
  227.1 19.0 %forward_streams.3 = (bf16[1024,2048]{1,0:T(8,128)(2,1)}, bf16[1024,2048]{1,0:T(8,128)(2,1)}, bf16[1024,2048]{1,0:T(8,128)(2,1)}, bf16[1024,2048]{1,0:T(8,128)(2...) custom-call(s32[1]{0:T(128)} %bitcast.refs_0_, ...), custom_call_target="tpu_custom_call", output_to_operand_aliasing={{0}: (9, {}), {1}: (10, {}), {2}: (11, {}), {3}: (12, {}), ... | custom-call | flops 83886080 | bytes 16777216 | tf_op jit(solution)/shard_map/forward_streams/pallas_call | solution.py:182
  256.0 10.9 %multiply_convert_fusion.1 = (bf16[1024,1024]{1,0:T(8,128)(2,1)}, f32[1024,1024]{1,0:T(8,128)}) fusion(bf16[1024,2048]{1,0:T(8,128)(2,1)} %get-tuple-element.150.refs_0_, bf16[2048,1024]{1,0:T(8,128)(2,1)} %all-gather.6.cloned.1.call-done), kind=kOutput, calls=%fused_computation.19 | convolution fusion | flops 4300210176 | bytes 14680064 | tf_op jit(solution)/shard_map/dot_general | solution.py:24
  266.9 8.9 %multiply_convert_fusion = (bf16[1024,1024]{1,0:T(8,128)(2,1)}, f32[1024,1024]{1,0:T(8,128)}) fusion(bf16[1024,2048]{1,0:T(8,128)(2,1)} %collective-permute-done.16.refs_1_, bf16[2048,1024]{1,0:T(8,128)(2,1)S(1)} %copy-done.29), kind=kOutput, calls=%fused_computation.18 | convolution fusion | flops 4300210176 | bytes 14680064 | tf_op jit(solution)/shard_map/dot_general | solution.py:24
  275.9 13.4 %outer.4 = bf16[2048,1024]{1,0:T(8,128)(2,1)} custom-call(bf16[1024,2048]{1,0:T(8,128)(2,1)} %constant_dynamic-update-slice_fusion.8.refs_0_.refs_3_.refs_12_, bf16[1024,2048]{1,0:T(8,128)(2,1)} %collective-permute-done.15.refs_1_.refs_3_.refs_13_, bf16[1024,1024]{1,0:T(8,128)(2,1)} %get-tuple-element.363.refs_2_, bf16[1024,1024]{1,0:T(8,128)(2,1)} %get-tuple-element.365.refs_3_), custom_call_target="tpu_custom_call" | custom-call | flops 8589934592 | bytes 16777216 | tf_op jit(solution)/shard_map/outer/pallas_call | solution.py:627
  293.4 14.3 %all-gather.4.cloned.1.call-done = bf16[2048,1024]{1,0:T(8,128)(2,1)} async-done(((bf16[512,1024]{1,0:T(8,128)(2,1)}), bf16[2048,1024]{1,0:T(8,128)(2,1)}) %all-gather.4.cloned.1.call-update) | async-done | bytes 4194320 | tf_op jit(solution)/shard_map/all_gather | solution.py:816
  307.7 10.4 %fusion.11.refs_3_ = bf16[1024,1024]{1,0:T(8,128)(2,1)} fusion(f32[1024,1024]{1,0:T(8,128)} %get-tuple-element.366, bf16[1024,2048]{1,0:T(8,128)(2,1)} %collective-permute-done.15.refs_1_.refs_3_.refs_13_, bf16[2048,1024]{1,0:T(8,128)(2,1)} %all-gather.4.cloned.1.call-done), kind=kOutput, calls=%fused_computation.15 | convolution fusion | flops 4305453056 | bytes 14680064 | tf_op jit(solution)/shard_map/dot_general | solution.py:24
  318.1 8.9 %fusion.5.refs_2_ = bf16[1024,1024]{1,0:T(8,128)(2,1)} fusion(f32[1024,1024]{1,0:T(8,128)S(1)} %copy-done.34, bf16[1024,2048]{1,0:T(8,128)(2,1)} %constant_dynamic-update-slice_fusion.8.refs_0_.refs_3_.refs_12_, bf16[2048,1024]{1,0:T(8,128)(2,1)S(1)} %copy-done.31), kind=kOutput, calls=%fused_computation.9 | convolution fusion | flops 4305453056 | bytes 14680064 | tf_op jit(solution)/shard_map/dot_general | solution.py:24
  330.1 13.4 %outer.3 = bf16[2048,1024]{1,0:T(8,128)(2,1)} custom-call(bf16[1024,2048]{1,0:T(8,128)(2,1)} %get-tuple-element.150.refs_0_, bf16[1024,2048]{1,0:T(8,128)(2,1)} %collective-permute-done.16.refs_1_, bf16[1024,1024]{1,0:T(8,128)(2,1)} %fusion.5.refs_2_, bf16[1024,1024]{1,0:T(8,128)(2,1)} %fusion.11.refs_3_), custom_call_target="tpu_custom_call" | custom-call | flops 8589934592 | bytes 16777216 | tf_op jit(solution)/shard_map/outer/pallas_call | solution.py:627
  343.5 9.4 %convolution_convert_fusion = bf16[1024,2048]{1,0:T(8,128)(2,1)} fusion(bf16[1024,1024]{1,0:T(8,128)(2,1)} %fusion.11.refs_3_, bf16[2048,1024]{1,0:T(8,128)(2,1)} %all-gather.6.cloned.1.call-done), kind=kOutput, calls=%fused_computation.22 | convolution fusion | flops 4297064448 | bytes 10485760 | tf_op jit(solution)/shard_map/dot_general | solution.py:24
  390.2 8.4 %fusion.59 = f32[1024,2048]{1,0:T(8,128)} fusion(bf16[1024,1024]{1,0:T(8,128)(2,1)} %get-tuple-element.365.refs_3_, bf16[2048,1024]{1,0:T(8,128)(2,1)S(1)} %copy-done.32), kind=kOutput, calls=%fused_computation.215 | convolution fusion | flops 4294967296 | bytes 14680064 | tf_op jit(solution)/shard_map/dot_general | solution.py:24
  399.5 11.0 %project.2 = (f32[1024,256]{1,0:T(8,128)}, f32[1024,256]{1,0:T(8,128)}, bf16[1024,256]{1,0:T(8,128)(2,1)}, bf16[1024,256]{1,0:T(8,128)(2,1)}) custom-call(bf16[1024,2048]{1,0:T(8,128)(2,1)} %get-tuple-element.165.refs_0_, bf16[1024,2048]{1,0:T(8,128)(2,1)} %get-tuple-element.166.refs_1_.refs_4_, bf16[1024,2048]{1,0:T(8,128)(2,1)} %get-tuple-element.167.refs_2_.refs_8_, ...), custom_call_target="tpu_custom_call" | custom-call | flops 4294967296 | bytes 16777216 | tf_op jit(solution)/shard_map/project/pallas_call | solution.py:532
  410.5 11.1 %project.3 = (f32[1024,256]{1,0:T(8,128)}, f32[1024,256]{1,0:T(8,128)}, bf16[1024,256]{1,0:T(8,128)(2,1)}, bf16[1024,256]{1,0:T(8,128)(2,1)}) custom-call(bf16[1024,2048]{1,0:T(8,128)(2,1)} %collective-permute-done.18.refs_0_.refs_1_, bf16[1024,2048]{1,0:T(8,128)(2,1)} %collective-permute-done.19.refs_1_.refs_5_, ...), custom_call_target="tpu_custom_call" | custom-call | flops 4294967296 | bytes 16777216 | tf_op jit(solution)/shard_map/project/pallas_call | solution.py:532
  425.5 39.3 %attention.1 = (bf16[2048,256]{1,0:T(8,128)(2,1)}, bf16[2048,256]{1,0:T(8,128)(2,1)}, bf16[2048,256]{1,0:T(8,128)(2,1)}, bf16[2048,256]{1,0:T(8,128)(2,1)}, bf16[2048,768]{1,0:T(8,128)(2,1)}) custom-call(s32[1]{0:T(128)} %bitcast.38.refs_0_.which, f32[1024,256]{1,0:T(8,128)} %get-tuple-element.169.refs_1_, f32[1024,256]{1,0:T(8,128)} %get-tuple-element.170.refs_2_, ...), custom_call_target="tpu_custom_call" | custom-call | flops 19327352832 | bytes 10485760 | tf_op jit(solution)/shard_map/attention/pallas_call | solution.py:499
  472.2 18.3 %outer.5 = bf16[2048,1024]{1,0:T(8,128)(2,1)} custom-call(bf16[1024,2048]{1,0:T(8,128)(2,1)} %get-tuple-element.165.refs_0_, bf16[1024,2048]{1,0:T(8,128)(2,1)} %collective-permute-done.18.refs_0_.refs_1_, bf16[2048,256]{1,0:T(8,128)(2,1)} %get-tuple-element.194.refs_2_.refs_3_, bf16[2048,256]{1,0:T(8,128)(2,1)} %get-tuple-element.194.refs_2_.refs_3_, ...), custom_call_target="tpu_custom_call" | custom-call | flops 8589934592 | bytes 41943040 | tf_op jit(solution)/shard_map/outer/pallas_call | solution.py:627
  493.2 12.5 %collective-permute-done.27.refs_2_ = bf16[512,768]{1,0:T(8,128)(2,1)} collective-permute-done((bf16[512,768]{1,0:T(8,128)(2,1)}, bf16[512,768]{1,0:T(8,128)(2,1)}, u32[]{:S(2)}, u32[]{:S(2)}) %collective-permute-start.27) | collective-permute-done | bytes 786464 | tf_op jit(solution)/shard_map/ppermute | solution.py:93
  505.7 13.0 %project_back.1 = (bf16[256,6144]{1,0:T(8,128)(2,1)}, bf16[256,6144]{1,0:T(8,128)(2,1)}) custom-call(bf16[512,768]{1,0:T(8,128)(2,1)} %get-tuple-element.198.refs_0_, bf16[512,768]{1,0:T(8,128)(2,1)} %collective-permute-done.26.refs_1_, bf16[512,768]{1,0:T(8,128)(2,1)} %collective-permute-done.27.refs_2_, bf16[512,768]{1,0:T(8,128)(2,1)} %collective-permute-done.28.refs_3_, ...), custom_call_target="tpu_custom_call" | custom-call | tf_op jit(solution)/shard_map/project_back/pallas_call | solution.py:560
  518.7 7.0 add_convert_fusion
  527.1 10.8 %fusion.58 = f32[1024,2048]{1,0:T(8,128)} fusion(bf16[1024,1024]{1,0:T(8,128)(2,1)} %get-tuple-element.363.refs_2_, bf16[2048,1024]{1,0:T(8,128)(2,1)} %all-gather.4.cloned.1.call-done), kind=kOutput, calls=%fused_computation.214 | convolution fusion | flops 4294967296 | bytes 14680064 | tf_op jit(solution)/shard_map/dot_general | solution.py:24
  542.3 7.2 %add_convert_fusion.1.a.c = bf16[1024,2048]{1,0:T(8,128)(2,1)} fusion(f32[1024,2048]{1,0:T(8,128)} %fusion.58, bf16[2048,1024]{1,0:T(8,128)(2,1)} %all-gather.8.cloned.1.call-done.refs_4_, bf16[2048,256]{1,0:T(8,128)(2,1)} %get-tuple-element.215.refs_14_.refs_15_), kind=kOutput, calls=%fused_computation.1 | convolution fusion | flops 1077936128 | bytes 14155776 | tf_op jit(solution)/shard_map/dot_general | solution.py:24
  560.0 22.1 %backward_streams.1 = (bf16[1024,2048]{1,0:T(8,128)(2,1)}, f32[4,2048]{1,0:T(4,128)}, f32[2048,128]{1,0:T(8,128)}, f32[128,128]{1,0:T(8,128)}, f32[1,128]{1,0:T(1,128)}) custom-call(s32[1]{0:T(128)} %bitcast.refs_0_, s32[4]{0:T(128)} %pad_add_fusion.order.refs_1_, bf16[256,2048]{1,0:T(8,128)(2,1)} %dynamic-slice_select_fusion.3.refs_2_, ...), custom_call_target="tpu_custom_call" | custom-call | flops 83886080 | bytes 20971520 | tf_op jit(solution)/shard_map/backward_streams/pallas_call | solution.py:312
  607.5 6.5 collective-permute-done.33
  631.7 6.6 all-to-all-done.3
  653.0 15.8 %collective-permute-done.40 = f32[256,128]{1,0:T(8,128)S(1)} collective-permute-done((f32[256,128]{1,0:T(8,128)S(1)}, f32[256,128]{1,0:T(8,128)S(1)}, u32[]{:S(2)}, u32[]{:S(2)}) %collective-permute-start.40) | collective-permute-done | bytes 131104 | tf_op jit(solution)/shard_map/ppermute | solution.py:93
  671.2 7.5 %interleave.1 = bf16[2048,2048]{1,0:T(8,128)(2,1)} custom-call(s32[1]{0:T(128)} %bitcast.38.refs_0_.which, bf16[1024,2048]{1,0:T(8,128)(2,1)} %bitcast.44.own_ref, bf16[1024,2048]{1,0:T(8,128)(2,1)} %collective-permute-done.39.sibling_ref), custom_call_target="tpu_custom_call" | custom-call | tf_op jit(solution)/shard_map/interleave/pallas_call | solution.py:685
  (320 shorter events, 241.1 us)
Async XLA Ops:
  7.2 248.8 %all-gather.6.cloned.1.call-start = ((), (), s32[]{:S(2)}) async-start(), calls=%async_computation.10 | async-start | bytes 5242880 | tf_op jit(solution)/shard_map/all_gather | solution.py:776
  35.0 255.6 %all-gather.8.cloned.1.call-start = ((), (), s32[]{:S(2)}) async-start(), calls=%async_computation.11 | async-start | bytes 5242880 | tf_op jit(solution)/shard_map/all_gather | solution.py:782
  66.7 26.6 %collective-permute-start.4 = (bf16[512,2048]{1,0:T(8,128)(2,1)}, bf16[512,2048]{1,0:T(8,128)(2,1)}, u32[]{:S(2)}, u32[]{:S(2)}) collective-permute-start(bf16[512,2048]{1,0:T(8,128)(2,1)} %bitcast.2.refs_1_), channel_id=1, source_target_pairs={{0,2},{1,5},{2,0},{3,7},{4,6},{5,1},{6,4},{7,3},{8,10},{9,13},{10,... | collective-permute-start | bytes 6291464 | tf_op jit(solution)/shard_map/ppermute | solution.py:61
  109.5 37.4 %collective-permute-start.10 = (bf16[512,2048]{1,0:T(8,128)(2,1)S(1)}, bf16[512,2048]{1,0:T(8,128)(2,1)}, u32[]{:S(2)}, u32[]{:S(2)}) collective-permute-start(bf16[512,2048]{1,0:T(8,128)(2,1)S(1)} %bitcast.120), channel_id=1, source_target_pairs={{0,4},{1,3},{2,6},{3,1},{4,0},{5,7},{6,2},{7,5},{8,12},{9,11},{10,... | collective-permute-start | bytes 6291464 | tf_op jit(solution)/shard_map/ppermute | solution.py:61
  110.8 58.6 %collective-permute-start.11 = (bf16[512,2048]{1,0:T(8,128)(2,1)}, bf16[512,2048]{1,0:T(8,128)(2,1)}, u32[]{:S(2)}, u32[]{:S(2)}) collective-permute-start(bf16[512,2048]{1,0:T(8,128)(2,1)} %copy-done.9), channel_id=1, source_target_pairs={{0,4},{1,3},{2,6},{3,1},{4,0},{5,7},{6,2},{7,5},{8,12},{9,11},{10,... | collective-permute-start | bytes 6291464 | tf_op jit(solution)/shard_map/ppermute | solution.py:61
  114.8 112.3 %collective-permute-start.5 = (bf16[512,2048]{1,0:T(8,128)(2,1)}, bf16[512,2048]{1,0:T(8,128)(2,1)}, u32[]{:S(2)}, u32[]{:S(2)}) collective-permute-start(bf16[512,2048]{1,0:T(8,128)(2,1)} %bitcast.2.refs_1_), channel_id=1, source_target_pairs={{0,4},{1,3},{2,6},{3,1},{4,0},{5,7},{6,2},{7,5},{8,12},{9,11},{10,... | collective-permute-start | bytes 6291464 | tf_op jit(solution)/shard_map/ppermute | solution.py:61
  116.1 111.0 %collective-permute-start.6 = (bf16[512,2048]{1,0:T(8,128)(2,1)}, bf16[512,2048]{1,0:T(8,128)(2,1)}, u32[]{:S(2)}, u32[]{:S(2)}) collective-permute-start(bf16[512,2048]{1,0:T(8,128)(2,1)} %collective-permute-done.4.refs_2_), channel_id=1, source_target_pairs={{0,4},{1,3},{2,6},{3,1},{4,0},{5,7},{6,2},{7,5},{8,12},{9,11},{10,... | collective-permute-start | bytes 6291464 | tf_op jit(solution)/shard_map/ppermute | solution.py:61
  122.6 71.2 %collective-permute-start.12 = (bf16[256,2048]{1,0:T(8,128)(2,1)S(1)}, bf16[256,2048]{1,0:T(8,128)(2,1)}, u32[]{:S(2)}, u32[]{:S(2)}) collective-permute-start(bf16[256,2048]{1,0:T(8,128)(2,1)S(1)} %get-tuple-element.148), channel_id=1, source_target_pairs={{0,2},{1,5},{2,0},{3,7},{4,6},{5,1},{6,4},{7,3},{8,10},{9,13},{10,... | collective-permute-start | bytes 3145736 | tf_op jit(solution)/shard_map/ppermute | solution.py:61
  188.3 37.1 %all-to-all-start = ((bf16[128,4,1024]{0,2,1:T(8,128)(2,1)}), bf16[128,4,1024]{0,2,1:T(8,128)(2,1)S(1)}, u32[]{:S(2)}, u32[]{:S(2)}) async-start(bf16[128,4,1024]{0,2,1:T(8,128)(2,1)} %bitcast.19), calls=%async_computation | async-start | bytes 2097152 | tf_op jit(solution)/shard_map/all_to_all | solution.py:773
  191.8 115.8 %all-gather.4.cloned.1.call-start = ((), (), s32[]{:S(2)}) async-start(), calls=%async_computation.9 | async-start | bytes 5242880 | tf_op jit(solution)/shard_map/all_gather | solution.py:816
  191.9 60.3 %collective-permute-start.13 = (bf16[256,2048]{1,0:T(8,128)(2,1)S(1)}, bf16[256,2048]{1,0:T(8,128)(2,1)S(1)}, u32[]{:S(2)}, u32[]{:S(2)}) collective-permute-start(bf16[256,2048]{1,0:T(8,128)(2,1)S(1)} %get-tuple-element.148), channel_id=1, source_target_pairs={{0,4},{1,3},{2,6},{3,1},{4,0},{5,7},{6,2},{7,5},{8,12},{9,11},{10,... | collective-permute-start | bytes 3145736 | tf_op jit(solution)/shard_map/ppermute | solution.py:61
  193.8 59.4 %collective-permute-start.14 = (bf16[256,2048]{1,0:T(8,128)(2,1)}, bf16[256,2048]{1,0:T(8,128)(2,1)}, u32[]{:S(2)}, u32[]{:S(2)}) collective-permute-start(bf16[256,2048]{1,0:T(8,128)(2,1)} %collective-permute-done.12), channel_id=1, source_target_pairs={{0,4},{1,3},{2,6},{3,1},{4,0},{5,7},{6,2},{7,5},{8,12},{9,11},{10,... | collective-permute-start | bytes 3145736 | tf_op jit(solution)/shard_map/ppermute | solution.py:61
  226.8 238.2 %reduce-scatter.4.cloned.1.call-start = ((), (), s32[]{:S(2)}) async-start(), calls=%async_computation.12 | async-start | bytes 5242880 | tf_op jit(solution)/shard_map/reduce_scatter | solution.py:841
  289.3 201.2 %reduce-scatter.6.cloned.1.call-start = ((), (), s32[]{:S(2)}) async-start(), calls=%async_computation.13 | async-start | bytes 5242880 | tf_op jit(solution)/shard_map/reduce_scatter | solution.py:846
  289.9 37.1 %collective-permute-start.18 = (bf16[1024,2048]{1,0:T(8,128)(2,1)}, bf16[1024,2048]{1,0:T(8,128)(2,1)}, u32[]{:S(2)}, u32[]{:S(2)}) collective-permute-start(bf16[1024,2048]{1,0:T(8,128)(2,1)} %get-tuple-element.165.refs_0_), channel_id=1, source_target_pairs={{0,1},{1,0},{2,3},{3,2},{4,5},{5,4},{6,7},{7,6},{8,9},{9,8},{10,11... | collective-permute-start | bytes 12582920 | tf_op jit(solution)/shard_map/ppermute | solution.py:124
  290.0 37.0 %collective-permute-start.19 = (bf16[1024,2048]{1,0:T(8,128)(2,1)}, bf16[1024,2048]{1,0:T(8,128)(2,1)}, u32[]{:S(2)}, u32[]{:S(2)}) collective-permute-start(bf16[1024,2048]{1,0:T(8,128)(2,1)} %get-tuple-element.166.refs_1_.refs_4_), channel_id=1, source_target_pairs={{0,1},{1,0},{2,3},{3,2},{4,5},{5,4},{6,7},{7,6},{8,9},{9,8},{10,11... | collective-permute-start | bytes 12582920 | tf_op jit(solution)/shard_map/ppermute | solution.py:124
  290.5 36.6 %collective-permute-start.20 = (bf16[1024,2048]{1,0:T(8,128)(2,1)}, bf16[1024,2048]{1,0:T(8,128)(2,1)}, u32[]{:S(2)}, u32[]{:S(2)}) collective-permute-start(bf16[1024,2048]{1,0:T(8,128)(2,1)} %get-tuple-element.167.refs_2_.refs_8_), channel_id=1, source_target_pairs={{0,1},{1,0},{2,3},{3,2},{4,5},{5,4},{6,7},{7,6},{8,9},{9,8},{10,11... | collective-permute-start | bytes 12582920 | tf_op jit(solution)/shard_map/ppermute | solution.py:124
  292.7 37.4 %collective-permute-start.17 = (bf16[2048,768]{1,0:T(8,128)(2,1)S(1)}, bf16[2048,768]{1,0:T(8,128)(2,1)}, u32[]{:S(2)}, u32[]{:S(2)}) collective-permute-start(bf16[2048,768]{1,0:T(8,128)(2,1)S(1)} %slice.238.refs_4_), channel_id=1, source_target_pairs={{0,2},{1,5},{2,0},{3,7},{4,6},{5,1},{6,4},{7,3},{8,10},{9,13},{10,... | collective-permute-start | bytes 9437192 | tf_op jit(solution)/shard_map/ppermute | solution.py:61
  353.5 278.2 %reduce-scatter.8.cloned.1.call-start = ((), (), s32[]{:S(2)}) async-start(), calls=%async_computation.14 | async-start | bytes 5242880 | tf_op jit(solution)/shard_map/reduce_scatter | solution.py:888
  360.2 38.4 %collective-permute-start.21 = (bf16[2048,768]{1,0:T(8,128)(2,1)S(1)}, bf16[2048,768]{1,0:T(8,128)(2,1)S(1)}, u32[]{:S(2)}, u32[]{:S(2)}) collective-permute-start(bf16[2048,768]{1,0:T(8,128)(2,1)S(1)} %copy-done.4), channel_id=1, source_target_pairs={{0,4},{1,3},{2,6},{3,1},{4,0},{5,7},{6,2},{7,5},{8,12},{9,11},{10,... | collective-permute-start | bytes 9437192 | tf_op jit(solution)/shard_map/ppermute | solution.py:61
  384.3 37.2 %collective-permute-start.23 = (bf16[512,2048]{1,0:T(8,128)(2,1)}, bf16[512,2048]{1,0:T(8,128)(2,1)}, u32[]{:S(2)}, u32[]{:S(2)}) collective-permute-start(bf16[512,2048]{1,0:T(8,128)(2,1)} %get-tuple-element.189), channel_id=1, source_target_pairs={{0,4},{1,3},{2,6},{3,1},{4,0},{5,7},{6,2},{7,5},{8,12},{9,11},{10,... | collective-permute-start | bytes 6291464 | tf_op jit(solution)/shard_map/ppermute | solution.py:61
  398.6 66.4 %collective-permute-start.25 = (bf16[2048,768]{1,0:T(8,128)(2,1)}, bf16[2048,768]{1,0:T(8,128)(2,1)}, u32[]{:S(2)}, u32[]{:S(2)}) collective-permute-start(bf16[2048,768]{1,0:T(8,128)(2,1)} %collective-permute-done.17.refs_5_), channel_id=1, source_target_pairs={{0,4},{1,3},{2,6},{3,1},{4,0},{5,7},{6,2},{7,5},{8,12},{9,11},{10,... | collective-permute-start | bytes 9437192 | tf_op jit(solution)/shard_map/ppermute | solution.py:61
  425.2 39.8 %collective-permute-start.24 = (bf16[256,2048]{1,0:T(8,128)(2,1)S(1)}, bf16[256,2048]{1,0:T(8,128)(2,1)S(1)}, u32[]{:S(2)}, u32[]{:S(2)}) collective-permute-start(bf16[256,2048]{1,0:T(8,128)(2,1)S(1)} %get-tuple-element.322), channel_id=1, source_target_pairs={{0,2},{1,5},{2,0},{3,7},{4,6},{5,1},{6,4},{7,3},{8,10},{9,13},{10,... | collective-permute-start | bytes 3145736 | tf_op jit(solution)/shard_map/ppermute | solution.py:61
  470.6 35.0 %collective-permute-start.27 = (bf16[512,768]{1,0:T(8,128)(2,1)}, bf16[512,768]{1,0:T(8,128)(2,1)}, u32[]{:S(2)}, u32[]{:S(2)}) collective-permute-start(bf16[512,768]{1,0:T(8,128)(2,1)} %get-tuple-element.315), channel_id=1, source_target_pairs={{0,4},{1,3},{2,6},{3,1},{4,0},{5,7},{6,2},{7,5},{8,12},{9,11},{10,... | collective-permute-start | bytes 2359304 | tf_op jit(solution)/shard_map/ppermute | solution.py:93
  471.7 34.0 %collective-permute-start.26 = (bf16[512,768]{1,0:T(8,128)(2,1)S(1)}, bf16[512,768]{1,0:T(8,128)(2,1)}, u32[]{:S(2)}, u32[]{:S(2)}) collective-permute-start(bf16[512,768]{1,0:T(8,128)(2,1)S(1)} %get-tuple-element.316), channel_id=1, source_target_pairs={{0,2},{1,5},{2,0},{3,7},{4,6},{5,1},{6,4},{7,3},{8,10},{9,13},{10,... | collective-permute-start | bytes 2359304 | tf_op jit(solution)/shard_map/ppermute | solution.py:93
  525.8 32.6 %collective-permute-start.29 = (bf16[256,6144]{1,0:T(8,128)(2,1)}, bf16[256,6144]{1,0:T(8,128)(2,1)S(1)}, u32[]{:S(2)}, u32[]{:S(2)}) collective-permute-start(bf16[256,6144]{1,0:T(8,128)(2,1)} %get-tuple-element.207), channel_id=1, source_target_pairs={{0,1},{1,0},{2,3},{3,2},{4,5},{5,4},{6,7},{7,6},{8,9},{9,8},{10,11... | collective-permute-start | bytes 9437192 | tf_op jit(solution)/shard_map/ppermute | solution.py:124
  537.8 48.3 %all-to-all-start.4 = ((bf16[4,128,2048]{2,1,0:T(8,128)(2,1)}), bf16[4,128,2048]{2,1,0:T(8,128)(2,1)}, u32[]{:S(2)}, u32[]{:S(2)}) async-start(bf16[4,128,2048]{2,1,0:T(8,128)(2,1)} %bitcast.129), calls=%async_computation.7 | async-start | bytes 4194304 | tf_op jit(solution)/shard_map/all_to_all | solution.py:902
  555.6 72.3 %collective-permute-start.38 = (bf16[512,2048]{1,0:T(8,128)(2,1)}, bf16[512,2048]{1,0:T(8,128)(2,1)}, u32[]{:S(2)}, u32[]{:S(2)}) collective-permute-start(bf16[512,2048]{1,0:T(8,128)(2,1)} %get-tuple-element.217), channel_id=1, source_target_pairs={{0,4},{1,3},{2,6},{3,1},{4,0},{5,7},{6,2},{7,5},{8,12},{9,11},{10,... | collective-permute-start | bytes 6291464 | tf_op jit(solution)/shard_map/ppermute | solution.py:61
  586.1 52.2 %all-to-all-start.3 = ((bf16[4,256,2048]{2,1,0:T(8,128)(2,1)}), bf16[4,256,2048]{2,1,0:T(8,128)(2,1)}, u32[]{:S(2)}, u32[]{:S(2)}) async-start(bf16[4,256,2048]{2,1,0:T(8,128)(2,1)} %bitcast.130), calls=%async_computation.5 | async-start | bytes 8388608 | tf_op jit(solution)/shard_map/all_to_all | solution.py:924
  638.3 32.9 %collective-permute-start.39 = (bf16[1024,2048]{1,0:T(8,128)(2,1)}, bf16[1024,2048]{1,0:T(8,128)(2,1)}, u32[]{:S(2)}, u32[]{:S(2)}) collective-permute-start(bf16[1024,2048]{1,0:T(8,128)(2,1)} %bitcast.44.own_ref), channel_id=1, source_target_pairs={{0,1},{1,0},{2,3},{3,2},{4,5},{5,4},{6,7},{7,6},{8,9},{9,8},{10,11... | collective-permute-start | bytes 12582920 | tf_op jit(solution)/shard_map/ppermute | solution.py:124
  638.3 40.4 %collective-permute-start.43 = (bf16[256,2048]{1,0:T(8,128)(2,1)}, bf16[256,2048]{1,0:T(8,128)(2,1)}, u32[]{:S(2)}, u32[]{:S(2)}) collective-permute-start(bf16[256,2048]{1,0:T(8,128)(2,1)} %get-tuple-element.320), channel_id=1, source_target_pairs={{0,2},{1,5},{2,0},{3,7},{4,6},{5,1},{6,4},{7,3},{8,10},{9,13},{10,... | collective-permute-start | bytes 3145736 | tf_op jit(solution)/shard_map/ppermute | solution.py:61
  640.8 37.9 %all-to-all-start.5 = ((bf16[4,128,1024]{2,1,0:T(8,128)(2,1)}), bf16[4,128,1024]{2,1,0:T(8,128)(2,1)}, u32[]{:S(2)}, u32[]{:S(2)}) async-start(bf16[4,128,1024]{2,1,0:T(8,128)(2,1)} %bitcast.141), calls=%async_computation.8 | async-start | bytes 2097152 | tf_op jit(solution)/shard_map/all_to_all | solution.py:902
  (64 other events, 1036.9 us)
Sparse Core Ops, SparseCore 0:
  35.1 80.7 all-gather.5
  117.5 79.2 all-gather.7
  226.9 80.7 all-gather.3
  309.8 75.2 reduce-scatter.3
  387.4 77.2 reduce-scatter.5
  525.9 76.6 reduce-scatter.7
